TPU v7x, 128 devices: a whole 4x4x4 slice. The times are simulated.
128 devices in a mesh: attn: 8 (over y, core), ffn: 16 (over x, z).
Axes of the slice: x: 4, y: 4, z: 4, core: 2. Of those that a mesh axis runs over, the one named last changes fastest.
Arguments:
- query_latent: bfloat16 [768, 64, 512], P('attn', 'ffn'), may hold values from -72 to 72
- query_rope: bfloat16 [768, 64, 64], P('attn', 'ffn'), may hold values from -6 to 6
- cache_latent: bfloat16 [768, 64, 512], P('attn'), may hold values from -6 to 6
- cache_rope: bfloat16 [768, 64, 64], P('attn'), may hold values from -6 to 6
- lengths: int32 [768], P('attn'), may hold values from 1 to 64, 16384 in all
- value_up: bfloat16 [64, 512, 128], P('ffn'), may hold values from -0.25 to 0.25
- out_proj: bfloat16 [64, 128, 7168], P('ffn'), may hold values from -0.0625 to 0.0625
- residual: bfloat16 [768, 7168], P(('attn', 'ffn')), may hold values from -6 to 6
- norm_gain: bfloat16 [7168], replicated, may hold values from 0.099609375 to 1.8984375
- expert_ids: int32 [768, 8], P(('attn', 'ffn')), may hold values from 0 to 15, all different within a row; in each aligned block of 6 rows (0 to 5, 6 to 11, ...) at most 4 rows name the same one
- route_weights: float32 [768, 8], P(('attn', 'ffn')), may hold values from 0.1 to 0.6
- gate_proj: bfloat16 [16, 7168, 2048], P('ffn', None, 'attn'), may hold values from -0.0625 to 0.0625
- up_proj: bfloat16 [16, 7168, 2048], P('ffn', None, 'attn'), may hold values from -0.0625 to 0.0625
- down_proj: bfloat16 [16, 2048, 7168], P('ffn', 'attn'), may hold values from -0.125 to 0.125
Outputs:
- layer_out: bfloat16 [768, 7168], P(('attn', 'ffn'))
Inputs may be any that keep to these rules, and one draw needn't show every extreme that they name: `expert_ids`: each row names 8 different experts; among the rows of one device (aligned blocks of 6 rows) no expert is named by more than 4 rows, and in some block one expert is named by exactly 4. `lengths`: the largest length is exactly 64.
All inputs are finite; a program needn't handle non-finite values. No bound on the sum of `lengths` on one device may be relied on, other than what follows from the above.
Results may differ from a plain program's by a relative error of at most 0.02.
Values may be sent and summed in bfloat16 or wider, within the bound.
No kernel may reach another device: no remote copies, remote signals or barrier semaphores. Data moves between devices by JAX's collectives and lax.ppermute only.
A program may use at most 128 MiB of HBM per device.

v0:
```python
import jax
import jax.numpy as jnp
from jax import lax
from jax.sharding import PartitionSpec as P


def local(
    query_latent,
    query_rope,
    cache_latent,
    cache_rope,
    lengths,
    value_up,
    out_proj,
    residual,
    norm_gain,
    expert_ids,
    route_weights,
    gate_proj,
    up_proj,
    down_proj,
):
    score_scale = (value_up.shape[2] + query_rope.shape[2]) ** (-0.5)
    cache_length = cache_latent.shape[1]
    row_count = residual.shape[0]
    scores = jnp.einsum(
        "rhc,rlc->rhl", query_latent, cache_latent, preferred_element_type=jnp.float32
    )
    scores = scores + jnp.einsum(
        "rhc,rlc->rhl", query_rope, cache_rope, preferred_element_type=jnp.float32
    )
    scores = scores * score_scale
    live = jnp.arange(cache_length, dtype=jnp.int32)[None, None, :] < lengths[:, None, None]
    scores = jnp.where(live, scores, jnp.float32(-1e30))
    top_score = jnp.max(scores, axis=2, keepdims=True)
    expo = jnp.where(live, jnp.exp(scores - top_score), jnp.float32(0.0))
    probs = (expo / jnp.sum(expo, axis=2, keepdims=True)).astype(jnp.bfloat16)
    head_latent = jnp.einsum(
        "rhl,rlc->rhc", probs, cache_latent, preferred_element_type=jnp.float32
    ).astype(jnp.bfloat16)
    head_values = jnp.einsum(
        "rhc,hcv->rhv", head_latent, value_up, preferred_element_type=jnp.float32
    ).astype(jnp.bfloat16)
    attended = lax.psum_scatter(
        jnp.einsum("rhv,hvd->rd", head_values, out_proj, preferred_element_type=jnp.float32).astype(
            jnp.bfloat16
        ),
        "ffn",
        scatter_dimension=0,
        tiled=True,
    ).astype(jnp.float32)
    mixed_in = residual.astype(jnp.float32) + attended
    inverse = lax.rsqrt(jnp.mean(mixed_in * mixed_in, axis=1, keepdims=True) + 1e-06)
    normed = (mixed_in * inverse * norm_gain.astype(jnp.float32)[None, :]).astype(jnp.bfloat16)
    owners = lax.axis_size("ffn")
    top_count = expert_ids.shape[1]
    capacity = min(row_count, row_count * top_count // owners + 1)
    width = residual.shape[1]
    expert_range = jnp.arange(owners, dtype=jnp.int32)
    named = expert_ids[:, :, None] == expert_range[None, None, :]
    routed = jnp.sum(named.astype(jnp.int32), axis=1)
    weight_table = jnp.sum(jnp.where(named, route_weights[:, :, None], jnp.float32(0.0)), axis=1)
    slot_rank = jnp.cumsum(routed, axis=0) - routed
    slot_range = jnp.arange(capacity, dtype=jnp.int32)
    placed = (routed.T[:, None, :] == 1) & (slot_rank.T[:, None, :] == slot_range[None, :, None])
    outgoing = jnp.einsum(
        "ecr,rd->ecd", placed.astype(jnp.bfloat16), normed, preferred_element_type=jnp.float32
    ).astype(jnp.bfloat16)
    arrived = lax.all_to_all(outgoing, "ffn", split_axis=0, concat_axis=0, tiled=True)
    flat_rows = arrived.reshape(owners * capacity, width)
    block_rows = lax.all_gather(flat_rows, "attn", axis=0, tiled=True)
    gate = jnp.dot(block_rows, gate_proj[0], preferred_element_type=jnp.float32)
    upper = jnp.dot(block_rows, up_proj[0], preferred_element_type=jnp.float32)
    hidden = (jax.nn.silu(gate) * upper).astype(jnp.bfloat16)
    partial_value = jnp.dot(hidden, down_proj[0], preferred_element_type=jnp.float32)
    summed = lax.psum_scatter(
        partial_value.astype(jnp.bfloat16), "attn", scatter_dimension=0, tiled=True
    )
    returned = lax.all_to_all(
        summed.reshape(owners, capacity, width), "ffn", split_axis=0, concat_axis=0, tiled=True
    )
    weighting = placed.astype(jnp.float32) * weight_table.T[:, None, :]
    routed_sum = jnp.einsum(
        "ecr,ecd->rd", weighting, returned.astype(jnp.float32), precision=lax.Precision.HIGHEST
    )
    return (mixed_in + routed_sum).astype(jnp.bfloat16)


def solution(mesh):
    return jax.shard_map(
        local,
        mesh=mesh,
        in_specs=(
            P("attn", "ffn", None),
            P("attn", "ffn", None),
            P("attn", None, None),
            P("attn", None, None),
            P("attn"),
            P("ffn", None, None),
            P("ffn", None, None),
            P(("attn", "ffn"), None),
            P(),
            P(("attn", "ffn"), None),
            P(("attn", "ffn"), None),
            P("ffn", None, "attn"),
            P("ffn", None, "attn"),
            P("ffn", "attn", None),
        ),
        out_specs=P(("attn", "ffn"), None),
        check_vma=False,
    )
```

profile of v0, /device:TPU:0, one launch (start us, length us, event | category | flops | bytes accessed | tf_op | source)
XLA Modules:
  0.0 286.8 jit_solution(5855977979135425560)
XLA Ops:
  6.5 3.4 %copy.28 = bf16[96,64,64]{2,1,0:T(8,128)(2,1)S(1)} copy(bf16[96,64,64]{0,2,1:T(8,128)(2,1)} %param.17) | data formatting | bytes 1572864 | tf_op args[3]
  9.9 1.0 copy.27
  10.9 0.7 iota_compare_fusion
  11.6 4.6 %fusion.47 = f32[96,4,64]{2,1,0:T(4,128)S(1)} fusion(bf16[96,4,512]{2,1,0:T(4,128)(2,1)} %param.14, bf16[96,64,512]{2,1,0:T(8,128)(2,1)} %param.16), kind=kOutput, calls=%fused_computation.56 | convolution fusion | flops 25165824 | bytes 6782976 | tf_op jit(solution)/shard_map/rhc,rlc->rhl/dot_general | solution.py:26
  16.3 1.1 fusion.46
  17.4 3.8 %convolution_convert_fusion.2 = bf16[96,4,512]{2,1,0:T(4,128)(2,1)S(1)} fusion(bf16[96,64,512]{2,1,0:T(8,128)(2,1)} %param.16, f32[96,4,64]{2,1,0:T(4,128)S(1)} %get-tuple-element.6, f32[96,4]{1,0:T(8,128)S(1)} %get-tuple-element.5), kind=kOutput, calls=%fused_computation.13 | convolution fusion | flops 25411584 | bytes 6784512 | tf_op jit(solution)/shard_map/rhl,rlc->rhc/dot_general | solution.py:38
  21.1 0.0 copy-start.3
  21.2 0.0 copy-start.5
  21.2 0.0 copy-start.2
  21.2 5.7 %fusion.1 = bf16[96,7168]{1,0:T(8,128)(2,1)} fusion(bf16[4,128,7168]{2,1,0:T(8,128)(2,1)} %param.20, bf16[4,512,128]{2,1,0:T(8,128)(2,1)S(1)} %copy-done, bf16[96,4,512]{2,1,0:T(4,128)(2,1)S(1)} %convolution_convert_fusion.2), kind=kOutput, calls=%fused_computation.3 | convolution fusion | flops 755712000 | bytes 9633792 | tf_op jit(solution)/shard_map/rhv,hvd->rd/dot_general | solution.py:45
  26.9 0.0 all-reduce.3.cloned.1.call-update
  26.9 0.0 all-gather.2.cloned.1.call-start
  27.0 0.6 dynamic-slice
  28.2 0.1 convert_reduce_fusion
  28.4 88.7 %all-reduce.3.cloned.1.call-done = bf16[96,7168]{1,0:T(8,128)(2,1)} async-done(((bf16[96,7168]{1,0:T(8,128)(2,1)}), bf16[96,7168]{1,0:T(8,128)(2,1)}) %all-reduce.3.cloned.1.call-update) | async-done | bytes 1376272
  117.1 1.1 multiply_reduce_fusion
  118.2 1.4 convolution_convert_fusion.1
  119.6 0.7 copy.30
  120.4 18.4 %all_to_all.10 = bf16[16,4,7168]{2,1,0:T(4,128)(2,1)S(1)} all-to-all(bf16[16,4,7168]{2,1,0:T(4,128)(2,1)S(1)} %copy.30), channel_id=1, replica_groups=mesh['attn'=8,'ffn'=16] {'ffn'}, dimensions={0} | all-to-all | bytes 1835008 | tf_op jit(solution)/shard_map/all_to_all | solution.py:69
  138.8 1.1 reshape.44
  139.9 0.0 all-gather.2.cloned.1.call-update
  140.0 0.2 reduce-scatter.2.cloned.1.call-start
  140.2 43.3 %all-gather.2.cloned.1.call-done = bf16[512,7168]{1,0:T(8,128)(2,1)} async-done(((bf16[64,7168]{1,0:T(8,128)(2,1)}), bf16[512,7168]{1,0:T(8,128)(2,1)}) %all-gather.2.cloned.1.call-update) | async-done | bytes 7340048 | tf_op jit(solution)/shard_map/all_gather | solution.py:71
  183.5 6.2 %fusion.7 = f32[512,256]{1,0:T(8,128)S(1)} fusion(bf16[512,7168]{1,0:T(8,128)(2,1)} %all-gather.2.cloned.1.call-done, bf16[1,7168,256]{2,1,0:T(8,128)(2,1)} %param.25), kind=kOutput, calls=%fused_computation.11 | convolution fusion | flops 1879048192 | bytes 11534336 | tf_op jit(solution)/shard_map/dot_general | solution.py:72
  189.7 16.0 %convolution_convert_fusion = bf16[512,7168]{1,0:T(8,128)(2,1)} fusion(bf16[1,256,7168]{2,1,0:T(8,128)(2,1)} %param.27, bf16[512,7168]{1,0:T(8,128)(2,1)} %all-gather.2.cloned.1.call-done, bf16[1,7168,256]{2,1,0:T(8,128)(2,1)} %param.26, f32[512,256]{1,0:T(8,128)S(1)} %fusion.7), kind=kOutput, calls=%fused_computation.1 | convolution fusion | flops 3762552832 | bytes 22544384 | tf_op jit(solution)/shard_map/dot_general | solution.py:75
  205.7 0.0 reduce-scatter.2.cloned.1.call-update
  205.7 47.7 %reduce-scatter.2.cloned.1.call-done = bf16[64,7168]{1,0:T(8,128)(2,1)} async-done(((bf16[512,7168]{1,0:T(8,128)(2,1)}), bf16[64,7168]{1,0:T(8,128)(2,1)}) %reduce-scatter.2.cloned.1.call-update) | async-done | bytes 917520 | tf_op jit(solution)/shard_map/reduce_scatter | solution.py:76
  253.4 2.5 reshape.45
  255.9 6.9 %all-to-all-start.1 = ((bf16[16,4,7168]{2,1,0:T(4,128)(2,1)}), bf16[16,4,7168]{2,1,0:T(4,128)(2,1)S(1)}, u32[]{:S(2)}, u32[]{:S(2)}) async-start(bf16[16,4,7168]{2,1,0:T(4,128)(2,1)} %reshape.45), calls=%async_computation.2 | async-start | bytes 1835008 | tf_op jit(solution)/shard_map/all_to_all | solution.py:79
  262.9 0.1 select_reduce_fusion
  263.0 15.0 %all-to-all-done.1 = bf16[16,4,7168]{2,1,0:T(4,128)(2,1)S(1)} async-done(((bf16[16,4,7168]{2,1,0:T(4,128)(2,1)}), bf16[16,4,7168]{2,1,0:T(4,128)(2,1)S(1)}, u32[]{:S(2)}, u32[]{:S(2)}) %all-to-all-start.1) | async-done | bytes 917536 | tf_op jit(solution)/shard_map/all_to_all | solution.py:79
  278.0 2.2 fusion.3
  (15 shorter events, 0.1 us)
Async XLA Ops:
  6.5 14.6 %copy-start = (bf16[4,512,128]{2,1,0:T(8,128)(2,1)S(1)}, bf16[4,512,128]{2,1,0:T(8,128)(2,1)}, u32[]{:S(2)}) copy-start(bf16[4,512,128]{2,1,0:T(8,128)(2,1)} %param.19) | copy-start | bytes 1572868
  6.5 110.5 %all-reduce.3.cloned.1.call-start = ((), (), s32[]{:S(2)}) async-start(), calls=%async_computation.5 | async-start | bytes 2752512
  21.1 5.8 %copy-start.3 = (bf16[7168]{0:T(1024)(128)(2,1)S(1)}, bf16[7168]{0:T(1024)(128)(2,1)}, u32[]{:S(2)}) copy-start(bf16[7168]{0:T(1024)(128)(2,1)} %param.22) | copy-start | bytes 43012
  21.2 5.8 %copy-start.5 = (u32[128]{0:T(128)S(1)}, u32[128]{0:T(128)}, u32[]{:S(2)}) copy-start(u32[128]{0:T(128)} %constant.36) | copy-start | bytes 1540
  21.2 7.1 %copy-start.2 = (s32[6,8]{1,0:T(8,128)S(1)}, s32[6,8]{1,0:T(8,128)}, u32[]{:S(2)}) copy-start(s32[6,8]{1,0:T(8,128)} %param.23) | copy-start | bytes 580
  21.2 95.9 %copy-start.1 = (bf16[6,7168]{1,0:T(8,128)(2,1)S(1)}, bf16[6,7168]{1,0:T(8,128)(2,1)}, u32[]{:S(2)}) copy-start(bf16[6,7168]{1,0:T(8,128)(2,1)} %param.21) | copy-start | bytes 258052
  26.9 156.6 %all-gather.2.cloned.1.call-start = ((), (), s32[]{:S(2)}) async-start(), calls=%async_computation.3 | async-start | bytes 8257536 | tf_op jit(solution)/shard_map/all_gather | solution.py:71
  140.0 113.5 %reduce-scatter.2.cloned.1.call-start = ((), (), s32[]{:S(2)}) async-start(), calls=%async_computation.4 | async-start | bytes 8257536 | tf_op jit(solution)/shard_map/reduce_scatter | solution.py:76
  205.7 57.2 %copy-start.4 = (f32[6,8]{1,0:T(8,128)S(1)}, f32[6,8]{1,0:T(8,128)}, u32[]{:S(2)}) copy-start(f32[6,8]{1,0:T(8,128)} %param.24) | copy-start | bytes 580
  255.9 22.1 %all-to-all-start.1 = ((bf16[16,4,7168]{2,1,0:T(4,128)(2,1)}), bf16[16,4,7168]{2,1,0:T(4,128)(2,1)S(1)}, u32[]{:S(2)}, u32[]{:S(2)}) async-start(bf16[16,4,7168]{2,1,0:T(4,128)(2,1)} %reshape.45), calls=%async_computation.2 | async-start | bytes 1835008 | tf_op jit(solution)/shard_map/all_to_all | solution.py:79
Sparse Core Ops, SparseCore 0:
  27.0 89.9 all-reduce.2
  140.1 43.3 all-gather.1
  205.8 47.5 reduce-scatter.1
where the time goes:
time: 288 us; the launch traced here: 287 us
  waiting for transfers between devices  195 us (68%)
  matrix products  41.1 us (14%)
  blocking collectives  18.4 us (6%)
  between operations  13.9 us (5%)
  local copies, waits for them, and re-layouts  9.31 us (3%)
  starting transfers between devices  7.21 us (3%)
    unnamed x4, waiting for transfers between devices  88.7 us
    reduce_scatter x1, waiting for transfers between devices, local(): lax.psum_scatter(partial_value.astype(jnp.bfloat16), 'attn', scatter_dime...  47.7 us
    all_gather x1, waiting for transfers between devices, local(): block_rows = lax.all_gather(flat_rows, 'attn', axis=0, tiled=True)  43.3 us
    all_to_all x1, blocking collectives, local(): lax.all_to_all(outgoing, 'ffn', split_axis=0, concat_axis=0, tiled=True)  18.4 us
    dot_general x1, matrix products, local(): jnp.dot(hidden, down_proj[0], preferred_element_type=jnp.float32)  16 us
    all_to_all x1, waiting for transfers between devices, local(): lax.all_to_all(summed.reshape(owners, capacity, width), 'ffn', split_axis...  15 us
    all_to_all x1, starting transfers between devices, local(): lax.all_to_all(summed.reshape(owners, capacity, width), 'ffn', split_axis...  6.94 us
    dot_general x1, matrix products, local(): gate = jnp.dot(block_rows, gate_proj[0], preferred_element_type=jnp.float32)  6.18 us
  transfers between devices with their start and end apart: 4, of which 4 were waited for; matrix products, arithmetic and copies ran while one was open for 0% of the time, Pallas kernels for 0%

commit v1 on v0

--- a/solution.py
+++ b/solution.py
@@ -41,21 +41,29 @@
     head_values = jnp.einsum(
         "rhc,hcv->rhv", head_latent, value_up, preferred_element_type=jnp.float32
     ).astype(jnp.bfloat16)
-    attended = lax.psum_scatter(
-        jnp.einsum("rhv,hvd->rd", head_values, out_proj, preferred_element_type=jnp.float32).astype(
-            jnp.bfloat16
-        ),
-        "ffn",
-        scatter_dimension=0,
-        tiled=True,
-    ).astype(jnp.float32)
+    owners = lax.axis_size("ffn")
+    width = residual.shape[1]
+    parts = 4
+    projected = jnp.einsum(
+        "rhv,hvd->rd", head_values, out_proj, preferred_element_type=jnp.float32
+    ).astype(jnp.bfloat16)
+    pieces = (
+        projected.reshape(owners, row_count, parts, width // parts)
+        .transpose(0, 2, 1, 3)
+        .reshape(owners, parts * row_count, width // parts)
+    )
+    pieces = lax.all_to_all(pieces, "ffn", split_axis=0, concat_axis=0, tiled=True)
+    attended = (
+        jnp.sum(pieces.astype(jnp.float32), axis=0)
+        .reshape(parts, row_count, width // parts)
+        .transpose(1, 0, 2)
+        .reshape(row_count, width)
+    )
     mixed_in = residual.astype(jnp.float32) + attended
     inverse = lax.rsqrt(jnp.mean(mixed_in * mixed_in, axis=1, keepdims=True) + 1e-06)
     normed = (mixed_in * inverse * norm_gain.astype(jnp.float32)[None, :]).astype(jnp.bfloat16)
-    owners = lax.axis_size("ffn")
     top_count = expert_ids.shape[1]
     capacity = min(row_count, row_count * top_count // owners + 1)
-    width = residual.shape[1]
     expert_range = jnp.arange(owners, dtype=jnp.int32)
     named = expert_ids[:, :, None] == expert_range[None, None, :]
     routed = jnp.sum(named.astype(jnp.int32), axis=1)

time: 288 us -> 225 us (0.78)
  waiting for transfers between devices: 195 us -> 128 us
  starting transfers between devices: 7.21 us -> 15.2 us
  matrix products: 41.1 us -> 38.1 us
    unnamed x4 -> x2, waiting for transfers between devices: 88.7 us -> 0.03 us
    all_to_all x0 -> x1, waiting for transfers between devices: none -> 21.3 us  [local(): lax.all_to_all(pieces, 'ffn', split_axis=0, concat_axis=0, tiled=True)]
    all_to_all x0 -> x1, starting transfers between devices: none -> 7.96 us  [local(): lax.all_to_all(pieces, 'ffn', split_axis=0, concat_axis=0, tiled=True)]
where the time goes in v1:
time: 225 us; the launch traced here: 224 us
  waiting for transfers between devices  128 us (57%)
  matrix products  38.1 us (17%)
  blocking collectives  17.1 us (8%)
  starting transfers between devices  15.2 us (7%)
  between operations  13.6 us (6%)
  local copies, waits for them, and re-layouts  11.5 us (5%)
    reduce_scatter x1, waiting for transfers between devices, local(): lax.psum_scatter(partial_value.astype(jnp.bfloat16), 'attn', scatter_dime...  47.7 us
    all_gather x1, waiting for transfers between devices, local(): block_rows = lax.all_gather(flat_rows, 'attn', axis=0, tiled=True)  43.5 us
    all_to_all x1, waiting for transfers between devices, local(): lax.all_to_all(pieces, 'ffn', split_axis=0, concat_axis=0, tiled=True)  21.3 us
    all_to_all x1, blocking collectives, local(): lax.all_to_all(outgoing, 'ffn', split_axis=0, concat_axis=0, tiled=True)  17.1 us
    dot_general x1, matrix products, local(): jnp.dot(hidden, down_proj[0], preferred_element_type=jnp.float32)  16 us
    all_to_all x1, waiting for transfers between devices, local(): lax.all_to_all(summed.reshape(owners, capacity, width), 'ffn', split_axis...  15 us
    all_to_all x1, starting transfers between devices, local(): lax.all_to_all(pieces, 'ffn', split_axis=0, concat_axis=0, tiled=True)  7.96 us
    all_to_all x1, starting transfers between devices, local(): lax.all_to_all(summed.reshape(owners, capacity, width), 'ffn', split_axis...  6.94 us
  transfers between devices with their start and end apart: 4, of which 4 were waited for; matrix products, arithmetic and copies ran while one was open for 0% of the time, Pallas kernels for 0%

profile of v1, /device:TPU:0, one launch (start us, length us, event | category | flops | bytes accessed | tf_op | source)
XLA Modules:
  0.0 224.4 jit_solution(411355490756260810)
XLA Ops:
  6.5 3.4 %copy.31 = bf16[96,64,64]{2,1,0:T(8,128)(2,1)S(1)} copy(bf16[96,64,64]{0,2,1:T(8,128)(2,1)} %param.17) | data formatting | bytes 1572864 | tf_op args[3]
  9.9 1.0 copy.30
  10.9 0.7 iota_compare_fusion
  11.6 4.6 %fusion.45 = f32[96,4,64]{2,1,0:T(4,128)S(1)} fusion(bf16[96,4,512]{2,1,0:T(4,128)(2,1)} %param.14, bf16[96,64,512]{2,1,0:T(8,128)(2,1)} %param.16), kind=kOutput, calls=%fused_computation.55 | convolution fusion | flops 25165824 | bytes 6782976 | tf_op jit(solution)/shard_map/rhc,rlc->rhl/dot_general | solution.py:26
  16.3 1.1 fusion.44
  17.4 3.8 %convolution_convert_fusion.2 = bf16[96,4,512]{2,1,0:T(4,128)(2,1)S(1)} fusion(bf16[96,64,512]{2,1,0:T(8,128)(2,1)} %param.16, f32[96,4,64]{2,1,0:T(4,128)S(1)} %get-tuple-element.6, f32[96,4]{1,0:T(8,128)S(1)} %get-tuple-element.5), kind=kOutput, calls=%fused_computation.14 | convolution fusion | flops 25411584 | bytes 6784512 | tf_op jit(solution)/shard_map/rhl,rlc->rhc/dot_general | solution.py:38
  21.1 4.6 %fusion.1 = bf16[96,7168]{1,0:T(8,128)(2,1)S(1)} fusion(bf16[4,128,7168]{2,1,0:T(8,128)(2,1)} %param.20, bf16[4,512,128]{2,1,0:T(8,128)(2,1)S(1)} %copy-done, bf16[96,4,512]{2,1,0:T(4,128)(2,1)S(1)} %convolution_convert_fusion.2), kind=kOutput, calls=%fused_computation.3 | convolution fusion | flops 755712000 | bytes 9633792 | tf_op jit(solution)/shard_map/rhv,hvd->rd/dot_general | solution.py:47
  25.7 1.1 reshape.56
  26.8 0.2 copy.33
  27.1 1.5 copy.34
  28.6 8.0 %all-to-all-start = ((bf16[16,24,1792]{2,1,0:T(8,128)(2,1)}), bf16[16,24,1792]{2,1,0:T(8,128)(2,1)S(1)}, u32[]{:S(2)}, u32[]{:S(2)}) async-start(bf16[16,24,1792]{2,1,0:T(8,128)(2,1)} %copy.34), calls=%async_computation | async-start | bytes 2752512 | tf_op jit(solution)/shard_map/all_to_all | solution.py:55
  36.5 0.0 all-gather.2.cloned.1.call-start
  36.6 0.1 convert_reduce_fusion.1
  36.7 21.3 %all-to-all-done = bf16[16,24,1792]{2,1,0:T(8,128)(2,1)S(1)} async-done(((bf16[16,24,1792]{2,1,0:T(8,128)(2,1)}), bf16[16,24,1792]{2,1,0:T(8,128)(2,1)S(1)}, u32[]{:S(2)}, u32[]{:S(2)}) %all-to-all-start) | async-done | bytes 1376288 | tf_op jit(solution)/shard_map/all_to_all | solution.py:55
  58.1 0.2 convert_reduce_fusion
  58.3 0.2 multiply_reduce_fusion
  58.5 0.5 convolution_convert_fusion.1
  59.0 0.7 copy.35
  59.7 17.1 %all_to_all.15 = bf16[16,4,7168]{2,1,0:T(4,128)(2,1)S(1)} all-to-all(bf16[16,4,7168]{2,1,0:T(4,128)(2,1)S(1)} %copy.35), channel_id=1, replica_groups=mesh['attn'=8,'ffn'=16] {'ffn'}, dimensions={0} | all-to-all | bytes 1835008 | tf_op jit(solution)/shard_map/all_to_all | solution.py:77
  76.8 1.1 reshape.60
  77.9 0.0 all-gather.2.cloned.1.call-update
  77.9 0.2 reduce-scatter.2.cloned.1.call-start
  78.2 43.5 %all-gather.2.cloned.1.call-done = bf16[512,7168]{1,0:T(8,128)(2,1)} async-done(((bf16[64,7168]{1,0:T(8,128)(2,1)}), bf16[512,7168]{1,0:T(8,128)(2,1)}) %all-gather.2.cloned.1.call-update) | async-done | bytes 7340048 | tf_op jit(solution)/shard_map/all_gather | solution.py:79
  121.6 6.2 %fusion.7 = f32[512,256]{1,0:T(8,128)S(1)} fusion(bf16[512,7168]{1,0:T(8,128)(2,1)} %all-gather.2.cloned.1.call-done, bf16[1,7168,256]{2,1,0:T(8,128)(2,1)} %param.25), kind=kOutput, calls=%fused_computation.11 | convolution fusion | flops 1879048192 | bytes 11534336 | tf_op jit(solution)/shard_map/dot_general | solution.py:80
  127.8 16.0 %convolution_convert_fusion = bf16[512,7168]{1,0:T(8,128)(2,1)} fusion(bf16[1,256,7168]{2,1,0:T(8,128)(2,1)} %param.27, bf16[512,7168]{1,0:T(8,128)(2,1)} %all-gather.2.cloned.1.call-done, bf16[1,7168,256]{2,1,0:T(8,128)(2,1)} %param.26, f32[512,256]{1,0:T(8,128)S(1)} %fusion.7), kind=kOutput, calls=%fused_computation.1 | convolution fusion | flops 3762552832 | bytes 22544384 | tf_op jit(solution)/shard_map/dot_general | solution.py:83
  143.8 0.0 reduce-scatter.2.cloned.1.call-update
  143.9 47.7 %reduce-scatter.2.cloned.1.call-done = bf16[64,7168]{1,0:T(8,128)(2,1)} async-done(((bf16[512,7168]{1,0:T(8,128)(2,1)}), bf16[64,7168]{1,0:T(8,128)(2,1)}) %reduce-scatter.2.cloned.1.call-update) | async-done | bytes 917520 | tf_op jit(solution)/shard_map/reduce_scatter | solution.py:84
  191.6 2.5 %reshape.61 = bf16[16,4,7168]{2,1,0:T(4,128)(2,1)} reshape(bf16[64,7168]{1,0:T(8,128)(2,1)} %reduce-scatter.2.cloned.1.call-done) | data formatting | bytes 1835008 | tf_op jit(solution)/shard_map/reshape | solution.py:88
  194.1 6.9 %all-to-all-start.2 = ((bf16[16,4,7168]{2,1,0:T(4,128)(2,1)}), bf16[16,4,7168]{2,1,0:T(4,128)(2,1)S(1)}, u32[]{:S(2)}, u32[]{:S(2)}) async-start(bf16[16,4,7168]{2,1,0:T(4,128)(2,1)} %reshape.61), calls=%async_computation.3 | async-start | bytes 1835008 | tf_op jit(solution)/shard_map/all_to_all | solution.py:87
  201.1 0.1 select_reduce_fusion
  201.2 15.0 %all-to-all-done.2 = bf16[16,4,7168]{2,1,0:T(4,128)(2,1)S(1)} async-done(((bf16[16,4,7168]{2,1,0:T(4,128)(2,1)}), bf16[16,4,7168]{2,1,0:T(4,128)(2,1)S(1)}, u32[]{:S(2)}, u32[]{:S(2)}) %all-to-all-start.2) | async-done | bytes 917536 | tf_op jit(solution)/shard_map/all_to_all | solution.py:87
  216.2 1.3 fusion.3
  (16 shorter events, 0.1 us)
Async XLA Ops:
  6.5 14.6 %copy-start = (bf16[4,512,128]{2,1,0:T(8,128)(2,1)S(1)}, bf16[4,512,128]{2,1,0:T(8,128)(2,1)}, u32[]{:S(2)}) copy-start(bf16[4,512,128]{2,1,0:T(8,128)(2,1)} %param.19) | copy-start | bytes 1572868
  26.8 9.8 %copy-start.3 = (bf16[7168]{0:T(1024)(128)(2,1)S(1)}, bf16[7168]{0:T(1024)(128)(2,1)}, u32[]{:S(2)}) copy-start(bf16[7168]{0:T(1024)(128)(2,1)} %param.22) | copy-start | bytes 43012
  26.8 9.8 %copy-start.2 = (s32[6,8]{1,0:T(8,128)S(1)}, s32[6,8]{1,0:T(8,128)}, u32[]{:S(2)}) copy-start(s32[6,8]{1,0:T(8,128)} %param.23) | copy-start | bytes 580
  27.1 31.2 %copy-start.1 = (bf16[6,7168]{1,0:T(8,128)(2,1)S(1)}, bf16[6,7168]{1,0:T(8,128)(2,1)}, u32[]{:S(2)}) copy-start(bf16[6,7168]{1,0:T(8,128)(2,1)} %param.21) | copy-start | bytes 258052
  28.6 29.5 %all-to-all-start = ((bf16[16,24,1792]{2,1,0:T(8,128)(2,1)}), bf16[16,24,1792]{2,1,0:T(8,128)(2,1)S(1)}, u32[]{:S(2)}, u32[]{:S(2)}) async-start(bf16[16,24,1792]{2,1,0:T(8,128)(2,1)} %copy.34), calls=%async_computation | async-start | bytes 2752512 | tf_op jit(solution)/shard_map/all_to_all | solution.py:55
  36.5 85.1 %all-gather.2.cloned.1.call-start = ((), (), s32[]{:S(2)}) async-start(), calls=%async_computation.4 | async-start | bytes 8257536 | tf_op jit(solution)/shard_map/all_gather | solution.py:79
  77.9 113.6 %reduce-scatter.2.cloned.1.call-start = ((), (), s32[]{:S(2)}) async-start(), calls=%async_computation.5 | async-start | bytes 8257536 | tf_op jit(solution)/shard_map/reduce_scatter | solution.py:84
  143.9 57.2 %copy-start.4 = (f32[6,8]{1,0:T(8,128)S(1)}, f32[6,8]{1,0:T(8,128)}, u32[]{:S(2)}) copy-start(f32[6,8]{1,0:T(8,128)} %param.24) | copy-start | bytes 580
  194.1 22.1 %all-to-all-start.2 = ((bf16[16,4,7168]{2,1,0:T(4,128)(2,1)}), bf16[16,4,7168]{2,1,0:T(4,128)(2,1)S(1)}, u32[]{:S(2)}, u32[]{:S(2)}) async-start(bf16[16,4,7168]{2,1,0:T(4,128)(2,1)} %reshape.61), calls=%async_computation.3 | async-start | bytes 1835008 | tf_op jit(solution)/shard_map/all_to_all | solution.py:87
Sparse Core Ops, SparseCore 0:
  78.1 43.5 all-gather.1
  144.0 47.5 reduce-scatter.1

commit v2 on v1

v2 whole, which is shorter than its diff:
```python
import jax
import jax.numpy as jnp
from jax import lax
from jax.experimental import pallas as pl
from jax.experimental.pallas import tpu as pltpu
from jax.sharding import PartitionSpec as P

PARTS = 4
UNIT = 512
IN_RING = 9 * UNIT
OUT_RING = 10 * UNIT
F32 = jnp.float32
BF16 = jnp.bfloat16


def dot(a, b):
    return jnp.dot(a, b, preferred_element_type=F32)


def order_matrix(plane, planes, owners, capacity, dtype):
    count = planes * owners * capacity
    out = lax.broadcasted_iota(jnp.int32, (count, count), 0)
    at = lax.broadcasted_iota(jnp.int32, (count, count), 1)
    y, f, c = out // (owners * capacity), (out // capacity) % owners, out % capacity
    source = (f * planes + (y - plane + planes) % planes) * capacity + c
    return (source == at).astype(dtype)


def rest_kernel(dims, place, order, mine, other, gate, upper, out, total):
    step = pl.program_id(0)
    planes, rows = dims

    @pl.when(step == 0)
    def _():
        total[...] = jnp.zeros_like(total)

    both = jnp.concatenate([gate[0], upper[0]], axis=1)
    for at, ref in enumerate((mine, other)):
        ordered = dot(order[...], ref[...]).astype(BF16)
        total[at] += dot(ordered, both)

    @pl.when(step == pl.num_programs(0) - 1)
    def _():
        for at in range(2):
            core = place[0] if at == 0 else 1 - place[0]
            for y in range(planes):
                out[y, core] = total[at, y * rows : (y + 1) * rows]


def gate_rest(place, order, mine, other, gate_proj, up_proj, start, tile=UNIT):
    count, depth = mine.shape
    hidden = gate_proj.shape[2]
    planes = 4
    weight = pl.BlockSpec((1, tile, hidden), lambda k, p: (0, start // tile + k, 0))
    rows = pl.BlockSpec((count, tile), lambda k, p: (0, k))
    shape = (planes, 2, count // planes, 2 * hidden)
    return pl.pallas_call(
        lambda *refs: rest_kernel((planes, count // planes), *refs),
        out_shape=jax.ShapeDtypeStruct(shape, F32),
        grid_spec=pltpu.PrefetchScalarGridSpec(
            num_scalar_prefetch=1,
            grid=(depth // tile,),
            in_specs=[pl.BlockSpec((count, count), lambda k, p: (0, 0)), rows, rows, weight, weight],
            out_specs=pl.BlockSpec(shape, lambda k, p: (0, 0, 0, 0)),
            scratch_shapes=[pltpu.VMEM((2, count, 2 * hidden), F32)],
        ),
        compiler_params=pltpu.CompilerParams(vmem_limit_bytes=60 << 20),
        cost_estimate=pl.CostEstimate(
            flops=4 * count * depth * (count + 2 * hidden),
            bytes_accessed=4 * count * depth + 4 * depth * hidden,
            transcendentals=0,
        ),
    )(place, order, mine, other, gate_proj, up_proj)


def ring_kernel(rows, gate, upper, rest, out, total):
    step = pl.program_id(0)
    hidden = out.shape[1]

    @pl.when(step == 0)
    def _():
        total[...] = rest[...]

    both = jnp.concatenate([gate[0], upper[0]], axis=1)
    total[...] += dot(rows[...], both)

    @pl.when(step == pl.num_programs(0) - 1)
    def _():
        gated = total[:, :hidden]
        out[...] = (gated * jax.nn.sigmoid(gated) * total[:, hidden:]).astype(out.dtype)


def gate_ring(rows, gate_proj, up_proj, rest, tile=UNIT):
    count, depth = rows.shape
    hidden = gate_proj.shape[2]
    weight = pl.BlockSpec((1, tile, hidden), lambda k: (0, k, 0))
    whole = pl.BlockSpec((count, 2 * hidden), lambda k: (0, 0))
    return pl.pallas_call(
        ring_kernel,
        out_shape=jax.ShapeDtypeStruct((count, hidden), BF16),
        grid=(depth // tile,),
        in_specs=[pl.BlockSpec((count, tile), lambda k: (0, k)), weight, weight, whole],
        out_specs=pl.BlockSpec((count, hidden), lambda k: (0, 0)),
        scratch_shapes=[pltpu.VMEM((count, 2 * hidden), F32)],
        compiler_params=pltpu.CompilerParams(vmem_limit_bytes=60 << 20),
        cost_estimate=pl.CostEstimate(
            flops=4 * count * depth * hidden,
            bytes_accessed=2 * count * depth + 4 * depth * hidden,
            transcendentals=count * hidden,
        ),
    )(rows, gate_proj, up_proj, rest)


def local(
    query_latent,
    query_rope,
    cache_latent,
    cache_rope,
    lengths,
    value_up,
    out_proj,
    residual,
    norm_gain,
    expert_ids,
    route_weights,
    gate_proj,
    up_proj,
    down_proj,
):
    score_scale = (value_up.shape[2] + query_rope.shape[2]) ** (-0.5)
    cache_length = cache_latent.shape[1]
    row_count, width = residual.shape
    owners = lax.axis_size("ffn")
    cores = 2
    planes = lax.axis_size("attn") // cores
    core = lax.axis_index("attn") % cores
    plane = lax.axis_index("attn") // cores
    swap = [(a, a ^ 1) for a in range(planes * cores)]

    def from_plane(v, ahead):
        pairs = [
            (((y + ahead) % planes) * cores + c, y * cores + c)
            for y in range(planes)
            for c in range(cores)
        ]
        return lax.ppermute(v, "attn", pairs)

    def along_planes(v):
        return jnp.stack([v] + [from_plane(v, ahead) for ahead in range(1, planes)])

    named = expert_ids[:, :, None] == jnp.arange(owners, dtype=jnp.int32)[None, None, :]
    table = jnp.concatenate(
        [
            jnp.sum(named.astype(F32), axis=1),
            jnp.sum(jnp.where(named, route_weights[:, :, None], F32(0.0)), axis=1),
        ],
        axis=1,
    )
    tables = along_planes(table)
    capacity = min(row_count, row_count * expert_ids.shape[1] // owners + 1)

    def slots_of(table):
        routed = table[..., :owners]
        weight = table[..., owners:]
        rank = jnp.cumsum(routed, axis=-2) - routed
        routed, weight, rank = (jnp.moveaxis(v, -1, 0)[..., None, :] for v in (routed, weight, rank))
        slot = jnp.arange(capacity, dtype=jnp.int32).astype(F32)[:, None]
        placed = ((routed == 1.0) & (rank == slot)).astype(F32)
        return placed, placed * weight

    placed, weighting = slots_of(table)
    placed_all, weighting_all = slots_of(tables)
    eye = jnp.eye(planes, dtype=F32)

    def block_diagonal(v):
        spread = v[:, :, :, None, :] * eye[None, :, None, :, None]
        return spread.reshape(owners * planes * capacity, planes * row_count)

    placed = placed.reshape(owners * capacity, row_count).astype(BF16)
    weighting = weighting.reshape(owners * capacity, row_count)
    placed_all = block_diagonal(placed_all).astype(BF16)
    weighting_all = block_diagonal(weighting_all)

    scores = jnp.einsum("rhc,rlc->rhl", query_latent, cache_latent, preferred_element_type=F32)
    scores = scores + jnp.einsum("rhc,rlc->rhl", query_rope, cache_rope, preferred_element_type=F32)
    scores = scores * score_scale
    live = jnp.arange(cache_length, dtype=jnp.int32)[None, None, :] < lengths[:, None, None]
    scores = jnp.where(live, scores, F32(-1e30))
    top_score = jnp.max(scores, axis=2, keepdims=True)
    expo = jnp.where(live, jnp.exp(scores - top_score), F32(0.0))
    probs = (expo / jnp.sum(expo, axis=2, keepdims=True)).astype(BF16)
    head_latent = jnp.einsum(
        "rhl,rlc->rhc", probs, cache_latent, preferred_element_type=F32
    ).astype(BF16)
    head_values = jnp.einsum(
        "rhc,hcv->rhv", head_latent, value_up, preferred_element_type=F32
    ).astype(BF16)

    projected = jnp.einsum(
        "rhv,hvd->rd", head_values, out_proj, preferred_element_type=F32
    ).astype(BF16)
    pieces = (
        projected.reshape(owners, row_count, PARTS, width // PARTS)
        .transpose(0, 2, 1, 3)
        .reshape(owners, PARTS * row_count, width // PARTS)
    )
    pieces = lax.all_to_all(pieces, "ffn", split_axis=0, concat_axis=0, tiled=True)
    attended = (
        jnp.sum(pieces.astype(F32), axis=0)
        .reshape(PARTS, row_count, width // PARTS)
        .transpose(1, 0, 2)
        .reshape(row_count, width)
    )
    mixed = residual.astype(F32) + attended
    inverse = lax.rsqrt(jnp.mean(mixed * mixed, axis=1, keepdims=True) + 1e-06)
    normed = (mixed * inverse * norm_gain.astype(F32)[None, :]).astype(BF16)

    outgoing = dot(placed, normed[:, :IN_RING]).astype(BF16).reshape(owners, capacity, IN_RING)
    arrived = lax.all_to_all(outgoing, "ffn", split_axis=0, concat_axis=0, tiled=True)
    arrived = arrived.reshape(owners * capacity, IN_RING)

    rest = width - IN_RING
    near = along_planes(normed[:, IN_RING:]).reshape(planes * row_count, rest)
    near, arrived = lax.optimization_barrier((near, arrived))
    ring_rows = lax.all_gather(arrived, "attn", axis=0, tiled=True)
    outgoing = dot(placed_all, near).astype(BF16).reshape(owners, planes * capacity, rest)
    mine = lax.all_to_all(outgoing, "ffn", split_axis=0, concat_axis=0, tiled=True)
    mine = mine.reshape(owners * planes * capacity, rest)
    other = lax.ppermute(mine, "attn", swap)
    order = order_matrix(plane, planes, owners, capacity, BF16)
    hidden_count = gate_proj.shape[2]
    sums = gate_rest(core.reshape(1), order, mine, other, gate_proj, up_proj, IN_RING)
    sums = sums.reshape(planes * cores * owners * capacity, 2 * hidden_count)
    hidden = gate_ring(ring_rows, gate_proj, up_proj, sums)

    partial_value = dot(hidden, down_proj[0, :, :OUT_RING]).astype(BF16)
    hidden, partial_value = lax.optimization_barrier((hidden, partial_value))
    summed = lax.psum_scatter(partial_value, "attn", scatter_dimension=0, tiled=True)

    by_core = hidden.reshape(planes, cores, owners * capacity, hidden_count)

    def share(core):
        rows = lax.dynamic_index_in_dim(by_core, core, 1, False)
        rows = rows.reshape(planes * owners * capacity, hidden_count)
        rows = dot(order.T, rows).astype(BF16)
        return dot(rows, down_proj[0, :, OUT_RING:])

    rest = width - OUT_RING
    theirs = lax.ppermute(share(1 - core).astype(BF16), "attn", swap)
    ours = (share(core) + theirs.astype(F32)).astype(BF16)
    ours = ours.reshape(owners, planes * capacity, rest)
    ours = lax.all_to_all(ours, "ffn", split_axis=0, concat_axis=0, tiled=True)
    ours = jnp.einsum(
        "sr,sd->rd",
        weighting_all,
        ours.reshape(owners * planes * capacity, rest).astype(F32),
        precision=lax.Precision.HIGHEST,
    ).astype(BF16)
    ours = ours.reshape(planes, row_count, rest)
    sum_rest = ours[0].astype(F32)
    for ahead in range(1, planes):
        sum_rest = sum_rest + from_plane(ours[planes - ahead], ahead).astype(F32)

    returned = lax.all_to_all(
        summed.reshape(owners, capacity, OUT_RING), "ffn", split_axis=0, concat_axis=0, tiled=True
    )
    sum_ring = jnp.einsum(
        "sr,sd->rd",
        weighting,
        returned.reshape(owners * capacity, OUT_RING).astype(F32),
        precision=lax.Precision.HIGHEST,
    )
    return (mixed + jnp.concatenate([sum_ring, sum_rest], axis=1)).astype(BF16)


def solution(mesh):
    return jax.shard_map(
        local,
        mesh=mesh,
        in_specs=(
            P("attn", "ffn", None),
            P("attn", "ffn", None),
            P("attn", None, None),
            P("attn", None, None),
            P("attn"),
            P("ffn", None, None),
            P("ffn", None, None),
            P(("attn", "ffn"), None),
            P(),
            P(("attn", "ffn"), None),
            P(("attn", "ffn"), None),
            P("ffn", None, "attn"),
            P("ffn", None, "attn"),
            P("ffn", "attn", None),
        ),
        out_specs=P(("attn", "ffn"), None),
        check_vma=False,
    )
```

time: 225 us -> 196 us (0.87)
  waiting for transfers between devices: 128 us -> 64.6 us
  starting transfers between devices: 15.2 us -> 35.7 us
  Pallas kernels: 0 us -> 16.8 us
  matrix products: 38.1 us -> 28.2 us
  local copies, waits for them, and re-layouts: 11.5 us -> 13.8 us
    reduce_scatter x1, waiting for transfers between devices: 47.7 us -> 0.39 us  [local(): lax.psum_scatter(partial_value, 'attn', scatter_dimension=0, tiled=True)]
    all_gather x1, waiting for transfers between devices: 43.5 us -> 0.01 us  [local(): ring_rows = lax.all_gather(arrived, 'attn', axis=0, tiled=True)]
    pallas_call x0 -> x2, Pallas kernels: none -> 16.8 us  [the longest x1 9.65 us: gate_ring(): pl.pallas_call(ring_kernel, out_shape=jax.ShapeDtypeStruct((count, hidden...]
    all_to_all x1 -> x3, waiting for transfers between devices: 15 us -> 29.8 us  [the longest x1 18.1 us: local(): ours = lax.all_to_all(ours, 'ffn', split_axis=0, concat_axis=0, tiled=True)]
    ppermute x0 -> x11, waiting for transfers between devices: none -> 13.5 us  [the longest x9 8.18 us: from_plane(): return lax.ppermute(v, 'attn', pairs)]
    ppermute x0 -> x11, starting transfers between devices: none -> 12.7 us  [the longest x9 12.6 us: from_plane(): return lax.ppermute(v, 'attn', pairs)]
    dot_general x6 -> x9, matrix products: 32.4 us -> 22.6 us  [the longest x5 13.2 us: dot(): return jnp.dot(a, b, preferred_element_type=F32)]
    all_to_all x1 -> x3, starting transfers between devices: 6.94 us -> 14.8 us  [the longest x1 7.56 us: local(): lax.all_to_all(summed.reshape(owners, capacity, OUT_RING), 'ffn', split_a...]
  transfers between devices with their start and end apart: 4 -> 17, of which waited for: 4 -> 12; matrix products, arithmetic and copies ran while one was open for 0% -> 7% of each run, Pallas kernels for 0% -> 4%
where the time goes in v2:
time: 196 us; the launch traced here: 195 us
  waiting for transfers between devices  64.6 us (33%)
  starting transfers between devices  35.7 us (18%)
  matrix products  28.2 us (14%)
  blocking collectives  18.5 us (9%)
  Pallas kernels  16.8 us (9%)
  local copies, waits for them, and re-layouts  13.8 us (7%)
  between operations  13.8 us (7%)
  other arithmetic  3.44 us (2%)
    all_to_all x1, waiting for transfers between devices, local(): lax.all_to_all(pieces, 'ffn', split_axis=0, concat_axis=0, tiled=True)  20.9 us
    all_to_all x1, blocking collectives, local(): lax.all_to_all(outgoing, 'ffn', split_axis=0, concat_axis=0, tiled=True)  18.5 us
    all_to_all x1, waiting for transfers between devices, local(): ours = lax.all_to_all(ours, 'ffn', split_axis=0, concat_axis=0, tiled=True)  18.1 us
    dot_general x5, matrix products, dot(): return jnp.dot(a, b, preferred_element_type=F32)  13.2 us
    ppermute x9, starting transfers between devices, from_plane(): return lax.ppermute(v, 'attn', pairs)  12.6 us
    all_to_all x1, waiting for transfers between devices, local(): lax.all_to_all(summed.reshape(owners, capacity, OUT_RING), 'ffn', split_a...  10.5 us
    pallas_call x1, Pallas kernels, gate_ring(): pl.pallas_call(ring_kernel, out_shape=jax.ShapeDtypeStruct((count, hidden...  9.65 us
    ppermute x9, waiting for transfers between devices, from_plane(): return lax.ppermute(v, 'attn', pairs)  8.18 us
  transfers between devices with their start and end apart: 17, of which 12 were waited for; matrix products, arithmetic and copies ran while one was open for 7% of the time, Pallas kernels for 4%

profile of v2, /device:TPU:0, one launch (start us, length us, event | category | flops | bytes accessed | tf_op | source)
XLA Modules:
  0.0 194.8 jit_solution(1511300378149461620)
XLA Ops:
  6.5 3.4 %copy.40 = bf16[96,64,64]{2,1,0:T(8,128)(2,1)S(1)} copy(bf16[96,64,64]{0,2,1:T(8,128)(2,1)} %param.17) | data formatting | bytes 1572864 | tf_op args[3]
  11.0 4.5 %fusion.43 = f32[96,4,64]{2,1,0:T(4,128)S(1)} fusion(bf16[96,4,512]{2,1,0:T(4,128)(2,1)S(1)} %copy-done.4, bf16[96,64,512]{2,1,0:T(8,128)(2,1)} %param.16), kind=kOutput, calls=%fused_computation.98 | convolution fusion | flops 25165824 | bytes 6782976 | tf_op jit(solution)/shard_map/rhc,rlc->rhl/dot_general | solution.py:184
  15.5 1.1 fusion.42
  16.6 3.8 %convolution_convert_fusion.5 = bf16[96,4,512]{2,1,0:T(4,128)(2,1)S(1)} fusion(bf16[96,64,512]{2,1,0:T(8,128)(2,1)} %param.16, f32[96,4,64]{2,1,0:T(4,128)S(1)} %get-tuple-element.27, f32[96,4]{1,0:T(8,128)S(1)} %get-tuple-element.26), kind=kOutput, calls=%fused_computation.13 | convolution fusion | flops 25411584 | bytes 6784512 | tf_op jit(solution)/shard_map/rhl,rlc->rhc/dot_general | solution.py:192
  20.4 4.6 %fusion.1 = bf16[96,7168]{1,0:T(8,128)(2,1)S(1)} fusion(bf16[4,128,7168]{2,1,0:T(8,128)(2,1)} %param.20, bf16[4,512,128]{2,1,0:T(8,128)(2,1)S(1)} %copy-done, bf16[96,4,512]{2,1,0:T(4,128)(2,1)S(1)} %convolution_convert_fusion.5), kind=kOutput, calls=%fused_computation.2 | convolution fusion | flops 755712000 | bytes 9633792 | tf_op jit(solution)/shard_map/rhv,hvd->rd/dot_general | solution.py:199
  25.0 1.1 reshape.150
  26.3 1.5 copy.43
  27.8 8.1 %all-to-all-start = ((bf16[16,24,1792]{2,1,0:T(8,128)(2,1)}), bf16[16,24,1792]{2,1,0:T(8,128)(2,1)S(1)}, u32[]{:S(2)}, u32[]{:S(2)}) async-start(bf16[16,24,1792]{2,1,0:T(8,128)(2,1)} %copy.43), calls=%async_computation | async-start | bytes 2752512 | tf_op jit(solution)/shard_map/all_to_all | solution.py:207
  36.6 20.9 %all-to-all-done = bf16[16,24,1792]{2,1,0:T(8,128)(2,1)S(1)} async-done(((bf16[16,24,1792]{2,1,0:T(8,128)(2,1)}), bf16[16,24,1792]{2,1,0:T(8,128)(2,1)S(1)}, u32[]{:S(2)}, u32[]{:S(2)}) %all-to-all-start) | async-done | bytes 1376288 | tf_op jit(solution)/shard_map/all_to_all | solution.py:207
  59.3 3.6 %all-to-all-start.1 = ((bf16[16,4,4608]{2,1,0:T(4,128)(2,1)}), bf16[16,4,4608]{2,1,0:T(4,128)(2,1)S(1)}, u32[]{:S(2)}, u32[]{:S(2)}) async-start(bf16[16,4,4608]{2,1,0:T(4,128)(2,1)} %reshape.155), calls=%async_computation.1 | async-start | bytes 1179648 | tf_op jit(solution)/shard_map/all_to_all | solution.py:219
  62.9 3.1 %collective-permute-start = (bf16[6,2560]{1,0:T(8,128)(2,1)S(1)}, bf16[6,2560]{1,0:T(8,128)(2,1)S(1)}, u32[]{:S(2)}, u32[]{:S(2)}) collective-permute-start(bf16[6,2560]{1,0:T(8,128)(2,1)S(1)} %get-tuple-element.18), channel_id=1, source_target_pairs={{32,0},{48,16},{64,32},{80,48},{96,64},{112,80},{0,96},{16,112},{3... | collective-permute-start | bytes 92168 | tf_op jit(solution)/shard_map/ppermute | solution.py:146
  67.7 3.8 %collective-permute-done.1 = bf16[6,2560]{1,0:T(8,128)(2,1)S(1)} collective-permute-done((bf16[6,2560]{1,0:T(8,128)(2,1)S(1)}, bf16[6,2560]{1,0:T(8,128)(2,1)S(1)}, u32[]{:S(2)}, u32[]{:S(2)}) %collective-permute-start.1) | collective-permute-done | bytes 30752 | tf_op jit(solution)/shard_map/ppermute | solution.py:146
  72.1 1.3 all-to-all-done.1
  73.3 1.0 reshape.156
  74.5 3.0 %collective-permute-start.3 = (f32[6,32]{1,0:T(8,128)S(1)}, f32[6,32]{1,0:T(8,128)S(1)}, u32[]{:S(2)}, u32[]{:S(2)}) collective-permute-start(f32[6,32]{1,0:T(8,128)S(1)} %pad_maximum_fusion.2), channel_id=1, source_target_pairs={{32,0},{48,16},{64,32},{80,48},{96,64},{112,80},{0,96},{16,112},{3... | collective-permute-start | bytes 2312 | tf_op jit(solution)/shard_map/ppermute | solution.py:146
  78.2 1.0 collective-permute-start.5
  79.2 3.5 %collective-permute-done.4 = f32[6,32]{1,0:T(8,128)S(1)} collective-permute-done((f32[6,32]{1,0:T(8,128)S(1)}, f32[6,32]{1,0:T(8,128)S(1)}, u32[]{:S(2)}, u32[]{:S(2)}) %collective-permute-start.4) | collective-permute-done | bytes 800 | tf_op jit(solution)/shard_map/ppermute | solution.py:146
  84.6 18.5 %all_to_all.25 = bf16[16,16,2560]{2,1,0:T(8,128)(2,1)S(1)} all-to-all(bf16[16,16,2560]{2,1,0:T(8,128)(2,1)S(1)} %bitcast.74), channel_id=1, replica_groups=mesh['attn'=8,'ffn'=16] {'ffn'}, dimensions={0} | all-to-all | bytes 2621440 | tf_op jit(solution)/shard_map/all_to_all | solution.py:227
  103.1 1.2 fusion.40.refs_1_
  104.3 1.9 collective-permute-done.6.refs_3_
  106.2 7.1 %shard_map.136 = f32[4,2,64,512]{3,2,1,0:T(8,128)} custom-call(s32[1]{0:T(128)} %bitcast.13.refs_0_, bf16[256,256]{1,0:T(8,128)(2,1)} %fusion.40.refs_1_, bf16[256,2560]{1,0:T(8,128)(2,1)} %bitcast.76, bf16[256,2560]{1,0:T(8,128)(2,1)} %collective-permute-done.6.refs_3_, bf16[1,7168,256]{2,1,0:T(8,128)(2,1)} %gate.1, bf16[1,7168,256]{2,1,0:T(8,128)(2,1)} %upper.1), custom_call_target="tpu_custom_call" | custom-call | flops 2013265920 | bytes 5242880 | tf_op jit(solution)/shard_map/pallas_call | solution.py:57
  113.4 9.6 %shard_map.137 = bf16[512,256]{1,0:T(8,128)(2,1)} custom-call(bf16[512,4608]{1,0:T(8,128)(2,1)} %all-gather.2.cloned.1.call-done.rows, bf16[1,7168,256]{2,1,0:T(8,128)(2,1)} %gate.1, bf16[1,7168,256]{2,1,0:T(8,128)(2,1)} %upper.1, f32[512,512]{1,0:T(8,128)} %bitcast.78), custom_call_target="tpu_custom_call" | custom-call | flops 2415919104 | bytes 9437184 | tf_op jit(solution)/shard_map/pallas_call | solution.py:98
  123.0 5.7 %convolution_convert_fusion = bf16[512,5120]{1,0:T(8,128)(2,1)} fusion(bf16[512,256]{1,0:T(8,128)(2,1)} %shard_map.137, bf16[1,256,7168]{2,1,0:T(8,128)(2,1)} %param.27), kind=kOutput, calls=%fused_computation.3 | convolution fusion | flops 1344798720 | bytes 8126464 | tf_op jit(solution)/shard_map/dot_general | solution.py:17
  129.7 3.2 %convolution_convert_fusion.3 = bf16[256,2048]{1,0:T(8,128)(2,1)} fusion(bf16[256,256]{1,0:T(8,128)(2,1)S(1)} %bitcast.85, bf16[1,256,7168]{2,1,0:T(8,128)(2,1)} %param.27, s32[256]{0:T(256)S(1)} %get-tuple-element.29, s32[256]{0:T(256)S(1)} %get-tuple-element.33, s32[]{:T(128)S(6)} %select_n.58, s32[256]{0:T(256)S(1)} %get-tuple-element.32, ...), kind=kOutput, calls=%fused_computation.10 | convolution fusion | flops 304676864 | bytes 2235140 | tf_op jit(solution)/shard_map/dot_general | solution.py:17
  132.9 3.4 %collective-permute-done.7 = bf16[256,2048]{1,0:T(8,128)(2,1)} collective-permute-done((bf16[256,2048]{1,0:T(8,128)(2,1)}, bf16[256,2048]{1,0:T(8,128)(2,1)}, u32[]{:S(2)}, u32[]{:S(2)}) %collective-permute-start.7) | collective-permute-done | bytes 1048608 | tf_op jit(solution)/shard_map/ppermute | solution.py:249
  136.3 3.5 %add_convert_fusion = bf16[256,2048]{1,0:T(8,128)(2,1)} fusion(bf16[256,2048]{1,0:T(8,128)(2,1)} %collective-permute-done.7, bf16[256,256]{1,0:T(8,128)(2,1)S(1)} %bitcast.84, bf16[1,256,7168]{2,1,0:T(8,128)(2,1)} %param.27, s32[256]{0:T(256)S(1)} %get-tuple-element.29, s32[256]{0:T(256)S(1)} %get-tuple-element.33, s32[]{:T(128)S(6)} %select_n.58, ...), kind=kOutput, calls=%fused_computation.12 | convolution fusion | flops 305725440 | bytes 3283716 | tf_op jit(solution)/shard_map/dot_general | solution.py:17
  139.8 3.7 %all-to-all-start.4 = ((bf16[16,16,2048]{2,1,0:T(8,128)(2,1)}), bf16[16,16,2048]{2,1,0:T(8,128)(2,1)S(1)}, u32[]{:S(2)}, u32[]{:S(2)}) async-start(bf16[16,16,2048]{2,1,0:T(8,128)(2,1)} %bitcast.30), calls=%async_computation.5 | async-start | bytes 2097152 | tf_op jit(solution)/shard_map/all_to_all | solution.py:252
  143.7 18.1 %all-to-all-done.4 = bf16[16,16,2048]{2,1,0:T(8,128)(2,1)S(1)} async-done(((bf16[16,16,2048]{2,1,0:T(8,128)(2,1)}), bf16[16,16,2048]{2,1,0:T(8,128)(2,1)S(1)}, u32[]{:S(2)}, u32[]{:S(2)}) %all-to-all-start.4) | async-done | bytes 1048608 | tf_op jit(solution)/shard_map/all_to_all | solution.py:252
  163.1 2.5 %collective-permute-start.8 = (bf16[6,2048]{1,0:T(8,128)(2,1)S(1)}, bf16[6,2048]{1,0:T(8,128)(2,1)S(1)}, u32[]{:S(2)}, u32[]{:S(2)}) collective-permute-start(bf16[6,2048]{1,0:T(8,128)(2,1)S(1)} %get-tuple-element.19), channel_id=1, source_target_pairs={{32,0},{48,16},{64,32},{80,48},{96,64},{112,80},{0,96},{16,112},{3... | collective-permute-start | bytes 73736 | tf_op jit(solution)/shard_map/ppermute | solution.py:146
  166.1 2.3 %reshape.161 = bf16[16,4,5120]{2,1,0:T(4,128)(2,1)} reshape(bf16[64,5120]{1,0:T(8,128)(2,1)} %reduce-scatter.2.cloned.1.call-done) | data formatting | bytes 1310720 | tf_op jit(solution)/shard_map/reshape | solution.py:265
  168.4 7.6 %all-to-all-start.3 = ((bf16[16,4,5120]{2,1,0:T(4,128)(2,1)}), bf16[16,4,5120]{2,1,0:T(4,128)(2,1)S(1)}, u32[]{:S(2)}, u32[]{:S(2)}) async-start(bf16[16,4,5120]{2,1,0:T(4,128)(2,1)} %reshape.161), calls=%async_computation.4 | async-start | bytes 1310720 | tf_op jit(solution)/shard_map/all_to_all | solution.py:264
  176.2 10.5 %all-to-all-done.3 = bf16[16,4,5120]{2,1,0:T(4,128)(2,1)S(1)} async-done(((bf16[16,4,5120]{2,1,0:T(4,128)(2,1)}), bf16[16,4,5120]{2,1,0:T(4,128)(2,1)S(1)}, u32[]{:S(2)}, u32[]{:S(2)}) %all-to-all-start.3) | async-done | bytes 655392 | tf_op jit(solution)/shard_map/all_to_all | solution.py:264
  (91 shorter events, 13.1 us)
Async XLA Ops:
  6.5 13.8 %copy-start = (bf16[4,512,128]{2,1,0:T(8,128)(2,1)S(1)}, bf16[4,512,128]{2,1,0:T(8,128)(2,1)}, u32[]{:S(2)}) copy-start(bf16[4,512,128]{2,1,0:T(8,128)(2,1)} %param.19) | copy-start | bytes 1572868
  6.5 4.4 %copy-start.8 = (s32[96]{0:T(128)S(1)}, s32[96]{0:T(128)}, u32[]{:S(2)}) copy-start(s32[96]{0:T(128)} %param.18) | copy-start | bytes 1156
  6.5 4.5 %copy-start.4 = (bf16[96,4,512]{2,1,0:T(4,128)(2,1)S(1)}, bf16[96,4,512]{2,1,0:T(4,128)(2,1)}, u32[]{:S(2)}) copy-start(bf16[96,4,512]{2,1,0:T(4,128)(2,1)} %param.14) | copy-start | bytes 1179652
  26.3 9.6 %copy-start.5 = (bf16[7168]{0:T(1024)(128)(2,1)S(1)}, bf16[7168]{0:T(1024)(128)(2,1)}, u32[]{:S(2)}) copy-start(bf16[7168]{0:T(1024)(128)(2,1)} %param.22) | copy-start | bytes 43012
  26.3 9.7 %copy-start.6 = (s32[6,8]{1,0:T(8,128)S(1)}, s32[6,8]{1,0:T(8,128)}, u32[]{:S(2)}) copy-start(s32[6,8]{1,0:T(8,128)} %param.23) | copy-start | bytes 580
  26.3 9.7 %copy-start.7 = (f32[6,8]{1,0:T(8,128)S(1)}, f32[6,8]{1,0:T(8,128)}, u32[]{:S(2)}) copy-start(f32[6,8]{1,0:T(8,128)} %param.24) | copy-start | bytes 580
  27.8 29.9 %copy-start.3 = (bf16[6,7168]{1,0:T(8,128)(2,1)S(1)}, bf16[6,7168]{1,0:T(8,128)(2,1)}, u32[]{:S(2)}) copy-start(bf16[6,7168]{1,0:T(8,128)(2,1)} %param.21) | copy-start | bytes 258052
  27.8 29.6 %all-to-all-start = ((bf16[16,24,1792]{2,1,0:T(8,128)(2,1)}), bf16[16,24,1792]{2,1,0:T(8,128)(2,1)S(1)}, u32[]{:S(2)}, u32[]{:S(2)}) async-start(bf16[16,24,1792]{2,1,0:T(8,128)(2,1)} %copy.43), calls=%async_computation | async-start | bytes 2752512 | tf_op jit(solution)/shard_map/all_to_all | solution.py:207
  59.3 14.0 %all-to-all-start.1 = ((bf16[16,4,4608]{2,1,0:T(4,128)(2,1)}), bf16[16,4,4608]{2,1,0:T(4,128)(2,1)S(1)}, u32[]{:S(2)}, u32[]{:S(2)}) async-start(bf16[16,4,4608]{2,1,0:T(4,128)(2,1)} %reshape.155), calls=%async_computation.1 | async-start | bytes 1179648 | tf_op jit(solution)/shard_map/all_to_all | solution.py:219
  62.9 50.5 %all-gather.2.cloned.1.call-start = ((), (), s32[]{:S(2)}) async-start(), calls=%async_computation.6 | async-start | bytes 5308416 | tf_op jit(solution)/shard_map/all_gather | solution.py:225
  62.9 4.8 %collective-permute-start = (bf16[6,2560]{1,0:T(8,128)(2,1)S(1)}, bf16[6,2560]{1,0:T(8,128)(2,1)S(1)}, u32[]{:S(2)}, u32[]{:S(2)}) collective-permute-start(bf16[6,2560]{1,0:T(8,128)(2,1)S(1)} %get-tuple-element.18), channel_id=1, source_target_pairs={{32,0},{48,16},{64,32},{80,48},{96,64},{112,80},{0,96},{16,112},{3... | collective-permute-start | bytes 92168 | tf_op jit(solution)/shard_map/ppermute | solution.py:146
  66.0 5.5 %collective-permute-start.1 = (bf16[6,2560]{1,0:T(8,128)(2,1)S(1)}, bf16[6,2560]{1,0:T(8,128)(2,1)S(1)}, u32[]{:S(2)}, u32[]{:S(2)}) collective-permute-start(bf16[6,2560]{1,0:T(8,128)(2,1)S(1)} %get-tuple-element.18), channel_id=1, source_target_pairs={{64,0},{80,16},{96,32},{112,48},{0,64},{16,80},{32,96},{48,112},{6... | collective-permute-start | bytes 92168 | tf_op jit(solution)/shard_map/ppermute | solution.py:146
  66.7 5.3 %collective-permute-start.2 = (bf16[6,2560]{1,0:T(8,128)(2,1)S(1)}, bf16[6,2560]{1,0:T(8,128)(2,1)S(1)}, u32[]{:S(2)}, u32[]{:S(2)}) collective-permute-start(bf16[6,2560]{1,0:T(8,128)(2,1)S(1)} %get-tuple-element.18), channel_id=1, source_target_pairs={{96,0},{112,16},{0,32},{16,48},{32,64},{48,80},{64,96},{80,112},{9... | collective-permute-start | bytes 92168 | tf_op jit(solution)/shard_map/ppermute | solution.py:146
  74.4 91.7 %reduce-scatter.2.cloned.1.call-start = ((), (), s32[]{:S(2)}) async-start(), calls=%async_computation.7 | async-start | bytes 5898240 | tf_op jit(solution)/shard_map/reduce_scatter | solution.py:238
  74.5 4.7 %collective-permute-start.3 = (f32[6,32]{1,0:T(8,128)S(1)}, f32[6,32]{1,0:T(8,128)S(1)}, u32[]{:S(2)}, u32[]{:S(2)}) collective-permute-start(f32[6,32]{1,0:T(8,128)S(1)} %pad_maximum_fusion.2), channel_id=1, source_target_pairs={{32,0},{48,16},{64,32},{80,48},{96,64},{112,80},{0,96},{16,112},{3... | collective-permute-start | bytes 2312 | tf_op jit(solution)/shard_map/ppermute | solution.py:146
  77.5 5.1 %collective-permute-start.4 = (f32[6,32]{1,0:T(8,128)S(1)}, f32[6,32]{1,0:T(8,128)S(1)}, u32[]{:S(2)}, u32[]{:S(2)}) collective-permute-start(f32[6,32]{1,0:T(8,128)S(1)} %pad_maximum_fusion.2), channel_id=1, source_target_pairs={{64,0},{80,16},{96,32},{112,48},{0,64},{16,80},{32,96},{48,112},{6... | collective-permute-start | bytes 2312 | tf_op jit(solution)/shard_map/ppermute | solution.py:146
  78.2 4.8 %collective-permute-start.5 = (f32[6,32]{1,0:T(8,128)S(1)}, f32[6,32]{1,0:T(8,128)S(1)}, u32[]{:S(2)}, u32[]{:S(2)}) collective-permute-start(f32[6,32]{1,0:T(8,128)S(1)} %pad_maximum_fusion.2), channel_id=1, source_target_pairs={{96,0},{112,16},{0,32},{16,48},{32,64},{48,80},{64,96},{80,112},{9... | collective-permute-start | bytes 2312 | tf_op jit(solution)/shard_map/ppermute | solution.py:146
  103.1 3.2 %copy-start.1 = (bf16[16,16,2560]{2,1,0:T(8,128)(2,1)}, bf16[16,16,2560]{2,1,0:T(8,128)(2,1)S(1)}, u32[]{:S(2)}) copy-start(bf16[16,16,2560]{2,1,0:T(8,128)(2,1)S(1)} %all_to_all.25) | copy-start | bytes 3932164
  103.1 3.2 %collective-permute-start.6 = (bf16[256,2560]{1,0:T(8,128)(2,1)S(1)}, bf16[256,2560]{1,0:T(8,128)(2,1)}, u32[]{:S(2)}, u32[]{:S(2)}) collective-permute-start(bf16[256,2560]{1,0:T(8,128)(2,1)S(1)} %bitcast.75), channel_id=1, source_target_pairs={{0,16},{16,0},{32,48},{48,32},{64,80},{80,64},{96,112},{112,96},{1... | collective-permute-start | bytes 3932168 | tf_op jit(solution)/shard_map/ppermute | solution.py:229
  128.7 0.9 copy-start.2
  132.8 3.5 %collective-permute-start.7 = (bf16[256,2048]{1,0:T(8,128)(2,1)}, bf16[256,2048]{1,0:T(8,128)(2,1)}, u32[]{:S(2)}, u32[]{:S(2)}) collective-permute-start(bf16[256,2048]{1,0:T(8,128)(2,1)} %convolution_convert_fusion.3), channel_id=1, source_target_pairs={{0,16},{16,0},{32,48},{48,32},{64,80},{80,64},{96,112},{112,96},{1... | collective-permute-start | bytes 3145736 | tf_op jit(solution)/shard_map/ppermute | solution.py:249
  139.8 22.0 %all-to-all-start.4 = ((bf16[16,16,2048]{2,1,0:T(8,128)(2,1)}), bf16[16,16,2048]{2,1,0:T(8,128)(2,1)S(1)}, u32[]{:S(2)}, u32[]{:S(2)}) async-start(bf16[16,16,2048]{2,1,0:T(8,128)(2,1)} %bitcast.30), calls=%async_computation.5 | async-start | bytes 2097152 | tf_op jit(solution)/shard_map/all_to_all | solution.py:252
  162.4 13.8 %collective-permute-start.10 = (bf16[6,2048]{1,0:T(8,128)(2,1)S(1)}, bf16[6,2048]{1,0:T(8,128)(2,1)S(1)}, u32[]{:S(2)}, u32[]{:S(2)}) collective-permute-start(bf16[6,2048]{1,0:T(8,128)(2,1)S(1)} %get-tuple-element.20), channel_id=1, source_target_pairs={{96,0},{112,16},{0,32},{16,48},{32,64},{48,80},{64,96},{80,112},{9... | collective-permute-start | bytes 73736 | tf_op jit(solution)/shard_map/ppermute | solution.py:146
  163.1 13.1 %collective-permute-start.8 = (bf16[6,2048]{1,0:T(8,128)(2,1)S(1)}, bf16[6,2048]{1,0:T(8,128)(2,1)S(1)}, u32[]{:S(2)}, u32[]{:S(2)}) collective-permute-start(bf16[6,2048]{1,0:T(8,128)(2,1)S(1)} %get-tuple-element.19), channel_id=1, source_target_pairs={{32,0},{48,16},{64,32},{80,48},{96,64},{112,80},{0,96},{16,112},{3... | collective-permute-start | bytes 73736 | tf_op jit(solution)/shard_map/ppermute | solution.py:146
  165.7 10.5 %collective-permute-start.9 = (bf16[6,2048]{1,0:T(8,128)(2,1)S(1)}, bf16[6,2048]{1,0:T(8,128)(2,1)S(1)}, u32[]{:S(2)}, u32[]{:S(2)}) collective-permute-start(bf16[6,2048]{1,0:T(8,128)(2,1)S(1)} %get-tuple-element.21), channel_id=1, source_target_pairs={{64,0},{80,16},{96,32},{112,48},{0,64},{16,80},{32,96},{48,112},{6... | collective-permute-start | bytes 73736 | tf_op jit(solution)/shard_map/ppermute | solution.py:146
  168.4 18.4 %all-to-all-start.3 = ((bf16[16,4,5120]{2,1,0:T(4,128)(2,1)}), bf16[16,4,5120]{2,1,0:T(4,128)(2,1)S(1)}, u32[]{:S(2)}, u32[]{:S(2)}) async-start(bf16[16,4,5120]{2,1,0:T(4,128)(2,1)} %reshape.161), calls=%async_computation.4 | async-start | bytes 1310720 | tf_op jit(solution)/shard_map/all_to_all | solution.py:264
Sparse Core Ops, SparseCore 0:
  74.5 33.1 all-gather.1
  128.8 37.1 reduce-scatter.1

commit v3 on v2

v3 whole, which is shorter than its diff:
```python
import math

import jax
import jax.numpy as jnp
from jax import lax
from jax.experimental import pallas as pl
from jax.experimental.pallas import tpu as pltpu
from jax.sharding import PartitionSpec as P

PARTS = 4
UNIT = 512
IN_RING = 4352
OUT_RING = 4352
F32 = jnp.float32
BF16 = jnp.bfloat16


def dot(a, b):
    return jnp.dot(a, b, preferred_element_type=F32)


GROUP = 4

def attend_kernel(
    scale,
    owners,
    parts,
    lengths,
    query,
    cache,
    query_rope,
    cache_rope,
    value_up,
    out_proj,
    out,
    rope,
    latent,
    values,
    weights,
    arrived,
):
    step = pl.program_id(0)
    heads = query.shape[1]
    depth, positions = cache.shape[2], cache.shape[1]
    rows = cache.shape[0]
    count = GROUP * heads
    width = weights.shape[1] // parts
    fetches = [
        pltpu.make_async_copy(
            out_proj.at[:, pl.ds(part * width, width)],
            weights.at[:, pl.ds(part * width, width)],
            arrived.at[part],
        )
        for part in range(parts)
    ]

    @pl.when(step == 0)
    def _():
        for fetch in fetches:
            fetch.start()
        for h in range(heads):
            vector = query_rope[h].astype(F32)
            parts = []
            for at in range(positions):
                parts.append(jnp.sum(vector * cache_rope[at].astype(F32), axis=0, keepdims=True))
            wide = jnp.concatenate(parts, axis=0).T
            rope[pl.ds(h, wide.shape[0], heads), :] = jnp.concatenate([wide] * 2, axis=1)

    groups = rows // GROUP
    total = rows * heads
    base = pl.multiple_of(step * total, total)
    keys = [
        cache[group * GROUP : (group + 1) * GROUP].reshape(GROUP * positions, depth)
        for group in range(groups)
    ]
    scores = []
    for group in range(groups):
        queries = jnp.concatenate([query[group * GROUP + i] for i in range(GROUP)], axis=0)
        scores.append(
            lax.dot_general(
                queries, keys[group], (((1,), (1,)), ((), ())), preferred_element_type=F32
            )
        )
    scores = jnp.concatenate(scores, axis=0)
    near = rope[pl.ds(base, total), :]
    scores = (scores + jnp.concatenate([near] * (GROUP // 2), axis=1)) * scale
    row = lax.broadcasted_iota(jnp.int32, scores.shape, 0) // heads
    own = lax.broadcasted_iota(jnp.int32, scores.shape, 1) - (row % GROUP) * positions
    limit = jnp.concatenate(
        [jnp.full((heads, GROUP * positions), lengths[step * rows + i], jnp.int32) for i in range(rows)],
        axis=0,
    )
    live = (own >= 0) & (own < limit)
    scores = jnp.where(live, scores, F32(-1e30))
    top = jnp.max(scores, axis=1, keepdims=True)
    expo = jnp.where(live, jnp.exp(scores - top), F32(0.0))
    probs = (expo / jnp.sum(expo, axis=1, keepdims=True)).astype(BF16)
    mixed = jnp.concatenate(
        [
            dot(probs[group * count : (group + 1) * count], keys[group])
            for group in range(groups)
        ],
        axis=0,
    )
    for part in range(depth // 128):
        latent[part, pl.ds(base, total), :] = mixed[:, part * 128 : (part + 1) * 128]

    @pl.when(step == pl.num_programs(0) - 1)
    def _():
        all_rows = values.shape[0]
        size = value_up.shape[2]
        for h in range(heads):
            mixed = jnp.concatenate(
                [latent[part, pl.ds(h, all_rows, heads), :] for part in range(depth // 128)], axis=1
            ).astype(BF16)
            values[:, h * size : (h + 1) * size] = dot(mixed, value_up[h]).astype(BF16)
        own_rows = all_rows // owners
        for part, fetch in enumerate(fetches):
            fetch.wait()
            result = dot(values[...], weights[:, part * width : (part + 1) * width]).astype(BF16)
            for f in range(owners):
                out[f, part * own_rows : (part + 1) * own_rows] = result[
                    f * own_rows : (f + 1) * own_rows
                ]


def attend(
    query, query_rope, cache, cache_rope, lengths, value_up, out_proj, scale, owners, parts, steps=2
):
    rows, heads, depth = query.shape
    positions = cache.shape[1]
    block = rows // steps
    size = heads * value_up.shape[2]
    width = out_proj.shape[2]
    shape = (owners, parts * (rows // owners), width // parts)
    whole = lambda shape: pl.BlockSpec(shape, lambda k, n: (0,) * len(shape))
    query_rope = jnp.transpose(query_rope, (1, 2, 0))
    cache_rope = jnp.transpose(cache_rope, (1, 2, 0))
    return pl.pallas_call(
        lambda *refs: attend_kernel(scale, owners, parts, *refs),
        out_shape=jax.ShapeDtypeStruct(shape, BF16),
        grid_spec=pltpu.PrefetchScalarGridSpec(
            num_scalar_prefetch=1,
            grid=(steps,),
            in_specs=[
                pl.BlockSpec((block, heads, depth), lambda k, n: (k, 0, 0)),
                pl.BlockSpec((block, positions, depth), lambda k, n: (k, 0, 0)),
                whole(query_rope.shape),
                whole(cache_rope.shape),
                whole(value_up.shape),
                pl.BlockSpec(memory_space=pl.ANY),
            ],
            out_specs=whole(shape),
            scratch_shapes=[
                pltpu.VMEM((rows * heads, 2 * positions), F32),
                pltpu.VMEM((depth // 128, rows * heads, 128), F32),
                pltpu.VMEM((rows, size), BF16),
                pltpu.VMEM((size, width), BF16),
                pltpu.SemaphoreType.DMA((parts,)),
            ],
        ),
        compiler_params=pltpu.CompilerParams(vmem_limit_bytes=60 << 20),
        cost_estimate=pl.CostEstimate(
            flops=4 * rows * heads * positions * depth * GROUP + 2 * rows * size * width,
            bytes_accessed=2 * rows * positions * depth + 2 * size * width,
            transcendentals=rows * heads * positions,
        ),
    )(lengths, query, cache, query_rope, cache_rope, value_up, out_proj.reshape(size, width))


OWNED = 4
INNER = 2
SLAB = 1024


def expert_kernel(
    place,
    rows,
    mine,
    other,
    gate_proj,
    up_proj,
    down_proj,
    out,
    theirs,
    ours,
    x,
    x_rest,
    gate_w,
    up_w,
    down_w,
    gate_rest,
    up_rest,
    gate,
    up,
    spread,
    slab,
    share,
    got,
    sent,
):
    core, plane = place[0], place[1]
    depth, rest = x.shape[1], x_rest.shape[1]
    count = mine.shape[0]
    hidden_count = gate_w.shape[1]
    planes, cores, block = gate.shape[:3]
    own = block // OWNED
    tile = depth // INNER
    size = out.shape[1]
    left = down_w.shape[1] - size
    ring_w = [(at * tile, tile) for at in range(INNER)] + [(depth, rest)]

    def fetch(source, target, sem):
        copy = pltpu.make_async_copy(source, target, sem)
        copy.start()
        return copy

    def fetch_weights(at):
        start, length = ring_w[at]
        rows_at = pl.ds(start, length)
        return [
            fetch(gate_proj.at[0, rows_at], gate_w.at[rows_at], got.at[4 * at]),
            fetch(up_proj.at[0, rows_at], up_w.at[rows_at], got.at[4 * at + 1]),
        ]

    waits = {}
    waits[INNER] = fetch_weights(INNER) + [
        fetch(mine, x_rest.at[pl.ds(0, count)], got.at[4 * INNER + 2]),
        fetch(other, x_rest.at[pl.ds(count, count)], got.at[4 * INNER + 3]),
    ]
    for at in range(INNER):
        columns = pl.ds(at * tile, tile)
        waits[at] = fetch_weights(at) + [
            fetch(rows.at[:, columns], x.at[:, columns], got.at[4 * at + 2])
        ]
    down_wait = fetch(down_proj.at[0], down_w, got.at[4 * INNER + 4])

    for copy in waits[INNER]:
        copy.wait()
    gate_rest[...] = dot(x_rest[...], gate_w[depth:])
    up_rest[...] = dot(x_rest[...], up_w[depth:])
    shape = gate.shape
    for at in range(INNER):
        for copy in waits[at]:
            copy.wait()
        start = at * tile
        part = x[:, start : start + tile]
        gate_part = dot(part, gate_w[start : start + tile]).reshape(shape)
        up_part = dot(part, up_w[start : start + tile]).reshape(shape)
        if at == 0:
            gate[...] = gate_part
            up[...] = up_part
        else:
            gate[...] += gate_part
            up[...] += up_part
    for turn in range(planes):
        y = (plane + turn) % planes
        for at in range(cores):
            c = core if at == 0 else 1 - core
            for f in range(own):
                source = slice(
                    at * count + (f * planes + turn) * OWNED,
                    at * count + (f * planes + turn + 1) * OWNED,
                )
                target = slice(f * OWNED, (f + 1) * OWNED)
                gate[y, c, target] += gate_rest[source]
                up[y, c, target] += up_rest[source]
    gated = gate[...]
    hidden = gated * jax.nn.sigmoid(gated) * up[...]
    gate[...] = hidden
    hidden = hidden.reshape(rows.shape[0], hidden_count).astype(BF16)
    for turn in range(planes):
        y = (plane + turn) % planes
        for at in range(cores):
            c = core if at == 0 else 1 - core
            for f in range(own):
                target = slice((f * planes + turn) * OWNED, (f * planes + turn + 1) * OWNED)
                spread[at, target] = gate[y, c, f * OWNED : (f + 1) * OWNED]
    down_wait.wait()
    sends = []
    for at, ref in ((1, theirs), (0, ours)):
        share[at] = dot(spread[at].astype(BF16), down_w[:, size:]).astype(BF16)
        sends.append(fetch(share.at[at], ref, sent.at[at]))
    for at in range(0, size, SLAB):
        length = min(SLAB, size - at)
        slab[:, at : at + length] = dot(hidden, down_w[:, at : at + length]).astype(BF16)
        columns = pl.ds(at, length)
        sends.append(fetch(slab.at[:, columns], out.at[:, columns], sent.at[cores + at // SLAB]))
    for copy in sends:
        copy.wait()


def expert(place, rows, mine, other, gate_proj, up_proj, down_proj, size, planes, cores, capacity):
    count, depth = rows.shape
    part, rest = mine.shape
    hidden = gate_proj.shape[2]
    width = down_proj.shape[2]
    block = count // (planes * cores)
    wide = (planes, cores, block, hidden)
    anywhere = pl.BlockSpec(memory_space=pl.ANY)
    return pl.pallas_call(
        expert_kernel,
        out_shape=(
            jax.ShapeDtypeStruct((count, size), BF16),
            jax.ShapeDtypeStruct((part, width - size), BF16),
            jax.ShapeDtypeStruct((part, width - size), BF16),
        ),
        in_specs=[pl.BlockSpec(memory_space=pltpu.SMEM)] + [anywhere] * 6,
        out_specs=[anywhere] * 3,
        scratch_shapes=[
            pltpu.VMEM((count, depth), BF16),
            pltpu.VMEM((2 * part, rest), BF16),
            pltpu.VMEM((depth + rest, hidden), BF16),
            pltpu.VMEM((depth + rest, hidden), BF16),
            pltpu.VMEM((hidden, width), BF16),
            pltpu.VMEM((2 * part, hidden), F32),
            pltpu.VMEM((2 * part, hidden), F32),
            pltpu.VMEM(wide, F32),
            pltpu.VMEM(wide, F32),
            pltpu.VMEM((cores, part, hidden), F32),
            pltpu.VMEM((count, size), BF16),
            pltpu.VMEM((cores, part, width - size), BF16),
            pltpu.SemaphoreType.DMA((4 * INNER + 5,)),
            pltpu.SemaphoreType.DMA((cores + pl.cdiv(size, SLAB),)),
        ],
        compiler_params=pltpu.CompilerParams(vmem_limit_bytes=60 << 20),
        cost_estimate=pl.CostEstimate(
            flops=6 * count * width * hidden,
            bytes_accessed=2 * count * (depth + size) + 6 * width * hidden,
            transcendentals=count * hidden,
        ),
    )(place, rows, mine, other, gate_proj, up_proj, down_proj)


def local(
    query_latent,
    query_rope,
    cache_latent,
    cache_rope,
    lengths,
    value_up,
    out_proj,
    residual,
    norm_gain,
    expert_ids,
    route_weights,
    gate_proj,
    up_proj,
    down_proj,
):
    row_count, width = residual.shape
    owners = lax.axis_size("ffn")
    cores = 2
    planes = lax.axis_size("attn") // cores
    core = lax.axis_index("attn") % cores
    plane = lax.axis_index("attn") // cores
    swap = [(a, a ^ 1) for a in range(planes * cores)]

    def from_plane(v, ahead):
        pairs = [
            (((y + ahead) % planes) * cores + c, y * cores + c)
            for y in range(planes)
            for c in range(cores)
        ]
        return lax.ppermute(v, "attn", pairs)

    def along_planes(v):
        return jnp.stack([v] + [from_plane(v, ahead) for ahead in range(1, planes)])

    named = expert_ids[:, :, None] == jnp.arange(owners, dtype=jnp.int32)[None, None, :]
    routed = jnp.sum(named.astype(F32), axis=1)
    weights = jnp.sum(jnp.where(named, route_weights[:, :, None], F32(0.0)), axis=1)
    capacity = min(row_count, row_count * expert_ids.shape[1] // owners + 1)

    def slots_of(routed, weight):
        rank = jnp.cumsum(routed, axis=-2) - routed
        routed, weight, rank = (jnp.moveaxis(v, -1, 0)[..., None, :] for v in (routed, weight, rank))
        slot = jnp.arange(capacity, dtype=jnp.int32).astype(F32)[:, None]
        placed = ((routed == 1.0) & (rank == slot)).astype(F32)
        return placed, placed * weight

    score_scale = (value_up.shape[2] + query_rope.shape[2]) ** (-0.5)
    pieces = attend(
        query_latent,
        query_rope,
        cache_latent,
        cache_rope,
        lengths,
        value_up,
        out_proj,
        score_scale,
        owners,
        PARTS,
    )
    eye = jnp.eye(planes, dtype=F32)

    def block_diagonal(v):
        spread = v[:, :, :, None, :] * eye[None, :, None, :, None]
        return spread.reshape(owners * planes * capacity, planes * row_count)

    placed, weighting = slots_of(routed, weights)
    placed = placed.reshape(owners * capacity, row_count).astype(BF16)
    weighting = weighting.reshape(owners * capacity, row_count)
    terms, left = [routed], weights
    for _ in range(3):
        term = lax.reduce_precision(left, 8, 7)
        terms.append(term)
        left = left - term
    table = jnp.pad(jnp.concatenate(terms, axis=1), ((0, 0), (0, 128 - 4 * owners))).astype(BF16)
    pieces = lax.all_to_all(pieces, "ffn", split_axis=0, concat_axis=0, tiled=True)
    attended = (
        jnp.sum(pieces.astype(F32), axis=0)
        .reshape(PARTS, row_count, width // PARTS)
        .transpose(1, 0, 2)
        .reshape(row_count, width)
    )
    mixed = residual.astype(F32) + attended
    inverse = lax.rsqrt(jnp.mean(mixed * mixed, axis=1, keepdims=True) + 1e-06)
    normed = (mixed * inverse * norm_gain.astype(F32)[None, :]).astype(BF16)

    outgoing = dot(placed, normed[:, :IN_RING]).astype(BF16).reshape(owners, capacity, IN_RING)
    near = jnp.concatenate([normed[:, IN_RING:], table], axis=1)
    arrived = lax.all_to_all(outgoing, "ffn", split_axis=0, concat_axis=0, tiled=True)
    arrived = arrived.reshape(owners * capacity, IN_RING)

    rest = width - IN_RING
    near, arrived = lax.optimization_barrier((near, arrived))
    near = along_planes(near)
    tables = near[:, :, rest:].astype(F32)
    tables = [tables[:, :, at * owners : (at + 1) * owners] for at in range(4)]
    placed_all, weighting_all = slots_of(tables[0], tables[1] + tables[2] + tables[3])
    placed_all = block_diagonal(placed_all).astype(BF16)
    weighting_all = block_diagonal(weighting_all)
    near = near[:, :, :rest].reshape(planes * row_count, rest)
    ring_rows = lax.all_gather(arrived, "attn", axis=0, tiled=True)
    outgoing = dot(placed_all, near).astype(BF16).reshape(owners, planes * capacity, rest)
    mine = lax.all_to_all(outgoing, "ffn", split_axis=0, concat_axis=0, tiled=True)
    mine = mine.reshape(owners * planes * capacity, rest)
    other = lax.ppermute(mine, "attn", swap)

    partial_value, theirs, ours = expert(
        jnp.stack([core, plane]),
        ring_rows,
        mine,
        other,
        gate_proj,
        up_proj,
        down_proj,
        OUT_RING,
        planes,
        cores,
        capacity,
    )
    summed = lax.psum_scatter(partial_value, "attn", scatter_dimension=0, tiled=True)

    rest = width - OUT_RING
    theirs = lax.ppermute(theirs, "attn", swap)
    ours = (ours.astype(F32) + theirs.astype(F32)).astype(BF16)
    ours = ours.reshape(owners, planes * capacity, rest)
    ours = lax.all_to_all(ours, "ffn", split_axis=0, concat_axis=0, tiled=True)
    ours = jnp.einsum(
        "sr,sd->rd",
        weighting_all,
        ours.reshape(owners * planes * capacity, rest).astype(F32),
        precision=lax.Precision.HIGHEST,
    ).astype(BF16)
    ours = ours.reshape(planes, row_count, rest)
    sum_rest = ours[0].astype(F32)
    for ahead in range(1, planes):
        sum_rest = sum_rest + from_plane(ours[planes - ahead], ahead).astype(F32)

    returned = lax.all_to_all(
        summed.reshape(owners, capacity, OUT_RING), "ffn", split_axis=0, concat_axis=0, tiled=True
    )
    sum_ring = jnp.einsum(
        "sr,sd->rd",
        weighting,
        returned.reshape(owners * capacity, OUT_RING).astype(F32),
        precision=lax.Precision.HIGHEST,
    )
    return (mixed + jnp.concatenate([sum_ring, sum_rest], axis=1)).astype(BF16)


def solution(mesh):
    return jax.shard_map(
        local,
        mesh=mesh,
        in_specs=(
            P("attn", "ffn", None),
            P("attn", "ffn", None),
            P("attn", None, None),
            P("attn", None, None),
            P("attn"),
            P("ffn", None, None),
            P("ffn", None, None),
            P(("attn", "ffn"), None),
            P(),
            P(("attn", "ffn"), None),
            P(("attn", "ffn"), None),
            P("ffn", None, "attn"),
            P("ffn", None, "attn"),
            P("ffn", "attn", None),
        ),
        out_specs=P(("attn", "ffn"), None),
        check_vma=False,
    )
```

time: 196 us -> 175 us (0.89)
  matrix products: 28.2 us -> 1.99 us
  local copies, waits for them, and re-layouts: 13.8 us -> 5.32 us
  waiting for transfers between devices: 64.6 us -> 72.5 us
  Pallas kernels: 16.8 us -> 22.5 us
    dot_general x3 -> x0, matrix products: 12.8 us -> none  [the longest x1 4.57 us: local(): jnp.einsum('rhv,hvd->rd', head_values, out_proj, preferred_element_type=F32)]
    dot_general x5 -> x2, matrix products: 13.2 us -> 0.86 us  [dot(): return jnp.dot(a, b, preferred_element_type=F32)]
    all_to_all x1, waiting for transfers between devices: 1.25 us -> 10.1 us  [local(): lax.all_to_all(outgoing, 'ffn', split_axis=0, concat_axis=0, tiled=True)]
    pallas_call x2, Pallas kernels: 16.8 us -> 22.5 us  [the longest x1 12 us: expert(): pl.pallas_call(expert_kernel, out_shape=(jax.ShapeDtypeStruct((count, siz...]
    ppermute x9 -> x6, waiting for transfers between devices: 8.18 us -> 2.72 us  [from_plane(): return lax.ppermute(v, 'attn', pairs)]
    unnamed x20 -> x12, local copies, waits for them, and re-layouts: 5.29 us -> 0.03 us
    all_to_all x1, waiting for transfers between devices: 18.1 us -> 22.7 us  [local(): ours = lax.all_to_all(ours, 'ffn', split_axis=0, concat_axis=0, tiled=True)]
    reshape x4 -> x1, local copies, waits for them, and re-layouts: 2.84 us -> 0.05 us  [local(): near = near[:, :, :rest].reshape(planes * row_count, rest)]
  transfers between devices with their start and end apart: 17 -> 14, of which waited for: 12 -> 8; matrix products, arithmetic and copies ran while one was open for 7% -> 4% of each run, Pallas kernels for 4% -> 0%
where the time goes in v3:
time: 175 us
  waiting for transfers between devices  72.5 us (41%)
  starting transfers between devices  34.3 us (20%)
  Pallas kernels  22.5 us (13%)
  blocking collectives  19.8 us (11%)
  between operations  13.7 us (8%)
  local copies, waits for them, and re-layouts  5.32 us (3%)
  other arithmetic  4.41 us (3%)
  matrix products  1.99 us (1%)
    all_to_all x1, waiting for transfers between devices, local(): ours = lax.all_to_all(ours, 'ffn', split_axis=0, concat_axis=0, tiled=True)  22.7 us
    all_to_all x1, waiting for transfers between devices, local(): lax.all_to_all(pieces, 'ffn', split_axis=0, concat_axis=0, tiled=True)  20.9 us
    all_to_all x1, blocking collectives, local(): lax.all_to_all(outgoing, 'ffn', split_axis=0, concat_axis=0, tiled=True)  19.8 us
    pallas_call x1, Pallas kernels, expert(): pl.pallas_call(expert_kernel, out_shape=(jax.ShapeDtypeStruct((count, siz...  12 us
    pallas_call x1, Pallas kernels, attend(): pl.pallas_call(lambda *refs: attend_kernel(scale, owners, parts, *refs),...  10.5 us
    ppermute x6, starting transfers between devices, from_plane(): return lax.ppermute(v, 'attn', pairs)  10.3 us
    all_to_all x1, waiting for transfers between devices, local(): lax.all_to_all(summed.reshape(owners, capacity, OUT_RING), 'ffn', split_a...  10.2 us
    all_to_all x1, waiting for transfers between devices, local(): lax.all_to_all(outgoing, 'ffn', split_axis=0, concat_axis=0, tiled=True)  10.1 us
  transfers between devices with their start and end apart: 14, of which 8 were waited for; matrix products, arithmetic and copies ran while one was open for 4% of the time, Pallas kernels for 0%

profile of v3, /device:TPU:0, one launch (start us, length us, event | category | flops | bytes accessed | tf_op | source)
XLA Modules:
  0.0 174.5 jit_solution(14653993778826459026)
XLA Ops:
  6.5 10.5 %shard_map.136 = bf16[16,24,1792]{2,1,0:T(8,128)(2,1)} custom-call(s32[96]{0:T(128)} %refs_0_.1, bf16[96,4,512]{2,1,0:T(4,128)(2,1)} %refs_1_.1, bf16[96,64,512]{2,1,0:T(8,128)(2,1)} %refs_2_.1, bf16[4,64,96]{2,1,0:T(8,128)(2,1)} %bitcast.57, bf16[64,64,96]{2,1,0:T(8,128)(2,1)} %bitcast.47, bf16[4,512,128]{2,1,0:T(8,128)(2,1)} %refs_5_.1, ...), custom_call_target="tpu_custom_call" | custom-call | flops 905969664 | bytes 13631488 | tf_op jit(solution)/shard_map/pallas_call | solution.py:139
  17.0 8.1 %all-to-all-start = ((bf16[16,24,1792]{2,1,0:T(8,128)(2,1)}), bf16[16,24,1792]{2,1,0:T(8,128)(2,1)S(1)}, u32[]{:S(2)}, u32[]{:S(2)}) async-start(bf16[16,24,1792]{2,1,0:T(8,128)(2,1)} %shard_map.136), calls=%async_computation | async-start | bytes 2752512 | tf_op jit(solution)/shard_map/all_to_all | solution.py:410
  25.8 20.9 %all-to-all-done = bf16[16,24,1792]{2,1,0:T(8,128)(2,1)S(1)} async-done(((bf16[16,24,1792]{2,1,0:T(8,128)(2,1)}), bf16[16,24,1792]{2,1,0:T(8,128)(2,1)S(1)}, u32[]{:S(2)}, u32[]{:S(2)}) %all-to-all-start) | async-done | bytes 1376288 | tf_op jit(solution)/shard_map/all_to_all | solution.py:410
  47.2 0.4 convolution_convert_fusion
  47.6 0.9 reshape.118
  48.5 3.6 %all-to-all-start.1 = ((bf16[16,4,4352]{2,1,0:T(4,128)(2,1)}), bf16[16,4,4352]{2,1,0:T(4,128)(2,1)S(1)}, u32[]{:S(2)}, u32[]{:S(2)}) async-start(bf16[16,4,4352]{2,1,0:T(4,128)(2,1)} %reshape.118), calls=%async_computation.1 | async-start | bytes 1114112 | tf_op jit(solution)/shard_map/all_to_all | solution.py:423
  52.2 10.1 %all-to-all-done.1 = bf16[16,4,4352]{2,1,0:T(4,128)(2,1)S(1)} async-done(((bf16[16,4,4352]{2,1,0:T(4,128)(2,1)}), bf16[16,4,4352]{2,1,0:T(4,128)(2,1)S(1)}, u32[]{:S(2)}, u32[]{:S(2)}) %all-to-all-start.1) | async-done | bytes 557088 | tf_op jit(solution)/shard_map/all_to_all | solution.py:423
  62.3 1.0 reshape.119
  63.4 1.7 collective-permute-start.2
  65.0 2.9 %collective-permute-start.1 = (bf16[6,2944]{1,0:T(8,128)(2,1)S(1)}, bf16[6,2944]{1,0:T(8,128)(2,1)S(1)}, u32[]{:S(2)}, u32[]{:S(2)}) collective-permute-start(bf16[6,2944]{1,0:T(8,128)(2,1)S(1)} %pad_maximum_fusion.3), channel_id=1, source_target_pairs={{64,0},{80,16},{96,32},{112,48},{0,64},{16,80},{32,96},{48,112},{6... | collective-permute-start | bytes 105992 | tf_op jit(solution)/shard_map/ppermute | solution.py:365
  67.9 1.3 collective-permute-start
  69.3 1.3 collective-permute-done.1
  70.6 1.4 collective-permute-done
  73.2 0.5 convolution_convert_fusion.1
  73.8 19.8 %all_to_all.25 = bf16[16,16,2816]{2,1,0:T(8,128)(2,1)S(1)} all-to-all(bf16[16,16,2816]{2,1,0:T(8,128)(2,1)S(1)} %bitcast.41), channel_id=1, replica_groups=mesh['attn'=8,'ffn'=16] {'ffn'}, dimensions={0} | all-to-all | bytes 2883584 | tf_op jit(solution)/shard_map/all_to_all | solution.py:437
  93.5 0.7 pad_add_fusion.place
  94.3 2.6 %collective-permute-done.3.other = bf16[256,2816]{1,0:T(8,128)(2,1)} collective-permute-done((bf16[256,2816]{1,0:T(8,128)(2,1)S(1)}, bf16[256,2816]{1,0:T(8,128)(2,1)}, u32[]{:S(2)}, u32[]{:S(2)}) %collective-permute-start.3) | collective-permute-done | bytes 1441824 | tf_op jit(solution)/shard_map/ppermute | solution.py:439
  96.9 12.0 %shard_map.137 = (bf16[512,4352]{1,0:T(8,128)(2,1)}, bf16[256,2816]{1,0:T(8,128)(2,1)}, bf16[256,2816]{1,0:T(8,128)(2,1)}) custom-call(s32[2]{0:T(128)} %pad_add_fusion.place, bf16[512,4352]{1,0:T(8,128)(2,1)} %all-gather.2.cloned.1.call-done.rows, bf16[256,2816]{1,0:T(8,128)(2,1)} %bitcast.46, bf16[256,2816]{1,0:T(8,128)(2,1)} %collective-permute-done.3.other, ...), custom_call_target="tpu_custom_call" | custom-call | flops 5637144576 | bytes 19922944 | tf_op jit(solution)/shard_map/pallas_call | solution.py:301
  109.1 3.3 %collective-permute-done.4 = bf16[256,2816]{1,0:T(8,128)(2,1)S(1)} collective-permute-done((bf16[256,2816]{1,0:T(8,128)(2,1)}, bf16[256,2816]{1,0:T(8,128)(2,1)S(1)}, u32[]{:S(2)}, u32[]{:S(2)}) %collective-permute-start.4) | collective-permute-done | bytes 1441824 | tf_op jit(solution)/shard_map/ppermute | solution.py:457
  112.4 1.5 add_convert_fusion
  113.9 4.7 %all-to-all-start.4 = ((bf16[16,16,2816]{2,1,0:T(8,128)(2,1)}), bf16[16,16,2816]{2,1,0:T(8,128)(2,1)S(1)}, u32[]{:S(2)}, u32[]{:S(2)}) async-start(bf16[16,16,2816]{2,1,0:T(8,128)(2,1)} %bitcast.20), calls=%async_computation.5 | async-start | bytes 2883584 | tf_op jit(solution)/shard_map/all_to_all | solution.py:460
  118.7 0.3 mul.93
  118.9 22.7 %all-to-all-done.4 = bf16[16,16,2816]{2,1,0:T(8,128)(2,1)S(1)} async-done(((bf16[16,16,2816]{2,1,0:T(8,128)(2,1)}), bf16[16,16,2816]{2,1,0:T(8,128)(2,1)S(1)}, u32[]{:S(2)}, u32[]{:S(2)}) %all-to-all-start.4) | async-done | bytes 1441824 | tf_op jit(solution)/shard_map/all_to_all | solution.py:460
  141.6 0.7 convolution_convert_fusion.2
  142.4 0.5 collective-permute-start.7
  142.9 2.8 %collective-permute-start.6 = (bf16[6,2816]{1,0:T(8,128)(2,1)S(1)}, bf16[6,2816]{1,0:T(8,128)(2,1)S(1)}, u32[]{:S(2)}, u32[]{:S(2)}) collective-permute-start(bf16[6,2816]{1,0:T(8,128)(2,1)S(1)} %get-tuple-element.19), channel_id=1, source_target_pairs={{64,0},{80,16},{96,32},{112,48},{0,64},{16,80},{32,96},{48,112},{6... | collective-permute-start | bytes 101384 | tf_op jit(solution)/shard_map/ppermute | solution.py:365
  145.6 1.1 collective-permute-start.5
  147.0 2.0 %reshape.123 = bf16[16,4,4352]{2,1,0:T(4,128)(2,1)} reshape(bf16[64,4352]{1,0:T(8,128)(2,1)} %reduce-scatter.2.cloned.1.call-done) | data formatting | bytes 1114112 | tf_op jit(solution)/shard_map/reshape | solution.py:473
  149.0 7.3 %all-to-all-start.3 = ((bf16[16,4,4352]{2,1,0:T(4,128)(2,1)}), bf16[16,4,4352]{2,1,0:T(4,128)(2,1)S(1)}, u32[]{:S(2)}, u32[]{:S(2)}) async-start(bf16[16,4,4352]{2,1,0:T(4,128)(2,1)} %reshape.123), calls=%async_computation.4 | async-start | bytes 1114112 | tf_op jit(solution)/shard_map/all_to_all | solution.py:472
  156.3 10.2 %all-to-all-done.3 = bf16[16,4,4352]{2,1,0:T(4,128)(2,1)S(1)} async-done(((bf16[16,4,4352]{2,1,0:T(4,128)(2,1)}), bf16[16,4,4352]{2,1,0:T(4,128)(2,1)S(1)}, u32[]{:S(2)}, u32[]{:S(2)}) %all-to-all-start.3) | async-done | bytes 557088 | tf_op jit(solution)/shard_map/all_to_all | solution.py:472
  166.5 0.4 convolution_bitcast_fusion
  167.0 0.7 fusion.1
  (62 shorter events, 3.0 us)
Async XLA Ops:
  17.0 8.1 %copy-start.3 = (bf16[7168]{0:T(1024)(128)(2,1)S(1)}, bf16[7168]{0:T(1024)(128)(2,1)}, u32[]{:S(2)}) copy-start(bf16[7168]{0:T(1024)(128)(2,1)} %param.22) | copy-start | bytes 43012
  17.0 8.2 %copy-start.4 = (s32[6,8]{1,0:T(8,128)S(1)}, s32[6,8]{1,0:T(8,128)}, u32[]{:S(2)}) copy-start(s32[6,8]{1,0:T(8,128)} %param.23) | copy-start | bytes 580
  17.0 8.2 %copy-start.5 = (f32[6,8]{1,0:T(8,128)S(1)}, f32[6,8]{1,0:T(8,128)}, u32[]{:S(2)}) copy-start(f32[6,8]{1,0:T(8,128)} %param.24) | copy-start | bytes 580
  17.0 29.6 %all-to-all-start = ((bf16[16,24,1792]{2,1,0:T(8,128)(2,1)}), bf16[16,24,1792]{2,1,0:T(8,128)(2,1)S(1)}, u32[]{:S(2)}, u32[]{:S(2)}) async-start(bf16[16,24,1792]{2,1,0:T(8,128)(2,1)} %shard_map.136), calls=%async_computation | async-start | bytes 2752512 | tf_op jit(solution)/shard_map/all_to_all | solution.py:410
  25.2 21.7 %copy-start.2 = (bf16[6,7168]{1,0:T(8,128)(2,1)S(1)}, bf16[6,7168]{1,0:T(8,128)(2,1)}, u32[]{:S(2)}) copy-start(bf16[6,7168]{1,0:T(8,128)(2,1)} %param.21) | copy-start | bytes 258052
  48.5 13.8 %all-to-all-start.1 = ((bf16[16,4,4352]{2,1,0:T(4,128)(2,1)}), bf16[16,4,4352]{2,1,0:T(4,128)(2,1)S(1)}, u32[]{:S(2)}, u32[]{:S(2)}) async-start(bf16[16,4,4352]{2,1,0:T(4,128)(2,1)} %reshape.118), calls=%async_computation.1 | async-start | bytes 1114112 | tf_op jit(solution)/shard_map/all_to_all | solution.py:423
  52.1 44.8 %all-gather.2.cloned.1.call-start = ((), (), s32[]{:S(2)}) async-start(), calls=%async_computation.6 | async-start | bytes 5013504 | tf_op jit(solution)/shard_map/all_gather | solution.py:435
  63.3 83.6 %reduce-scatter.2.cloned.1.call-start = ((), (), s32[]{:S(2)}) async-start(), calls=%async_computation.7 | async-start | bytes 5013504 | tf_op jit(solution)/shard_map/reduce_scatter | solution.py:454
  63.4 5.9 %collective-permute-start.2 = (bf16[6,2944]{1,0:T(8,128)(2,1)S(1)}, bf16[6,2944]{1,0:T(8,128)(2,1)S(1)}, u32[]{:S(2)}, u32[]{:S(2)}) collective-permute-start(bf16[6,2944]{1,0:T(8,128)(2,1)S(1)} %pad_maximum_fusion.3), channel_id=1, source_target_pairs={{96,0},{112,16},{0,32},{16,48},{32,64},{48,80},{64,96},{80,112},{9... | collective-permute-start | bytes 105992 | tf_op jit(solution)/shard_map/ppermute | solution.py:365
  65.0 5.6 %collective-permute-start.1 = (bf16[6,2944]{1,0:T(8,128)(2,1)S(1)}, bf16[6,2944]{1,0:T(8,128)(2,1)S(1)}, u32[]{:S(2)}, u32[]{:S(2)}) collective-permute-start(bf16[6,2944]{1,0:T(8,128)(2,1)S(1)} %pad_maximum_fusion.3), channel_id=1, source_target_pairs={{64,0},{80,16},{96,32},{112,48},{0,64},{16,80},{32,96},{48,112},{6... | collective-permute-start | bytes 105992 | tf_op jit(solution)/shard_map/ppermute | solution.py:365
  67.9 4.1 %collective-permute-start = (bf16[6,2944]{1,0:T(8,128)(2,1)S(1)}, bf16[6,2944]{1,0:T(8,128)(2,1)S(1)}, u32[]{:S(2)}, u32[]{:S(2)}) collective-permute-start(bf16[6,2944]{1,0:T(8,128)(2,1)S(1)} %pad_maximum_fusion.3), channel_id=1, source_target_pairs={{32,0},{48,16},{64,32},{80,48},{96,64},{112,80},{0,96},{16,112},{3... | collective-permute-start | bytes 105992 | tf_op jit(solution)/shard_map/ppermute | solution.py:365
  93.5 3.4 %copy-start = (bf16[16,16,2816]{2,1,0:T(8,128)(2,1)}, bf16[16,16,2816]{2,1,0:T(8,128)(2,1)S(1)}, u32[]{:S(2)}) copy-start(bf16[16,16,2816]{2,1,0:T(8,128)(2,1)S(1)} %all_to_all.25) | copy-start | bytes 4325380
  93.5 3.4 %collective-permute-start.3 = (bf16[256,2816]{1,0:T(8,128)(2,1)S(1)}, bf16[256,2816]{1,0:T(8,128)(2,1)}, u32[]{:S(2)}, u32[]{:S(2)}) collective-permute-start(bf16[256,2816]{1,0:T(8,128)(2,1)S(1)} %bitcast.45), channel_id=1, source_target_pairs={{0,16},{16,0},{32,48},{48,32},{64,80},{80,64},{96,112},{112,96},{1... | collective-permute-start | bytes 4325384 | tf_op jit(solution)/shard_map/ppermute | solution.py:439
  108.9 3.5 %copy-start.1 = (bf16[256,2816]{1,0:T(8,128)(2,1)S(1)}, bf16[256,2816]{1,0:T(8,128)(2,1)}, u32[]{:S(2)}) copy-start(bf16[256,2816]{1,0:T(8,128)(2,1)} %get-tuple-element.13) | copy-start | bytes 4325380
  108.9 3.5 %collective-permute-start.4 = (bf16[256,2816]{1,0:T(8,128)(2,1)}, bf16[256,2816]{1,0:T(8,128)(2,1)S(1)}, u32[]{:S(2)}, u32[]{:S(2)}) collective-permute-start(bf16[256,2816]{1,0:T(8,128)(2,1)} %get-tuple-element.14), channel_id=1, source_target_pairs={{0,16},{16,0},{32,48},{48,32},{64,80},{80,64},{96,112},{112,96},{1... | collective-permute-start | bytes 4325384 | tf_op jit(solution)/shard_map/ppermute | solution.py:457
  113.9 27.7 %all-to-all-start.4 = ((bf16[16,16,2816]{2,1,0:T(8,128)(2,1)}), bf16[16,16,2816]{2,1,0:T(8,128)(2,1)S(1)}, u32[]{:S(2)}, u32[]{:S(2)}) async-start(bf16[16,16,2816]{2,1,0:T(8,128)(2,1)} %bitcast.20), calls=%async_computation.5 | async-start | bytes 2883584 | tf_op jit(solution)/shard_map/all_to_all | solution.py:460
  142.4 13.9 %collective-permute-start.7 = (bf16[6,2816]{1,0:T(8,128)(2,1)S(1)}, bf16[6,2816]{1,0:T(8,128)(2,1)S(1)}, u32[]{:S(2)}, u32[]{:S(2)}) collective-permute-start(bf16[6,2816]{1,0:T(8,128)(2,1)S(1)} %get-tuple-element.18), channel_id=1, source_target_pairs={{96,0},{112,16},{0,32},{16,48},{32,64},{48,80},{64,96},{80,112},{9... | collective-permute-start | bytes 101384 | tf_op jit(solution)/shard_map/ppermute | solution.py:365
  142.9 13.4 %collective-permute-start.6 = (bf16[6,2816]{1,0:T(8,128)(2,1)S(1)}, bf16[6,2816]{1,0:T(8,128)(2,1)S(1)}, u32[]{:S(2)}, u32[]{:S(2)}) collective-permute-start(bf16[6,2816]{1,0:T(8,128)(2,1)S(1)} %get-tuple-element.19), channel_id=1, source_target_pairs={{64,0},{80,16},{96,32},{112,48},{0,64},{16,80},{32,96},{48,112},{6... | collective-permute-start | bytes 101384 | tf_op jit(solution)/shard_map/ppermute | solution.py:365
  145.6 10.7 %collective-permute-start.5 = (bf16[6,2816]{1,0:T(8,128)(2,1)S(1)}, bf16[6,2816]{1,0:T(8,128)(2,1)S(1)}, u32[]{:S(2)}, u32[]{:S(2)}) collective-permute-start(bf16[6,2816]{1,0:T(8,128)(2,1)S(1)} %get-tuple-element.17), channel_id=1, source_target_pairs={{32,0},{48,16},{64,32},{80,48},{96,64},{112,80},{0,96},{16,112},{3... | collective-permute-start | bytes 101384 | tf_op jit(solution)/shard_map/ppermute | solution.py:365
  149.0 17.6 %all-to-all-start.3 = ((bf16[16,4,4352]{2,1,0:T(4,128)(2,1)}), bf16[16,4,4352]{2,1,0:T(4,128)(2,1)S(1)}, u32[]{:S(2)}, u32[]{:S(2)}) async-start(bf16[16,4,4352]{2,1,0:T(4,128)(2,1)} %reshape.123), calls=%async_computation.4 | async-start | bytes 1114112 | tf_op jit(solution)/shard_map/all_to_all | solution.py:472
Sparse Core Ops, SparseCore 0:
  63.4 31.2 all-gather.1
  109.0 37.4 reduce-scatter.1

commit v4 on v3

--- a/solution.py
+++ b/solution.py
@@ -9,8 +9,8 @@
 
 PARTS = 4
 UNIT = 512
-IN_RING = 4352
-OUT_RING = 4352
+IN_RING = 3584
+OUT_RING = 4096
 F32 = jnp.float32
 BF16 = jnp.bfloat16
 
@@ -170,72 +170,56 @@
 
 OWNED = 4
 INNER = 2
-SLAB = 1024
-
-
-def expert_kernel(
-    place,
-    rows,
-    mine,
-    other,
-    gate_proj,
-    up_proj,
-    down_proj,
-    out,
-    theirs,
-    ours,
-    x,
-    x_rest,
-    gate_w,
-    up_w,
-    down_w,
-    gate_rest,
-    up_rest,
-    gate,
-    up,
-    spread,
-    slab,
-    share,
-    got,
-    sent,
-):
+
+
+def expert_kernel(planes, cores, place, *refs):
+    blocks = refs[: planes * cores]
+    mine, other, gate_proj, up_proj, down_proj, *refs = refs[planes * cores :]
+    outs, refs = refs[: planes * cores + cores], refs[planes * cores + cores :]
+    x, x_rest, gate_w, up_w, down_w, *refs = refs
+    gate_rest, up_rest, gate, up, spread, share_ring, share_rest = refs[:-3]
+    row_sem, weight_sem, sent = refs[-3:]
     core, plane = place[0], place[1]
     depth, rest = x.shape[1], x_rest.shape[1]
     count = mine.shape[0]
-    hidden_count = gate_w.shape[1]
-    planes, cores, block = gate.shape[:3]
+    block = gate.shape[2]
     own = block // OWNED
     tile = depth // INNER
-    size = out.shape[1]
-    left = down_w.shape[1] - size
-    ring_w = [(at * tile, tile) for at in range(INNER)] + [(depth, rest)]
+    size = share_ring.shape[2]
 
     def fetch(source, target, sem):
         copy = pltpu.make_async_copy(source, target, sem)
         copy.start()
         return copy
 
-    def fetch_weights(at):
-        start, length = ring_w[at]
+    def fetch_weights(at, start, length):
         rows_at = pl.ds(start, length)
         return [
-            fetch(gate_proj.at[0, rows_at], gate_w.at[rows_at], got.at[4 * at]),
-            fetch(up_proj.at[0, rows_at], up_w.at[rows_at], got.at[4 * at + 1]),
+            fetch(gate_proj.at[0, rows_at], gate_w.at[rows_at], weight_sem.at[2 * at]),
+            fetch(up_proj.at[0, rows_at], up_w.at[rows_at], weight_sem.at[2 * at + 1]),
         ]
 
-    waits = {}
-    waits[INNER] = fetch_weights(INNER) + [
-        fetch(mine, x_rest.at[pl.ds(0, count)], got.at[4 * INNER + 2]),
-        fetch(other, x_rest.at[pl.ds(count, count)], got.at[4 * INNER + 3]),
+    def row_of(at):
+        turn, c = at // cores, at % cores
+        c = core if c == 0 else 1 - core
+        return (plane + turn) % planes, c
+
+    rest_waits = fetch_weights(INNER, depth, rest) + [
+        fetch(mine, x_rest.at[pl.ds(0, count)], row_sem.at[INNER, 0]),
+        fetch(other, x_rest.at[pl.ds(count, count)], row_sem.at[INNER, 1]),
     ]
+    waits = []
     for at in range(INNER):
         columns = pl.ds(at * tile, tile)
-        waits[at] = fetch_weights(at) + [
-            fetch(rows.at[:, columns], x.at[:, columns], got.at[4 * at + 2])
-        ]
-    down_wait = fetch(down_proj.at[0], down_w, got.at[4 * INNER + 4])
-
-    for copy in waits[INNER]:
+        copies = fetch_weights(at, at * tile, tile)
+        for i, ref in enumerate(blocks):
+            y, c = row_of(i)
+            target = x.at[pl.ds(pl.multiple_of((y * cores + c) * block, block), block), columns]
+            copies.append(fetch(ref.at[:, columns], target, row_sem.at[at, i]))
+        waits.append(copies)
+    down_wait = fetch(down_proj.at[0], down_w, weight_sem.at[2 * INNER + 2])
+
+    for copy in rest_waits:
         copy.wait()
     gate_rest[...] = dot(x_rest[...], gate_w[depth:])
     up_rest[...] = dot(x_rest[...], up_w[depth:])
@@ -253,60 +237,53 @@
         else:
             gate[...] += gate_part
             up[...] += up_part
-    for turn in range(planes):
-        y = (plane + turn) % planes
-        for at in range(cores):
-            c = core if at == 0 else 1 - core
-            for f in range(own):
-                source = slice(
-                    at * count + (f * planes + turn) * OWNED,
-                    at * count + (f * planes + turn + 1) * OWNED,
-                )
-                target = slice(f * OWNED, (f + 1) * OWNED)
-                gate[y, c, target] += gate_rest[source]
-                up[y, c, target] += up_rest[source]
+    for i in range(planes * cores):
+        y, c = row_of(i)
+        turn, at = i // cores, i % cores
+        for f in range(own):
+            start = at * count + (f * planes + turn) * OWNED
+            target = slice(f * OWNED, (f + 1) * OWNED)
+            gate[y, c, target] += gate_rest[start : start + OWNED]
+            up[y, c, target] += up_rest[start : start + OWNED]
     gated = gate[...]
-    hidden = gated * jax.nn.sigmoid(gated) * up[...]
-    gate[...] = hidden
-    hidden = hidden.reshape(rows.shape[0], hidden_count).astype(BF16)
-    for turn in range(planes):
-        y = (plane + turn) % planes
-        for at in range(cores):
-            c = core if at == 0 else 1 - core
-            for f in range(own):
-                target = slice((f * planes + turn) * OWNED, (f * planes + turn + 1) * OWNED)
-                spread[at, target] = gate[y, c, f * OWNED : (f + 1) * OWNED]
+    gate[...] = gated * jax.nn.sigmoid(gated) * up[...]
     down_wait.wait()
     sends = []
-    for at, ref in ((1, theirs), (0, ours)):
-        share[at] = dot(spread[at].astype(BF16), down_w[:, size:]).astype(BF16)
-        sends.append(fetch(share.at[at], ref, sent.at[at]))
-    for at in range(0, size, SLAB):
-        length = min(SLAB, size - at)
-        slab[:, at : at + length] = dot(hidden, down_w[:, at : at + length]).astype(BF16)
-        columns = pl.ds(at, length)
-        sends.append(fetch(slab.at[:, columns], out.at[:, columns], sent.at[cores + at // SLAB]))
+    for at in range(cores - 1, -1, -1):
+        pieces = []
+        for turn in range(planes):
+            y, c = row_of(turn * cores + at)
+            pieces.append(gate[y, c])
+            for f in range(own):
+                start = (f * planes + turn) * OWNED
+                spread[at, start : start + OWNED] = gate[y, c, f * OWNED : (f + 1) * OWNED]
+        ring = jnp.concatenate(pieces, axis=0).astype(BF16)
+        share_ring[at] = dot(ring, down_w[:, :size]).astype(BF16)
+        for turn in range(planes):
+            i = at * planes + turn
+            piece = share_ring.at[at, pl.ds(turn * block, block)]
+            sends.append(fetch(piece, outs[i], sent.at[i]))
+    for at in range(cores - 1, -1, -1):
+        share_rest[at] = dot(spread[at].astype(BF16), down_w[:, size:]).astype(BF16)
+        sends.append(fetch(share_rest.at[at], outs[planes * cores + at], sent.at[planes * cores + at]))
     for copy in sends:
         copy.wait()
 
 
-def expert(place, rows, mine, other, gate_proj, up_proj, down_proj, size, planes, cores, capacity):
-    count, depth = rows.shape
+def expert(place, blocks, mine, other, gate_proj, up_proj, down_proj, size, planes, cores):
+    block, depth = blocks[0].shape
+    count = planes * cores * block
     part, rest = mine.shape
     hidden = gate_proj.shape[2]
     width = down_proj.shape[2]
-    block = count // (planes * cores)
     wide = (planes, cores, block, hidden)
     anywhere = pl.BlockSpec(memory_space=pl.ANY)
     return pl.pallas_call(
-        expert_kernel,
-        out_shape=(
-            jax.ShapeDtypeStruct((count, size), BF16),
-            jax.ShapeDtypeStruct((part, width - size), BF16),
-            jax.ShapeDtypeStruct((part, width - size), BF16),
-        ),
-        in_specs=[pl.BlockSpec(memory_space=pltpu.SMEM)] + [anywhere] * 6,
-        out_specs=[anywhere] * 3,
+        lambda *refs: expert_kernel(planes, cores, *refs),
+        out_shape=[jax.ShapeDtypeStruct((block, size), BF16)] * (planes * cores)
+        + [jax.ShapeDtypeStruct((part, width - size), BF16)] * cores,
+        in_specs=[pl.BlockSpec(memory_space=pltpu.SMEM)] + [anywhere] * (len(blocks) + 5),
+        out_specs=[anywhere] * (planes * cores + cores),
         scratch_shapes=[
             pltpu.VMEM((count, depth), BF16),
             pltpu.VMEM((2 * part, rest), BF16),
@@ -318,18 +295,19 @@
             pltpu.VMEM(wide, F32),
             pltpu.VMEM(wide, F32),
             pltpu.VMEM((cores, part, hidden), F32),
-            pltpu.VMEM((count, size), BF16),
+            pltpu.VMEM((cores, part, size), BF16),
             pltpu.VMEM((cores, part, width - size), BF16),
-            pltpu.SemaphoreType.DMA((4 * INNER + 5,)),
-            pltpu.SemaphoreType.DMA((cores + pl.cdiv(size, SLAB),)),
+            pltpu.SemaphoreType.DMA((INNER + 1, len(blocks))),
+            pltpu.SemaphoreType.DMA((2 * INNER + 3,)),
+            pltpu.SemaphoreType.DMA((planes * cores + cores,)),
         ],
         compiler_params=pltpu.CompilerParams(vmem_limit_bytes=60 << 20),
         cost_estimate=pl.CostEstimate(
             flops=6 * count * width * hidden,
-            bytes_accessed=2 * count * (depth + size) + 6 * width * hidden,
+            bytes_accessed=4 * count * width + 6 * width * hidden,
             transcendentals=count * hidden,
         ),
-    )(place, rows, mine, other, gate_proj, up_proj, down_proj)
+    )(place, *blocks, mine, other, gate_proj, up_proj, down_proj)
 
 
 def local(
@@ -424,7 +402,7 @@
     arrived = arrived.reshape(owners * capacity, IN_RING)
 
     rest = width - IN_RING
-    near, arrived = lax.optimization_barrier((near, arrived))
+    by_plane = [arrived] + [from_plane(arrived, ahead) for ahead in range(1, planes)]
     near = along_planes(near)
     tables = near[:, :, rest:].astype(F32)
     tables = [tables[:, :, at * owners : (at + 1) * owners] for at in range(4)]
@@ -432,15 +410,16 @@
     placed_all = block_diagonal(placed_all).astype(BF16)
     weighting_all = block_diagonal(weighting_all)
     near = near[:, :, :rest].reshape(planes * row_count, rest)
-    ring_rows = lax.all_gather(arrived, "attn", axis=0, tiled=True)
     outgoing = dot(placed_all, near).astype(BF16).reshape(owners, planes * capacity, rest)
     mine = lax.all_to_all(outgoing, "ffn", split_axis=0, concat_axis=0, tiled=True)
+    *_, mine = lax.optimization_barrier((*by_plane, mine))
+    blocks = [v for held in by_plane for v in (held, lax.ppermute(held, "attn", swap))]
     mine = mine.reshape(owners * planes * capacity, rest)
     other = lax.ppermute(mine, "attn", swap)
 
-    partial_value, theirs, ours = expert(
+    *pieces, ours, theirs = expert(
         jnp.stack([core, plane]),
-        ring_rows,
+        blocks,
         mine,
         other,
         gate_proj,
@@ -449,13 +428,21 @@
         OUT_RING,
         planes,
         cores,
-        capacity,
-    )
-    summed = lax.psum_scatter(partial_value, "attn", scatter_dimension=0, tiled=True)
+    )
+
+    def add(a, b):
+        return (a.astype(F32) + b.astype(F32)).astype(BF16)
+
+    ring = {}
+    for turn in (2, 1, 3, 0):
+        ring[turn] = add(pieces[turn], lax.ppermute(pieces[planes + turn], "attn", swap))
+    summed = ring[0].astype(F32)
+    for ahead in range(1, planes):
+        summed = summed + from_plane(ring[planes - ahead], ahead).astype(F32)
+    summed = summed.astype(BF16)
 
     rest = width - OUT_RING
-    theirs = lax.ppermute(theirs, "attn", swap)
-    ours = (ours.astype(F32) + theirs.astype(F32)).astype(BF16)
+    ours = add(ours, lax.ppermute(theirs, "attn", swap))
     ours = ours.reshape(owners, planes * capacity, rest)
     ours = lax.all_to_all(ours, "ffn", split_axis=0, concat_axis=0, tiled=True)
     ours = jnp.einsum(

time: 175 us -> 165 us (0.943)
  blocking collectives: 19.8 us -> 0 us
  between operations: 13.7 us -> 0.48 us
  waiting for transfers between devices: 72.5 us -> 81.9 us
  starting transfers between devices: 34.3 us -> 42 us
  other arithmetic: 4.41 us -> 9.61 us
  local copies, waits for them, and re-layouts: 5.32 us -> 3.47 us
    ppermute x6 -> x12, waiting for transfers between devices: 2.72 us -> 31.6 us  [from_plane(): return lax.ppermute(v, 'attn', pairs)]
    all_to_all x1 -> x0, blocking collectives: 19.8 us -> none  [local(): lax.all_to_all(outgoing, 'ffn', split_axis=0, concat_axis=0, tiled=True)]
    all_to_all x1, waiting for transfers between devices: 22.7 us -> 5.75 us  [local(): ours = lax.all_to_all(ours, 'ffn', split_axis=0, concat_axis=0, tiled=True)]
    ppermute x6 -> x12, starting transfers between devices: 10.3 us -> 16.1 us  [from_plane(): return lax.ppermute(v, 'attn', pairs)]
    convert_element_type x1 -> x5, other arithmetic: 1.5 us -> 6.83 us  [the longest x4 4.83 us: add(): return (a.astype(F32) + b.astype(F32)).astype(BF16)]
    all_to_all x1 -> x2, starting transfers between devices: 3.58 us -> 8.01 us  [local(): lax.all_to_all(outgoing, 'ffn', split_axis=0, concat_axis=0, tiled=True)]
    ppermute x1 -> x9, waiting for transfers between devices: 3.3 us -> 7.7 us  [the longest x4 4.9 us: local(): lax.ppermute(held, 'attn', swap)]
    all_to_all x1, waiting for transfers between devices: 10.2 us -> 5.97 us  [local(): lax.all_to_all(summed.reshape(owners, capacity, OUT_RING), 'ffn', split_a...]
  transfers between devices with their start and end apart: 14 -> 27, of which waited for: 8 -> 17; matrix products, arithmetic and copies ran while one was open for 4% -> 9% of each run, Pallas kernels for 0% -> 0%
where the time goes in v4:
time: 165 us
  waiting for transfers between devices  81.9 us (50%)
  starting transfers between devices  42 us (25%)
  Pallas kernels  23.5 us (14%)
  other arithmetic  9.61 us (6%)
  matrix products  3.49 us (2%)
  local copies, waits for them, and re-layouts  3.47 us (2%)
    ppermute x12, waiting for transfers between devices, from_plane(): return lax.ppermute(v, 'attn', pairs)  31.6 us
    all_to_all x1, waiting for transfers between devices, local(): lax.all_to_all(pieces, 'ffn', split_axis=0, concat_axis=0, tiled=True)  20.8 us
    ppermute x12, starting transfers between devices, from_plane(): return lax.ppermute(v, 'attn', pairs)  16.1 us
    pallas_call x1, Pallas kernels, expert(): pl.pallas_call(lambda *refs: expert_kernel(planes, cores, *refs), out_sha...  13.1 us
    pallas_call x1, Pallas kernels, attend(): pl.pallas_call(lambda *refs: attend_kernel(scale, owners, parts, *refs),...  10.5 us
    all_to_all x2, waiting for transfers between devices, local(): lax.all_to_all(outgoing, 'ffn', split_axis=0, concat_axis=0, tiled=True)  9.89 us
    all_to_all x1, starting transfers between devices, local(): lax.all_to_all(pieces, 'ffn', split_axis=0, concat_axis=0, tiled=True)  8.1 us
    all_to_all x2, starting transfers between devices, local(): lax.all_to_all(outgoing, 'ffn', split_axis=0, concat_axis=0, tiled=True)  8.01 us
  transfers between devices with their start and end apart: 27, of which 17 were waited for; matrix products, arithmetic and copies ran while one was open for 9% of the time, Pallas kernels for 0%

profile of v4, /device:TPU:0, one launch (start us, length us, event | category | flops | bytes accessed | tf_op | source)
XLA Modules:
  0.0 164.5 jit_solution(6932171945828486108)
XLA Ops:
  0.0 10.5 %shard_map.136 = bf16[16,24,1792]{2,1,0:T(8,128)(2,1)} custom-call(s32[96]{0:T(128)} %refs_0_.1, bf16[96,4,512]{2,1,0:T(4,128)(2,1)} %refs_1_.1, bf16[96,64,512]{2,1,0:T(8,128)(2,1)} %refs_2_.1, bf16[4,64,96]{2,1,0:T(8,128)(2,1)} %bitcast.53, bf16[64,64,96]{2,1,0:T(8,128)(2,1)} %bitcast.45, bf16[4,512,128]{2,1,0:T(8,128)(2,1)} %refs_5_.1, ...), custom_call_target="tpu_custom_call" | custom-call | flops 905969664 | bytes 13631488 | tf_op jit(solution)/shard_map/pallas_call | solution.py:139
  10.5 8.1 %all-to-all-start = ((bf16[16,24,1792]{2,1,0:T(8,128)(2,1)}), bf16[16,24,1792]{2,1,0:T(8,128)(2,1)S(1)}, u32[]{:S(2)}, u32[]{:S(2)}) async-start(bf16[16,24,1792]{2,1,0:T(8,128)(2,1)} %shard_map.136), calls=%async_computation | async-start | bytes 2752512 | tf_op jit(solution)/shard_map/all_to_all | solution.py:388
  19.4 20.8 %all-to-all-done = bf16[16,24,1792]{2,1,0:T(8,128)(2,1)S(1)} async-done(((bf16[16,24,1792]{2,1,0:T(8,128)(2,1)}), bf16[16,24,1792]{2,1,0:T(8,128)(2,1)S(1)}, u32[]{:S(2)}, u32[]{:S(2)}) %all-to-all-start) | async-done | bytes 1376288 | tf_op jit(solution)/shard_map/all_to_all | solution.py:388
  40.7 1.6 %collective-permute-start.9 = (bf16[6,3712]{1,0:T(8,128)(2,1)S(1)}, bf16[6,3712]{1,0:T(8,128)(2,1)S(1)}, u32[]{:S(2)}, u32[]{:S(2)}) collective-permute-start(bf16[6,3712]{1,0:T(8,128)(2,1)S(1)} %get-tuple-element.33), channel_id=1, source_target_pairs={{96,0},{112,16},{0,32},{16,48},{32,64},{48,80},{64,96},{80,112},{9... | collective-permute-start | bytes 133640 | tf_op jit(solution)/shard_map/ppermute | solution.py:343
  42.4 2.9 %collective-permute-start.8 = (bf16[6,3712]{1,0:T(8,128)(2,1)S(1)}, bf16[6,3712]{1,0:T(8,128)(2,1)S(1)}, u32[]{:S(2)}, u32[]{:S(2)}) collective-permute-start(bf16[6,3712]{1,0:T(8,128)(2,1)S(1)} %get-tuple-element.33), channel_id=1, source_target_pairs={{64,0},{80,16},{96,32},{112,48},{0,64},{16,80},{32,96},{48,112},{6... | collective-permute-start | bytes 133640 | tf_op jit(solution)/shard_map/ppermute | solution.py:343
  45.3 1.3 collective-permute-start.7
  47.8 3.6 %all-to-all-start.1 = ((bf16[16,4,3584]{2,1,0:T(4,128)(2,1)}), bf16[16,4,3584]{2,1,0:T(4,128)(2,1)S(1)}, u32[]{:S(2)}, u32[]{:S(2)}) async-start(bf16[16,4,3584]{2,1,0:T(4,128)(2,1)} %reshape.118), calls=%async_computation.1 | async-start | bytes 917504 | tf_op jit(solution)/shard_map/all_to_all | solution.py:401
  52.7 1.8 %convolution_convert_fusion = bf16[256,3584]{1,0:T(8,128)(2,1)} fusion(bf16[256,24]{1,0:T(8,128)(2,1)S(1)} %convert_element_type.171, bf16[24,3584]{1,0:T(8,128)(2,1)S(1)} %reshape.120), kind=kOutput, calls=%fused_computation | convolution fusion | flops 44957696 | bytes 2019328 | tf_op jit(solution)/shard_map/dot_general | solution.py:19
  54.6 6.6 %all-to-all-done.1 = bf16[16,4,3584]{2,1,0:T(4,128)(2,1)S(1)} async-done(((bf16[16,4,3584]{2,1,0:T(4,128)(2,1)}), bf16[16,4,3584]{2,1,0:T(4,128)(2,1)S(1)}, u32[]{:S(2)}, u32[]{:S(2)}) %all-to-all-start.1) | async-done | bytes 458784 | tf_op jit(solution)/shard_map/all_to_all | solution.py:401
  61.2 4.4 %all-to-all-start.2 = ((bf16[16,16,3584]{2,1,0:T(8,128)(2,1)}), bf16[16,16,3584]{2,1,0:T(8,128)(2,1)}, u32[]{:S(2)}, u32[]{:S(2)}) async-start(bf16[16,16,3584]{2,1,0:T(8,128)(2,1)} %bitcast.16), calls=%async_computation.2 | async-start | bytes 3670016 | tf_op jit(solution)/shard_map/all_to_all | solution.py:414
  65.8 2.7 %collective-permute-start.3 = (bf16[64,3584]{1,0:T(8,128)(2,1)S(1)}, bf16[64,3584]{1,0:T(8,128)(2,1)S(1)}, u32[]{:S(2)}, u32[]{:S(2)}) collective-permute-start(bf16[64,3584]{1,0:T(8,128)(2,1)S(1)} %reshape.119.refs_1_), channel_id=1, source_target_pairs={{64,0},{80,16},{96,32},{112,48},{0,64},{16,80},{32,96},{48,112},{6... | collective-permute-start | bytes 1376264 | tf_op jit(solution)/shard_map/ppermute | solution.py:343
  68.6 10.6 %collective-permute-done.1.refs_3_ = bf16[64,3584]{1,0:T(8,128)(2,1)S(1)} collective-permute-done((bf16[64,3584]{1,0:T(8,128)(2,1)S(1)}, bf16[64,3584]{1,0:T(8,128)(2,1)S(1)}, u32[]{:S(2)}, u32[]{:S(2)}) %collective-permute-start.1) | collective-permute-done | bytes 458784 | tf_op jit(solution)/shard_map/ppermute | solution.py:343
  79.1 1.6 collective-permute-done.3.refs_5_
  80.8 4.9 %collective-permute-done.5.refs_7_ = bf16[64,3584]{1,0:T(8,128)(2,1)S(1)} collective-permute-done((bf16[64,3584]{1,0:T(8,128)(2,1)S(1)}, bf16[64,3584]{1,0:T(8,128)(2,1)S(1)}, u32[]{:S(2)}, u32[]{:S(2)}) %collective-permute-start.5) | collective-permute-done | bytes 458784 | tf_op jit(solution)/shard_map/ppermute | solution.py:343
  85.6 3.3 %all-to-all-done.2 = bf16[16,16,3584]{2,1,0:T(8,128)(2,1)} async-done(((bf16[16,16,3584]{2,1,0:T(8,128)(2,1)}), bf16[16,16,3584]{2,1,0:T(8,128)(2,1)}, u32[]{:S(2)}, u32[]{:S(2)}) %all-to-all-start.2) | async-done | bytes 1835040 | tf_op jit(solution)/shard_map/all_to_all | solution.py:414
  90.6 3.1 %collective-permute-done.refs_2_ = bf16[64,3584]{1,0:T(8,128)(2,1)S(1)} collective-permute-done((bf16[64,3584]{1,0:T(8,128)(2,1)S(1)}, bf16[64,3584]{1,0:T(8,128)(2,1)S(1)}, u32[]{:S(2)}, u32[]{:S(2)}) %collective-permute-start) | collective-permute-done | bytes 458784 | tf_op jit(solution)/shard_map/ppermute | solution.py:416
  94.4 1.0 collective-permute-done.6.refs_8_
  95.7 13.1 %shard_map.137 = (bf16[64,4096]{1,0:T(8,128)(2,1)}, bf16[64,4096]{1,0:T(8,128)(2,1)}, bf16[64,4096]{1,0:T(8,128)(2,1)}, bf16[64,4096]{1,0:T(8,128)(2,1)}, bf16[6...) custom-call(s32[2]{0:T(128)} %pad_add_fusion.refs_0_, ...), custom_call_target="tpu_custom_call" | custom-call | flops 5637144576 | bytes 25690112 | tf_op jit(solution)/shard_map/pallas_call | solution.py:281
  111.0 1.2 add_convert_fusion.2
  112.9 1.8 %collective-permute-done.14 = bf16[64,4096]{1,0:T(8,128)(2,1)S(1)} collective-permute-done((bf16[64,4096]{1,0:T(8,128)(2,1)}, bf16[64,4096]{1,0:T(8,128)(2,1)S(1)}, u32[]{:S(2)}, u32[]{:S(2)}) %collective-permute-start.14) | collective-permute-done | bytes 524320 | tf_op jit(solution)/shard_map/ppermute | solution.py:438
  116.7 3.3 %collective-permute-start.13 = (bf16[64,4096]{1,0:T(8,128)(2,1)}, bf16[64,4096]{1,0:T(8,128)(2,1)}, u32[]{:S(2)}, u32[]{:S(2)}) collective-permute-start(bf16[64,4096]{1,0:T(8,128)(2,1)} %add_convert_fusion.4), channel_id=1, source_target_pairs={{32,0},{48,16},{64,32},{80,48},{96,64},{112,80},{0,96},{16,112},{3... | collective-permute-start | bytes 1572872 | tf_op jit(solution)/shard_map/ppermute | solution.py:343
  120.0 1.8 %add_convert_fusion = bf16[256,3072]{1,0:T(8,128)(2,1)} fusion(bf16[256,3072]{1,0:T(8,128)(2,1)S(1)} %collective-permute-done.18, bf16[256,3072]{1,0:T(8,128)(2,1)S(1)} %copy-done), kind=kLoop, calls=%fused_computation.4 | loop fusion | flops 3145728 | bytes 4718592 | tf_op jit(solution)/shard_map/convert_element_type | solution.py:434
  121.8 3.7 %all-to-all-start.4 = ((bf16[16,16,3072]{2,1,0:T(8,128)(2,1)}), bf16[16,16,3072]{2,1,0:T(8,128)(2,1)S(1)}, u32[]{:S(2)}, u32[]{:S(2)}) async-start(bf16[16,16,3072]{2,1,0:T(8,128)(2,1)} %bitcast.20), calls=%async_computation.4 | async-start | bytes 3145728 | tf_op jit(solution)/shard_map/all_to_all | solution.py:447
  126.0 12.8 %collective-permute-done.17 = bf16[64,4096]{1,0:T(8,128)(2,1)} collective-permute-done((bf16[64,4096]{1,0:T(8,128)(2,1)S(1)}, bf16[64,4096]{1,0:T(8,128)(2,1)}, u32[]{:S(2)}, u32[]{:S(2)}) %collective-permute-start.17) | collective-permute-done | bytes 524320 | tf_op jit(solution)/shard_map/ppermute | solution.py:343
  138.7 1.8 %collective-permute-done.13 = bf16[64,4096]{1,0:T(8,128)(2,1)} collective-permute-done((bf16[64,4096]{1,0:T(8,128)(2,1)}, bf16[64,4096]{1,0:T(8,128)(2,1)}, u32[]{:S(2)}, u32[]{:S(2)}) %collective-permute-start.13) | collective-permute-done | bytes 524320 | tf_op jit(solution)/shard_map/ppermute | solution.py:343
  140.5 2.0 %add_convert_fusion.1 = bf16[64,4096]{1,0:T(8,128)(2,1)S(1)} fusion(bf16[64,4096]{1,0:T(8,128)(2,1)} %collective-permute-done.17, bf16[64,4096]{1,0:T(8,128)(2,1)} %collective-permute-done.15, bf16[64,4096]{1,0:T(8,128)(2,1)} %collective-permute-done.13, bf16[64,4096]{1,0:T(8,128)(2,1)} %collective-permute-done.11, bf16[64,4096]{1,0:T(8,128)(2,1)} %get-tuple-element.17), kind=kLoop, calls=%fused_computation.6 | loop fusion | flops 3145728 | bytes 3145728 | tf_op jit(solution)/shard_map/convert_element_type | solution.py:442
  142.5 1.0 reshape.123
  143.5 5.8 %all-to-all-done.4 = bf16[16,16,3072]{2,1,0:T(8,128)(2,1)S(1)} async-done(((bf16[16,16,3072]{2,1,0:T(8,128)(2,1)}), bf16[16,16,3072]{2,1,0:T(8,128)(2,1)S(1)}, u32[]{:S(2)}, u32[]{:S(2)}) %all-to-all-start.4) | async-done | bytes 1572896 | tf_op jit(solution)/shard_map/all_to_all | solution.py:447
  149.2 3.8 %all-to-all-start.3 = ((bf16[16,4,4096]{2,1,0:T(4,128)(2,1)}), bf16[16,4,4096]{2,1,0:T(4,128)(2,1)S(1)}, u32[]{:S(2)}, u32[]{:S(2)}) async-start(bf16[16,4,4096]{2,1,0:T(4,128)(2,1)} %reshape.123), calls=%async_computation.3 | async-start | bytes 1048576 | tf_op jit(solution)/shard_map/all_to_all | solution.py:459
  154.0 2.2 %collective-permute-start.20 = (bf16[6,3072]{1,0:T(8,128)(2,1)S(1)}, bf16[6,3072]{1,0:T(8,128)(2,1)S(1)}, u32[]{:S(2)}, u32[]{:S(2)}) collective-permute-start(bf16[6,3072]{1,0:T(8,128)(2,1)S(1)} %get-tuple-element.31), channel_id=1, source_target_pairs={{64,0},{80,16},{96,32},{112,48},{0,64},{16,80},{32,96},{48,112},{6... | collective-permute-start | bytes 110600 | tf_op jit(solution)/shard_map/ppermute | solution.py:343
  156.2 1.0 collective-permute-start.19
  157.2 6.0 %all-to-all-done.3 = bf16[16,4,4096]{2,1,0:T(4,128)(2,1)S(1)} async-done(((bf16[16,4,4096]{2,1,0:T(4,128)(2,1)}), bf16[16,4,4096]{2,1,0:T(4,128)(2,1)S(1)}, u32[]{:S(2)}, u32[]{:S(2)}) %all-to-all-start.3) | async-done | bytes 524320 | tf_op jit(solution)/shard_map/all_to_all | solution.py:459
  (101 shorter events, 14.0 us)
Async XLA Ops:
  10.5 29.9 %copy-start.1 = (bf16[6,7168]{1,0:T(8,128)(2,1)S(1)}, bf16[6,7168]{1,0:T(8,128)(2,1)}, u32[]{:S(2)}) copy-start(bf16[6,7168]{1,0:T(8,128)(2,1)} %param.21) | copy-start | bytes 258052
  10.5 29.7 %all-to-all-start = ((bf16[16,24,1792]{2,1,0:T(8,128)(2,1)}), bf16[16,24,1792]{2,1,0:T(8,128)(2,1)S(1)}, u32[]{:S(2)}, u32[]{:S(2)}) async-start(bf16[16,24,1792]{2,1,0:T(8,128)(2,1)} %shard_map.136), calls=%async_computation | async-start | bytes 2752512 | tf_op jit(solution)/shard_map/all_to_all | solution.py:388
  40.7 10.7 %collective-permute-start.9 = (bf16[6,3712]{1,0:T(8,128)(2,1)S(1)}, bf16[6,3712]{1,0:T(8,128)(2,1)S(1)}, u32[]{:S(2)}, u32[]{:S(2)}) collective-permute-start(bf16[6,3712]{1,0:T(8,128)(2,1)S(1)} %get-tuple-element.33), channel_id=1, source_target_pairs={{96,0},{112,16},{0,32},{16,48},{32,64},{48,80},{64,96},{80,112},{9... | collective-permute-start | bytes 133640 | tf_op jit(solution)/shard_map/ppermute | solution.py:343
  42.4 9.1 %collective-permute-start.8 = (bf16[6,3712]{1,0:T(8,128)(2,1)S(1)}, bf16[6,3712]{1,0:T(8,128)(2,1)S(1)}, u32[]{:S(2)}, u32[]{:S(2)}) collective-permute-start(bf16[6,3712]{1,0:T(8,128)(2,1)S(1)} %get-tuple-element.33), channel_id=1, source_target_pairs={{64,0},{80,16},{96,32},{112,48},{0,64},{16,80},{32,96},{48,112},{6... | collective-permute-start | bytes 133640 | tf_op jit(solution)/shard_map/ppermute | solution.py:343
  45.3 6.2 %collective-permute-start.7 = (bf16[6,3712]{1,0:T(8,128)(2,1)S(1)}, bf16[6,3712]{1,0:T(8,128)(2,1)S(1)}, u32[]{:S(2)}, u32[]{:S(2)}) collective-permute-start(bf16[6,3712]{1,0:T(8,128)(2,1)S(1)} %get-tuple-element.33), channel_id=1, source_target_pairs={{32,0},{48,16},{64,32},{80,48},{96,64},{112,80},{0,96},{16,112},{3... | collective-permute-start | bytes 133640 | tf_op jit(solution)/shard_map/ppermute | solution.py:343
  47.8 13.3 %all-to-all-start.1 = ((bf16[16,4,3584]{2,1,0:T(4,128)(2,1)}), bf16[16,4,3584]{2,1,0:T(4,128)(2,1)S(1)}, u32[]{:S(2)}, u32[]{:S(2)}) async-start(bf16[16,4,3584]{2,1,0:T(4,128)(2,1)} %reshape.118), calls=%async_computation.1 | async-start | bytes 917504 | tf_op jit(solution)/shard_map/all_to_all | solution.py:401
  61.2 27.7 %all-to-all-start.2 = ((bf16[16,16,3584]{2,1,0:T(8,128)(2,1)}), bf16[16,16,3584]{2,1,0:T(8,128)(2,1)}, u32[]{:S(2)}, u32[]{:S(2)}) async-start(bf16[16,16,3584]{2,1,0:T(8,128)(2,1)} %bitcast.16), calls=%async_computation.2 | async-start | bytes 3670016 | tf_op jit(solution)/shard_map/all_to_all | solution.py:414
  65.7 29.9 %copy-start.4 = (bf16[64,3584]{1,0:T(8,128)(2,1)}, bf16[64,3584]{1,0:T(8,128)(2,1)S(1)}, u32[]{:S(2)}) copy-start(bf16[64,3584]{1,0:T(8,128)(2,1)S(1)} %reshape.119.refs_1_) | copy-start | bytes 1376260
  65.7 13.4 %collective-permute-start.1 = (bf16[64,3584]{1,0:T(8,128)(2,1)S(1)}, bf16[64,3584]{1,0:T(8,128)(2,1)S(1)}, u32[]{:S(2)}, u32[]{:S(2)}) collective-permute-start(bf16[64,3584]{1,0:T(8,128)(2,1)S(1)} %reshape.119.refs_1_), channel_id=1, source_target_pairs={{32,0},{48,16},{64,32},{80,48},{96,64},{112,80},{0,96},{16,112},{3... | collective-permute-start | bytes 1376264 | tf_op jit(solution)/shard_map/ppermute | solution.py:343
  65.8 15.0 %collective-permute-start.3 = (bf16[64,3584]{1,0:T(8,128)(2,1)S(1)}, bf16[64,3584]{1,0:T(8,128)(2,1)S(1)}, u32[]{:S(2)}, u32[]{:S(2)}) collective-permute-start(bf16[64,3584]{1,0:T(8,128)(2,1)S(1)} %reshape.119.refs_1_), channel_id=1, source_target_pairs={{64,0},{80,16},{96,32},{112,48},{0,64},{16,80},{32,96},{48,112},{6... | collective-permute-start | bytes 1376264 | tf_op jit(solution)/shard_map/ppermute | solution.py:343
  68.6 17.1 %collective-permute-start.5 = (bf16[64,3584]{1,0:T(8,128)(2,1)S(1)}, bf16[64,3584]{1,0:T(8,128)(2,1)S(1)}, u32[]{:S(2)}, u32[]{:S(2)}) collective-permute-start(bf16[64,3584]{1,0:T(8,128)(2,1)S(1)} %reshape.119.refs_1_), channel_id=1, source_target_pairs={{96,0},{112,16},{0,32},{16,48},{32,64},{48,80},{64,96},{80,112},{9... | collective-permute-start | bytes 1376264 | tf_op jit(solution)/shard_map/ppermute | solution.py:343
  79.1 16.5 %copy-start.8 = (bf16[64,3584]{1,0:T(8,128)(2,1)}, bf16[64,3584]{1,0:T(8,128)(2,1)S(1)}, u32[]{:S(2)}) copy-start(bf16[64,3584]{1,0:T(8,128)(2,1)S(1)} %collective-permute-done.1.refs_3_) | copy-start | bytes 1376260
  80.8 14.9 %copy-start.9 = (bf16[64,3584]{1,0:T(8,128)(2,1)}, bf16[64,3584]{1,0:T(8,128)(2,1)S(1)}, u32[]{:S(2)}) copy-start(bf16[64,3584]{1,0:T(8,128)(2,1)S(1)} %collective-permute-done.3.refs_5_) | copy-start | bytes 1376260
  85.6 10.0 %copy-start.10 = (bf16[64,3584]{1,0:T(8,128)(2,1)}, bf16[64,3584]{1,0:T(8,128)(2,1)S(1)}, u32[]{:S(2)}) copy-start(bf16[64,3584]{1,0:T(8,128)(2,1)S(1)} %collective-permute-done.5.refs_7_) | copy-start | bytes 1376260
  88.9 6.7 %collective-permute-start.10 = (bf16[256,3584]{1,0:T(8,128)(2,1)}, bf16[256,3584]{1,0:T(8,128)(2,1)}, u32[]{:S(2)}, u32[]{:S(2)}) collective-permute-start(bf16[256,3584]{1,0:T(8,128)(2,1)} %bitcast.17.refs_9_), channel_id=1, source_target_pairs={{0,16},{16,0},{32,48},{48,32},{64,80},{80,64},{96,112},{112,96},{1... | collective-permute-start | bytes 5505032 | tf_op jit(solution)/shard_map/ppermute | solution.py:418
  88.9 4.7 %collective-permute-start = (bf16[64,3584]{1,0:T(8,128)(2,1)S(1)}, bf16[64,3584]{1,0:T(8,128)(2,1)S(1)}, u32[]{:S(2)}, u32[]{:S(2)}) collective-permute-start(bf16[64,3584]{1,0:T(8,128)(2,1)S(1)} %reshape.119.refs_1_), channel_id=1, source_target_pairs={{0,16},{16,0},{32,48},{48,32},{64,80},{80,64},{96,112},{112,96},{1... | collective-permute-start | bytes 1376264 | tf_op jit(solution)/shard_map/ppermute | solution.py:416
  89.4 4.3 %collective-permute-start.2 = (bf16[64,3584]{1,0:T(8,128)(2,1)S(1)}, bf16[64,3584]{1,0:T(8,128)(2,1)}, u32[]{:S(2)}, u32[]{:S(2)}) collective-permute-start(bf16[64,3584]{1,0:T(8,128)(2,1)S(1)} %collective-permute-done.1.refs_3_), channel_id=1, source_target_pairs={{0,16},{16,0},{32,48},{48,32},{64,80},{80,64},{96,112},{112,96},{1... | collective-permute-start | bytes 1376264 | tf_op jit(solution)/shard_map/ppermute | solution.py:416
  89.4 5.0 %collective-permute-start.4 = (bf16[64,3584]{1,0:T(8,128)(2,1)S(1)}, bf16[64,3584]{1,0:T(8,128)(2,1)}, u32[]{:S(2)}, u32[]{:S(2)}) collective-permute-start(bf16[64,3584]{1,0:T(8,128)(2,1)S(1)} %collective-permute-done.3.refs_5_), channel_id=1, source_target_pairs={{0,16},{16,0},{32,48},{48,32},{64,80},{80,64},{96,112},{112,96},{1... | collective-permute-start | bytes 1376264 | tf_op jit(solution)/shard_map/ppermute | solution.py:416
  89.9 5.5 %collective-permute-start.6 = (bf16[64,3584]{1,0:T(8,128)(2,1)S(1)}, bf16[64,3584]{1,0:T(8,128)(2,1)}, u32[]{:S(2)}, u32[]{:S(2)}) collective-permute-start(bf16[64,3584]{1,0:T(8,128)(2,1)S(1)} %collective-permute-done.5.refs_7_), channel_id=1, source_target_pairs={{0,16},{16,0},{32,48},{48,32},{64,80},{80,64},{96,112},{112,96},{1... | collective-permute-start | bytes 1376264 | tf_op jit(solution)/shard_map/ppermute | solution.py:416
  108.8 2.2 %collective-permute-start.16 = (bf16[64,4096]{1,0:T(8,128)(2,1)}, bf16[64,4096]{1,0:T(8,128)(2,1)S(1)}, u32[]{:S(2)}, u32[]{:S(2)}) collective-permute-start(bf16[64,4096]{1,0:T(8,128)(2,1)} %get-tuple-element.24), channel_id=1, source_target_pairs={{0,16},{16,0},{32,48},{48,32},{64,80},{80,64},{96,112},{112,96},{1... | collective-permute-start | bytes 1572872 | tf_op jit(solution)/shard_map/ppermute | solution.py:438
  109.0 11.0 %collective-permute-start.18 = (bf16[256,3072]{1,0:T(8,128)(2,1)}, bf16[256,3072]{1,0:T(8,128)(2,1)S(1)}, u32[]{:S(2)}, u32[]{:S(2)}) collective-permute-start(bf16[256,3072]{1,0:T(8,128)(2,1)} %get-tuple-element.26), channel_id=1, source_target_pairs={{0,16},{16,0},{32,48},{48,32},{64,80},{80,64},{96,112},{112,96},{1... | collective-permute-start | bytes 4718600 | tf_op jit(solution)/shard_map/ppermute | solution.py:445
  109.4 5.4 %collective-permute-start.14 = (bf16[64,4096]{1,0:T(8,128)(2,1)}, bf16[64,4096]{1,0:T(8,128)(2,1)S(1)}, u32[]{:S(2)}, u32[]{:S(2)}) collective-permute-start(bf16[64,4096]{1,0:T(8,128)(2,1)} %get-tuple-element.22), channel_id=1, source_target_pairs={{0,16},{16,0},{32,48},{48,32},{64,80},{80,64},{96,112},{112,96},{1... | collective-permute-start | bytes 1572872 | tf_op jit(solution)/shard_map/ppermute | solution.py:438
  109.5 6.2 %collective-permute-start.12 = (bf16[64,4096]{1,0:T(8,128)(2,1)}, bf16[64,4096]{1,0:T(8,128)(2,1)S(1)}, u32[]{:S(2)}, u32[]{:S(2)}) collective-permute-start(bf16[64,4096]{1,0:T(8,128)(2,1)} %get-tuple-element.20), channel_id=1, source_target_pairs={{0,16},{16,0},{32,48},{48,32},{64,80},{80,64},{96,112},{112,96},{1... | collective-permute-start | bytes 1572872 | tf_op jit(solution)/shard_map/ppermute | solution.py:438
  109.9 16.1 %collective-permute-start.11 = (bf16[64,4096]{1,0:T(8,128)(2,1)}, bf16[64,4096]{1,0:T(8,128)(2,1)}, u32[]{:S(2)}, u32[]{:S(2)}) collective-permute-start(bf16[64,4096]{1,0:T(8,128)(2,1)} %get-tuple-element.18), channel_id=1, source_target_pairs={{0,16},{16,0},{32,48},{48,32},{64,80},{80,64},{96,112},{112,96},{1... | collective-permute-start | bytes 1572872 | tf_op jit(solution)/shard_map/ppermute | solution.py:438
  112.2 26.6 %collective-permute-start.17 = (bf16[64,4096]{1,0:T(8,128)(2,1)S(1)}, bf16[64,4096]{1,0:T(8,128)(2,1)}, u32[]{:S(2)}, u32[]{:S(2)}) collective-permute-start(bf16[64,4096]{1,0:T(8,128)(2,1)S(1)} %add_convert_fusion.2), channel_id=1, source_target_pairs={{96,0},{112,16},{0,32},{16,48},{32,64},{48,80},{64,96},{80,112},{9... | collective-permute-start | bytes 1572872 | tf_op jit(solution)/shard_map/ppermute | solution.py:343
  115.7 23.1 %collective-permute-start.15 = (bf16[64,4096]{1,0:T(8,128)(2,1)}, bf16[64,4096]{1,0:T(8,128)(2,1)}, u32[]{:S(2)}, u32[]{:S(2)}) collective-permute-start(bf16[64,4096]{1,0:T(8,128)(2,1)} %add_convert_fusion.3), channel_id=1, source_target_pairs={{64,0},{80,16},{96,32},{112,48},{0,64},{16,80},{32,96},{48,112},{6... | collective-permute-start | bytes 1572872 | tf_op jit(solution)/shard_map/ppermute | solution.py:343
  116.7 23.8 %collective-permute-start.13 = (bf16[64,4096]{1,0:T(8,128)(2,1)}, bf16[64,4096]{1,0:T(8,128)(2,1)}, u32[]{:S(2)}, u32[]{:S(2)}) collective-permute-start(bf16[64,4096]{1,0:T(8,128)(2,1)} %add_convert_fusion.4), channel_id=1, source_target_pairs={{32,0},{48,16},{64,32},{80,48},{96,64},{112,80},{0,96},{16,112},{3... | collective-permute-start | bytes 1572872 | tf_op jit(solution)/shard_map/ppermute | solution.py:343
  121.8 27.5 %all-to-all-start.4 = ((bf16[16,16,3072]{2,1,0:T(8,128)(2,1)}), bf16[16,16,3072]{2,1,0:T(8,128)(2,1)S(1)}, u32[]{:S(2)}, u32[]{:S(2)}) async-start(bf16[16,16,3072]{2,1,0:T(8,128)(2,1)} %bitcast.20), calls=%async_computation.4 | async-start | bytes 3145728 | tf_op jit(solution)/shard_map/all_to_all | solution.py:447
  149.2 14.0 %all-to-all-start.3 = ((bf16[16,4,4096]{2,1,0:T(4,128)(2,1)}), bf16[16,4,4096]{2,1,0:T(4,128)(2,1)S(1)}, u32[]{:S(2)}, u32[]{:S(2)}) async-start(bf16[16,4,4096]{2,1,0:T(4,128)(2,1)} %reshape.123), calls=%async_computation.3 | async-start | bytes 1048576 | tf_op jit(solution)/shard_map/all_to_all | solution.py:459
  153.9 9.9 %collective-permute-start.21 = (bf16[6,3072]{1,0:T(8,128)(2,1)S(1)}, bf16[6,3072]{1,0:T(8,128)(2,1)S(1)}, u32[]{:S(2)}, u32[]{:S(2)}) collective-permute-start(bf16[6,3072]{1,0:T(8,128)(2,1)S(1)} %get-tuple-element.30), channel_id=1, source_target_pairs={{96,0},{112,16},{0,32},{16,48},{32,64},{48,80},{64,96},{80,112},{9... | collective-permute-start | bytes 110600 | tf_op jit(solution)/shard_map/ppermute | solution.py:343
  154.0 9.8 %collective-permute-start.20 = (bf16[6,3072]{1,0:T(8,128)(2,1)S(1)}, bf16[6,3072]{1,0:T(8,128)(2,1)S(1)}, u32[]{:S(2)}, u32[]{:S(2)}) collective-permute-start(bf16[6,3072]{1,0:T(8,128)(2,1)S(1)} %get-tuple-element.31), channel_id=1, source_target_pairs={{64,0},{80,16},{96,32},{112,48},{0,64},{16,80},{32,96},{48,112},{6... | collective-permute-start | bytes 110600 | tf_op jit(solution)/shard_map/ppermute | solution.py:343
  156.2 7.6 %collective-permute-start.19 = (bf16[6,3072]{1,0:T(8,128)(2,1)S(1)}, bf16[6,3072]{1,0:T(8,128)(2,1)S(1)}, u32[]{:S(2)}, u32[]{:S(2)}) collective-permute-start(bf16[6,3072]{1,0:T(8,128)(2,1)S(1)} %get-tuple-element.29), channel_id=1, source_target_pairs={{32,0},{48,16},{64,32},{80,48},{96,64},{112,80},{0,96},{16,112},{3... | collective-permute-start | bytes 110600 | tf_op jit(solution)/shard_map/ppermute | solution.py:343
  (7 other events, 47.3 us)

commit v5 on v4

--- a/solution.py
+++ b/solution.py
@@ -169,23 +169,25 @@
 
 
 OWNED = 4
+SLAB = 2048
 INNER = 2
 
 
-def expert_kernel(planes, cores, place, *refs):
-    blocks = refs[: planes * cores]
-    mine, other, gate_proj, up_proj, down_proj, *refs = refs[planes * cores :]
-    outs, refs = refs[: planes * cores + cores], refs[planes * cores + cores :]
+def expert_kernel(planes, sides, *refs):
+    blocks, refs = refs[:planes], refs[planes:]
+    mine, refs = refs[0], refs[1:]
+    weights = [refs[3 * side : 3 * side + 3] for side in range(sides)]
+    refs = refs[3 * sides :]
+    outs, refs = refs[: planes + 1], refs[planes + 1 :]
     x, x_rest, gate_w, up_w, down_w, *refs = refs
     gate_rest, up_rest, gate, up, spread, share_ring, share_rest = refs[:-3]
     row_sem, weight_sem, sent = refs[-3:]
-    core, plane = place[0], place[1]
     depth, rest = x.shape[1], x_rest.shape[1]
-    count = mine.shape[0]
-    block = gate.shape[2]
+    block = gate.shape[1]
     own = block // OWNED
     tile = depth // INNER
-    size = share_ring.shape[2]
+    size = share_ring.shape[1]
+    half = gate_w.shape[1] // sides
 
     def fetch(source, target, sem):
         copy = pltpu.make_async_copy(source, target, sem)
@@ -194,30 +196,29 @@
 
     def fetch_weights(at, start, length):
         rows_at = pl.ds(start, length)
-        return [
-            fetch(gate_proj.at[0, rows_at], gate_w.at[rows_at], weight_sem.at[2 * at]),
-            fetch(up_proj.at[0, rows_at], up_w.at[rows_at], weight_sem.at[2 * at + 1]),
-        ]
-
-    def row_of(at):
-        turn, c = at // cores, at % cores
-        c = core if c == 0 else 1 - core
-        return (plane + turn) % planes, c
-
-    rest_waits = fetch_weights(INNER, depth, rest) + [
-        fetch(mine, x_rest.at[pl.ds(0, count)], row_sem.at[INNER, 0]),
-        fetch(other, x_rest.at[pl.ds(count, count)], row_sem.at[INNER, 1]),
-    ]
+        copies = []
+        for side in range(sides):
+            columns = pl.ds(side * half, half)
+            for i, target in enumerate((gate_w, up_w)):
+                source = weights[side][i].at[0, rows_at]
+                copies.append(
+                    fetch(source, target.at[rows_at, columns], weight_sem.at[at, 2 * side + i])
+                )
+        return copies
+
+    rest_waits = fetch_weights(INNER, depth, rest) + [fetch(mine, x_rest, row_sem.at[INNER, 0])]
     waits = []
     for at in range(INNER):
         columns = pl.ds(at * tile, tile)
         copies = fetch_weights(at, at * tile, tile)
         for i, ref in enumerate(blocks):
-            y, c = row_of(i)
-            target = x.at[pl.ds(pl.multiple_of((y * cores + c) * block, block), block), columns]
+            target = x.at[pl.ds(i * block, block), columns]
             copies.append(fetch(ref.at[:, columns], target, row_sem.at[at, i]))
         waits.append(copies)
-    down_wait = fetch(down_proj.at[0], down_w, weight_sem.at[2 * INNER + 2])
+    down_waits = [
+        fetch(weights[side][2].at[0], down_w.at[pl.ds(side * half, half)], weight_sem.at[INNER + 1, side])
+        for side in range(sides)
+    ]
 
     for copy in rest_waits:
         copy.wait()
@@ -237,69 +238,64 @@
         else:
             gate[...] += gate_part
             up[...] += up_part
-    for i in range(planes * cores):
-        y, c = row_of(i)
-        turn, at = i // cores, i % cores
+    for turn in range(planes):
         for f in range(own):
-            start = at * count + (f * planes + turn) * OWNED
+            start = (f * planes + turn) * OWNED
             target = slice(f * OWNED, (f + 1) * OWNED)
-            gate[y, c, target] += gate_rest[start : start + OWNED]
-            up[y, c, target] += up_rest[start : start + OWNED]
+            gate[turn, target] += gate_rest[start : start + OWNED]
+            up[turn, target] += up_rest[start : start + OWNED]
     gated = gate[...]
-    gate[...] = gated * jax.nn.sigmoid(gated) * up[...]
-    down_wait.wait()
+    hidden = gated * jax.nn.sigmoid(gated) * up[...]
+    gate[...] = hidden
+    for copy in down_waits:
+        copy.wait()
+    hidden = hidden.reshape(planes * block, gate.shape[2]).astype(BF16)
     sends = []
-    for at in range(cores - 1, -1, -1):
-        pieces = []
-        for turn in range(planes):
-            y, c = row_of(turn * cores + at)
-            pieces.append(gate[y, c])
-            for f in range(own):
-                start = (f * planes + turn) * OWNED
-                spread[at, start : start + OWNED] = gate[y, c, f * OWNED : (f + 1) * OWNED]
-        ring = jnp.concatenate(pieces, axis=0).astype(BF16)
-        share_ring[at] = dot(ring, down_w[:, :size]).astype(BF16)
-        for turn in range(planes):
-            i = at * planes + turn
-            piece = share_ring.at[at, pl.ds(turn * block, block)]
-            sends.append(fetch(piece, outs[i], sent.at[i]))
-    for at in range(cores - 1, -1, -1):
-        share_rest[at] = dot(spread[at].astype(BF16), down_w[:, size:]).astype(BF16)
-        sends.append(fetch(share_rest.at[at], outs[planes * cores + at], sent.at[planes * cores + at]))
+    for at in range(0, size, SLAB):
+        columns = slice(at, min(at + SLAB, size))
+        share_ring[:, columns] = dot(hidden, down_w[:, columns]).astype(BF16)
+    for turn in range(planes):
+        piece = share_ring.at[pl.ds(turn * block, block)]
+        sends.append(fetch(piece, outs[turn], sent.at[turn]))
+        for f in range(own):
+            start = (f * planes + turn) * OWNED
+            spread[start : start + OWNED] = gate[turn, f * OWNED : (f + 1) * OWNED]
+    share_rest[...] = dot(spread[...].astype(BF16), down_w[:, size:]).astype(BF16)
+    sends.append(fetch(share_rest, outs[planes], sent.at[planes]))
     for copy in sends:
         copy.wait()
 
 
-def expert(place, blocks, mine, other, gate_proj, up_proj, down_proj, size, planes, cores):
+def expert(blocks, mine, weights, size):
+    planes, sides = len(blocks), len(weights)
     block, depth = blocks[0].shape
-    count = planes * cores * block
-    part, rest = mine.shape
-    hidden = gate_proj.shape[2]
-    width = down_proj.shape[2]
-    wide = (planes, cores, block, hidden)
+    count, rest = mine.shape
+    hidden = sides * weights[0][0].shape[2]
+    width = weights[0][2].shape[2]
+    wide = (planes, block, hidden)
     anywhere = pl.BlockSpec(memory_space=pl.ANY)
     return pl.pallas_call(
-        lambda *refs: expert_kernel(planes, cores, *refs),
-        out_shape=[jax.ShapeDtypeStruct((block, size), BF16)] * (planes * cores)
-        + [jax.ShapeDtypeStruct((part, width - size), BF16)] * cores,
-        in_specs=[pl.BlockSpec(memory_space=pltpu.SMEM)] + [anywhere] * (len(blocks) + 5),
-        out_specs=[anywhere] * (planes * cores + cores),
+        lambda *refs: expert_kernel(planes, sides, *refs),
+        out_shape=[jax.ShapeDtypeStruct((block, size), BF16)] * planes
+        + [jax.ShapeDtypeStruct((count, width - size), BF16)],
+        in_specs=[anywhere] * (planes + 1 + 3 * sides),
+        out_specs=[anywhere] * (planes + 1),
         scratch_shapes=[
             pltpu.VMEM((count, depth), BF16),
-            pltpu.VMEM((2 * part, rest), BF16),
+            pltpu.VMEM((count, rest), BF16),
             pltpu.VMEM((depth + rest, hidden), BF16),
             pltpu.VMEM((depth + rest, hidden), BF16),
             pltpu.VMEM((hidden, width), BF16),
-            pltpu.VMEM((2 * part, hidden), F32),
-            pltpu.VMEM((2 * part, hidden), F32),
+            pltpu.VMEM((count, hidden), F32),
+            pltpu.VMEM((count, hidden), F32),
             pltpu.VMEM(wide, F32),
             pltpu.VMEM(wide, F32),
-            pltpu.VMEM((cores, part, hidden), F32),
-            pltpu.VMEM((cores, part, size), BF16),
-            pltpu.VMEM((cores, part, width - size), BF16),
-            pltpu.SemaphoreType.DMA((INNER + 1, len(blocks))),
-            pltpu.SemaphoreType.DMA((2 * INNER + 3,)),
-            pltpu.SemaphoreType.DMA((planes * cores + cores,)),
+            pltpu.VMEM((count, hidden), F32),
+            pltpu.VMEM((count, size), BF16),
+            pltpu.VMEM((count, width - size), BF16),
+            pltpu.SemaphoreType.DMA((INNER + 1, planes)),
+            pltpu.SemaphoreType.DMA((INNER + 2, 2 * sides)),
+            pltpu.SemaphoreType.DMA((planes + 1,)),
         ],
         compiler_params=pltpu.CompilerParams(vmem_limit_bytes=60 << 20),
         cost_estimate=pl.CostEstimate(
@@ -307,7 +303,7 @@
             bytes_accessed=4 * count * width + 6 * width * hidden,
             transcendentals=count * hidden,
         ),
-    )(place, *blocks, mine, other, gate_proj, up_proj, down_proj)
+    )(*blocks, mine, *[v for side in weights for v in side])
 
 
 def local(
@@ -330,8 +326,6 @@
     owners = lax.axis_size("ffn")
     cores = 2
     planes = lax.axis_size("attn") // cores
-    core = lax.axis_index("attn") % cores
-    plane = lax.axis_index("attn") // cores
     swap = [(a, a ^ 1) for a in range(planes * cores)]
 
     def from_plane(v, ahead):
@@ -386,6 +380,9 @@
         left = left - term
     table = jnp.pad(jnp.concatenate(terms, axis=1), ((0, 0), (0, 128 - 4 * owners))).astype(BF16)
     pieces = lax.all_to_all(pieces, "ffn", split_axis=0, concat_axis=0, tiled=True)
+    weights_here = (gate_proj, up_proj, down_proj)
+    weights_there = [lax.ppermute(v, "attn", swap) for v in weights_here]
+    pieces, weights_there = lax.optimization_barrier((pieces, weights_there))
     attended = (
         jnp.sum(pieces.astype(F32), axis=0)
         .reshape(PARTS, row_count, width // PARTS)
@@ -412,37 +409,16 @@
     near = near[:, :, :rest].reshape(planes * row_count, rest)
     outgoing = dot(placed_all, near).astype(BF16).reshape(owners, planes * capacity, rest)
     mine = lax.all_to_all(outgoing, "ffn", split_axis=0, concat_axis=0, tiled=True)
-    *_, mine = lax.optimization_barrier((*by_plane, mine))
-    blocks = [v for held in by_plane for v in (held, lax.ppermute(held, "attn", swap))]
+    *by_plane, mine = lax.optimization_barrier((*by_plane, mine))
     mine = mine.reshape(owners * planes * capacity, rest)
-    other = lax.ppermute(mine, "attn", swap)
-
-    *pieces, ours, theirs = expert(
-        jnp.stack([core, plane]),
-        blocks,
-        mine,
-        other,
-        gate_proj,
-        up_proj,
-        down_proj,
-        OUT_RING,
-        planes,
-        cores,
-    )
-
-    def add(a, b):
-        return (a.astype(F32) + b.astype(F32)).astype(BF16)
-
-    ring = {}
-    for turn in (2, 1, 3, 0):
-        ring[turn] = add(pieces[turn], lax.ppermute(pieces[planes + turn], "attn", swap))
+    *ring, ours = expert(by_plane, mine, (weights_here, weights_there), OUT_RING)
+
     summed = ring[0].astype(F32)
     for ahead in range(1, planes):
         summed = summed + from_plane(ring[planes - ahead], ahead).astype(F32)
     summed = summed.astype(BF16)
 
     rest = width - OUT_RING
-    ours = add(ours, lax.ppermute(theirs, "attn", swap))
     ours = ours.reshape(owners, planes * capacity, rest)
     ours = lax.all_to_all(ours, "ffn", split_axis=0, concat_axis=0, tiled=True)
     ours = jnp.einsum(

time: 165 us -> 151 us (0.915)
  waiting for transfers between devices: 81.9 us -> 72.1 us
  other arithmetic: 9.61 us -> 3.78 us
  local copies, waits for them, and re-layouts: 3.47 us -> 5.59 us
    ppermute x10 -> x3, waiting for transfers between devices: 7.87 us -> 0.01 us  [local(): weights_there = [lax.ppermute(v, 'attn', swap) for v in weights_here]]
    convert_element_type x4 -> x0, other arithmetic: 4.83 us -> none  [add(): return (a.astype(F32) + b.astype(F32)).astype(BF16)]
    unnamed x24 -> x20, local copies, waits for them, and re-layouts: 0.06 us -> 2.13 us
    all_to_all x1, waiting for transfers between devices: 5.75 us -> 3.71 us  [local(): ours = lax.all_to_all(ours, 'ffn', split_axis=0, concat_axis=0, tiled=True)]
    ppermute x10 -> x3, starting transfers between devices: 2.25 us -> 0.51 us  [local(): weights_there = [lax.ppermute(v, 'attn', swap) for v in weights_here]]
    all_to_all x1, waiting for transfers between devices: 5.97 us -> 4.26 us  [local(): lax.all_to_all(summed.reshape(owners, capacity, OUT_RING), 'ffn', split_a...]
  transfers between devices with their start and end apart: 27 -> 20, of which waited for: 17 -> 10; matrix products, arithmetic and copies ran while one was open for 9% -> 6% of each run, Pallas kernels for 0% -> 7%
where the time goes in v5:
time: 151 us; the launch traced here: 150 us
  waiting for transfers between devices  72.1 us (48%)
  starting transfers between devices  42 us (28%)
  Pallas kernels  22.6 us (15%)
  local copies, waits for them, and re-layouts  5.59 us (4%)
  other arithmetic  3.78 us (3%)
  matrix products  3.57 us (2%)
    ppermute x12, waiting for transfers between devices, from_plane(): return lax.ppermute(v, 'attn', pairs)  33 us
    all_to_all x1, waiting for transfers between devices, local(): lax.all_to_all(pieces, 'ffn', split_axis=0, concat_axis=0, tiled=True)  21.8 us
    ppermute x12, starting transfers between devices, from_plane(): return lax.ppermute(v, 'attn', pairs)  17.3 us
    pallas_call x1, Pallas kernels, expert(): pl.pallas_call(lambda *refs: expert_kernel(planes, sides, *refs), out_sha...  12.1 us
    pallas_call x1, Pallas kernels, attend(): pl.pallas_call(lambda *refs: attend_kernel(scale, owners, parts, *refs),...  10.5 us
    all_to_all x2, waiting for transfers between devices, local(): lax.all_to_all(outgoing, 'ffn', split_axis=0, concat_axis=0, tiled=True)  9.35 us
    all_to_all x1, starting transfers between devices, local(): lax.all_to_all(pieces, 'ffn', split_axis=0, concat_axis=0, tiled=True)  8.1 us
    all_to_all x2, starting transfers between devices, local(): lax.all_to_all(outgoing, 'ffn', split_axis=0, concat_axis=0, tiled=True)  7.37 us
  transfers between devices with their start and end apart: 20, of which 10 were waited for; matrix products, arithmetic and copies ran while one was open for 6% of the time, Pallas kernels for 7%

profile of v5, /device:TPU:0, one launch (start us, length us, event | category | flops | bytes accessed | tf_op | source)
XLA Modules:
  0.0 150.1 jit_solution(13079351039637923848)
XLA Ops:
  0.5 10.5 %shard_map.136 = bf16[16,24,1792]{2,1,0:T(8,128)(2,1)} custom-call(s32[96]{0:T(128)} %refs_0_.1, bf16[96,4,512]{2,1,0:T(4,128)(2,1)} %refs_1_.1, bf16[96,64,512]{2,1,0:T(8,128)(2,1)} %refs_2_.1, bf16[4,64,96]{2,1,0:T(8,128)(2,1)} %bitcast.54, bf16[64,64,96]{2,1,0:T(8,128)(2,1)} %bitcast.46, bf16[4,512,128]{2,1,0:T(8,128)(2,1)} %refs_5_.2, ...), custom_call_target="tpu_custom_call" | custom-call | flops 905969664 | bytes 13631488 | tf_op jit(solution)/shard_map/pallas_call | solution.py:139
  11.0 8.1 %all-to-all-start = ((bf16[16,24,1792]{2,1,0:T(8,128)(2,1)}), bf16[16,24,1792]{2,1,0:T(8,128)(2,1)S(1)}, u32[]{:S(2)}, u32[]{:S(2)}) async-start(bf16[16,24,1792]{2,1,0:T(8,128)(2,1)} %shard_map.136), calls=%async_computation | async-start | bytes 2752512 | tf_op jit(solution)/shard_map/all_to_all | solution.py:382
  19.9 21.8 %all-to-all-done = bf16[16,24,1792]{2,1,0:T(8,128)(2,1)S(1)} async-done(((bf16[16,24,1792]{2,1,0:T(8,128)(2,1)}), bf16[16,24,1792]{2,1,0:T(8,128)(2,1)S(1)}, u32[]{:S(2)}, u32[]{:S(2)}) %all-to-all-start) | async-done | bytes 1376288 | tf_op jit(solution)/shard_map/all_to_all | solution.py:382
  42.3 1.7 %collective-permute-start.8 = (bf16[6,3712]{1,0:T(8,128)(2,1)S(1)}, bf16[6,3712]{1,0:T(8,128)(2,1)S(1)}, u32[]{:S(2)}, u32[]{:S(2)}) collective-permute-start(bf16[6,3712]{1,0:T(8,128)(2,1)S(1)} %get-tuple-element.39), channel_id=1, source_target_pairs={{96,0},{112,16},{0,32},{16,48},{32,64},{48,80},{64,96},{80,112},{9... | collective-permute-start | bytes 133640 | tf_op jit(solution)/shard_map/ppermute | solution.py:337
  43.9 2.9 %collective-permute-start.7 = (bf16[6,3712]{1,0:T(8,128)(2,1)S(1)}, bf16[6,3712]{1,0:T(8,128)(2,1)S(1)}, u32[]{:S(2)}, u32[]{:S(2)}) collective-permute-start(bf16[6,3712]{1,0:T(8,128)(2,1)S(1)} %get-tuple-element.39), channel_id=1, source_target_pairs={{64,0},{80,16},{96,32},{112,48},{0,64},{16,80},{32,96},{48,112},{6... | collective-permute-start | bytes 133640 | tf_op jit(solution)/shard_map/ppermute | solution.py:337
  46.9 1.3 collective-permute-start.6
  48.5 0.9 reshape.118
  49.4 3.7 %all-to-all-start.1 = ((bf16[16,4,3584]{2,1,0:T(4,128)(2,1)}), bf16[16,4,3584]{2,1,0:T(4,128)(2,1)S(1)}, u32[]{:S(2)}, u32[]{:S(2)}) async-start(bf16[16,4,3584]{2,1,0:T(4,128)(2,1)} %reshape.118), calls=%async_computation.1 | async-start | bytes 917504 | tf_op jit(solution)/shard_map/all_to_all | solution.py:398
  54.4 1.9 %convolution_convert_fusion = bf16[256,3584]{1,0:T(8,128)(2,1)} fusion(bf16[256,24]{1,0:T(8,128)(2,1)S(1)} %convert_element_type.126, bf16[24,3584]{1,0:T(8,128)(2,1)S(1)} %reshape.120), kind=kOutput, calls=%fused_computation | convolution fusion | flops 44957696 | bytes 2019328 | tf_op jit(solution)/shard_map/dot_general | solution.py:19
  56.3 6.5 %all-to-all-done.1 = bf16[16,4,3584]{2,1,0:T(4,128)(2,1)S(1)} async-done(((bf16[16,4,3584]{2,1,0:T(4,128)(2,1)}), bf16[16,4,3584]{2,1,0:T(4,128)(2,1)S(1)}, u32[]{:S(2)}, u32[]{:S(2)}) %all-to-all-start.1) | async-done | bytes 458784 | tf_op jit(solution)/shard_map/all_to_all | solution.py:398
  62.9 3.7 %all-to-all-start.2 = ((bf16[16,16,3584]{2,1,0:T(8,128)(2,1)}), bf16[16,16,3584]{2,1,0:T(8,128)(2,1)S(1)}, u32[]{:S(2)}, u32[]{:S(2)}) async-start(bf16[16,16,3584]{2,1,0:T(8,128)(2,1)} %bitcast.40), calls=%async_computation.2 | async-start | bytes 3670016 | tf_op jit(solution)/shard_map/all_to_all | solution.py:411
  66.8 2.7 %collective-permute-start.4 = (bf16[64,3584]{1,0:T(8,128)(2,1)S(1)}, bf16[64,3584]{1,0:T(8,128)(2,1)S(1)}, u32[]{:S(2)}, u32[]{:S(2)}) collective-permute-start(bf16[64,3584]{1,0:T(8,128)(2,1)S(1)} %reshape.119.refs_0_), channel_id=1, source_target_pairs={{64,0},{80,16},{96,32},{112,48},{0,64},{16,80},{32,96},{48,112},{6... | collective-permute-start | bytes 1376264 | tf_op jit(solution)/shard_map/ppermute | solution.py:337
  69.5 10.7 %collective-permute-done.3.refs_1_ = bf16[64,3584]{1,0:T(8,128)(2,1)S(1)} collective-permute-done((bf16[64,3584]{1,0:T(8,128)(2,1)S(1)}, bf16[64,3584]{1,0:T(8,128)(2,1)S(1)}, u32[]{:S(2)}, u32[]{:S(2)}) %collective-permute-start.3) | collective-permute-done | bytes 458784 | tf_op jit(solution)/shard_map/ppermute | solution.py:337
  80.2 1.6 %collective-permute-done.4.refs_2_ = bf16[64,3584]{1,0:T(8,128)(2,1)S(1)} collective-permute-done((bf16[64,3584]{1,0:T(8,128)(2,1)S(1)}, bf16[64,3584]{1,0:T(8,128)(2,1)S(1)}, u32[]{:S(2)}, u32[]{:S(2)}) %collective-permute-start.4) | collective-permute-done | bytes 458784 | tf_op jit(solution)/shard_map/ppermute | solution.py:337
  81.8 0.8 copy-done.6
  82.6 5.3 %collective-permute-done.5.refs_3_ = bf16[64,3584]{1,0:T(8,128)(2,1)} collective-permute-done((bf16[64,3584]{1,0:T(8,128)(2,1)S(1)}, bf16[64,3584]{1,0:T(8,128)(2,1)}, u32[]{:S(2)}, u32[]{:S(2)}) %collective-permute-start.5) | collective-permute-done | bytes 458784 | tf_op jit(solution)/shard_map/ppermute | solution.py:337
  88.0 2.8 %all-to-all-done.2 = bf16[16,16,3584]{2,1,0:T(8,128)(2,1)S(1)} async-done(((bf16[16,16,3584]{2,1,0:T(8,128)(2,1)}), bf16[16,16,3584]{2,1,0:T(8,128)(2,1)S(1)}, u32[]{:S(2)}, u32[]{:S(2)}) %all-to-all-start.2) | async-done | bytes 1835040 | tf_op jit(solution)/shard_map/all_to_all | solution.py:411
  90.8 1.3 copy-done
  92.1 12.1 %shard_map.137 = (bf16[64,4096]{1,0:T(8,128)(2,1)}, bf16[64,4096]{1,0:T(8,128)(2,1)}, bf16[64,4096]{1,0:T(8,128)(2,1)}, bf16[64,4096]{1,0:T(8,128)(2,1)}, bf16[256,3072]{1,0:T(8,128)(2,1)}) custom-call(bf16[64,3584]{1,0:T(8,128)(2,1)} %copy-done.1, bf16[64,3584]{1,0:T(8,128)(2,1)} %copy-done.5, bf16[64,3584]{1,0:T(8,128)(2,1)} %copy-done.6, ...), custom_call_target="tpu_custom_call" | custom-call | flops 5637144576 | bytes 29360128 | tf_op jit(solution)/shard_map/pallas_call | solution.py:277
  105.0 0.9 collective-permute-start.10
  105.9 1.8 %collective-permute-start.9 = (bf16[64,4096]{1,0:T(8,128)(2,1)}, bf16[64,4096]{1,0:T(8,128)(2,1)}, u32[]{:S(2)}, u32[]{:S(2)}) collective-permute-start(bf16[64,4096]{1,0:T(8,128)(2,1)} %get-tuple-element.29), channel_id=1, source_target_pairs={{32,0},{48,16},{64,32},{80,48},{96,64},{112,80},{0,96},{16,112},{3... | collective-permute-start | bytes 1572872 | tf_op jit(solution)/shard_map/ppermute | solution.py:337
  107.7 5.1 %all-to-all-start.4 = ((bf16[16,16,3072]{2,1,0:T(8,128)(2,1)}), bf16[16,16,3072]{2,1,0:T(8,128)(2,1)S(1)}, u32[]{:S(2)}, u32[]{:S(2)}) async-start(bf16[16,16,3072]{2,1,0:T(8,128)(2,1)} %bitcast.45), calls=%async_computation.4 | async-start | bytes 3145728 | tf_op jit(solution)/shard_map/all_to_all | solution.py:423
  113.4 14.7 %collective-permute-done.11 = bf16[64,4096]{1,0:T(8,128)(2,1)} collective-permute-done((bf16[64,4096]{1,0:T(8,128)(2,1)}, bf16[64,4096]{1,0:T(8,128)(2,1)}, u32[]{:S(2)}, u32[]{:S(2)}) %collective-permute-start.11) | collective-permute-done | bytes 524320 | tf_op jit(solution)/shard_map/ppermute | solution.py:337
  128.7 1.6 %add_convert_fusion = bf16[64,4096]{1,0:T(8,128)(2,1)S(1)} fusion(bf16[64,4096]{1,0:T(8,128)(2,1)} %collective-permute-done.11, bf16[64,4096]{1,0:T(8,128)(2,1)} %collective-permute-done.10, bf16[64,4096]{1,0:T(8,128)(2,1)} %collective-permute-done.9, bf16[64,4096]{1,0:T(8,128)(2,1)S(1)} %copy-done.4), kind=kLoop, calls=%fused_computation.5 | loop fusion | flops 2097152 | bytes 2621440 | tf_op jit(solution)/shard_map/convert_element_type | solution.py:419
  130.3 1.0 reshape.123
  131.3 3.7 %all-to-all-done.4 = bf16[16,16,3072]{2,1,0:T(8,128)(2,1)S(1)} async-done(((bf16[16,16,3072]{2,1,0:T(8,128)(2,1)}), bf16[16,16,3072]{2,1,0:T(8,128)(2,1)S(1)}, u32[]{:S(2)}, u32[]{:S(2)}) %all-to-all-start.4) | async-done | bytes 1572896 | tf_op jit(solution)/shard_map/all_to_all | solution.py:423
  135.0 3.6 %all-to-all-start.3 = ((bf16[16,4,4096]{2,1,0:T(4,128)(2,1)}), bf16[16,4,4096]{2,1,0:T(4,128)(2,1)S(1)}, u32[]{:S(2)}, u32[]{:S(2)}) async-start(bf16[16,4,4096]{2,1,0:T(4,128)(2,1)} %reshape.123), calls=%async_computation.3 | async-start | bytes 1048576 | tf_op jit(solution)/shard_map/all_to_all | solution.py:435
  138.6 0.8 convolution_convert_fusion.2
  139.4 0.8 collective-permute-start.14
  140.3 2.8 %collective-permute-start.13 = (bf16[6,3072]{1,0:T(8,128)(2,1)S(1)}, bf16[6,3072]{1,0:T(8,128)(2,1)S(1)}, u32[]{:S(2)}, u32[]{:S(2)}) collective-permute-start(bf16[6,3072]{1,0:T(8,128)(2,1)S(1)} %get-tuple-element.37), channel_id=1, source_target_pairs={{64,0},{80,16},{96,32},{112,48},{0,64},{16,80},{32,96},{48,112},{6... | collective-permute-start | bytes 110600 | tf_op jit(solution)/shard_map/ppermute | solution.py:337
  143.1 1.4 collective-permute-start.12
  144.5 4.3 %all-to-all-done.3 = bf16[16,4,4096]{2,1,0:T(4,128)(2,1)S(1)} async-done(((bf16[16,4,4096]{2,1,0:T(4,128)(2,1)}), bf16[16,4,4096]{2,1,0:T(4,128)(2,1)S(1)}, u32[]{:S(2)}, u32[]{:S(2)}) %all-to-all-start.3) | async-done | bytes 524320 | tf_op jit(solution)/shard_map/all_to_all | solution.py:435
  (78 shorter events, 6.6 us)
Async XLA Ops:
  0.0 41.7 %collective-permute-start = (bf16[1,7168,256]{2,1,0:T(8,128)(2,1)}, bf16[1,7168,256]{2,1,0:T(8,128)(2,1)}, u32[]{:S(2)}, u32[]{:S(2)}) collective-permute-start(bf16[1,7168,256]{2,1,0:T(8,128)(2,1)} %refs_5_.3), channel_id=1, source_target_pairs={{0,16},{16,0},{32,48},{48,32},{64,80},{80,64},{96,112},{112,96},{1... | collective-permute-start | bytes 11010056 | tf_op jit(solution)/shard_map/ppermute | solution.py:384
  0.0 41.7 %collective-permute-start.1 = (bf16[1,7168,256]{2,1,0:T(8,128)(2,1)}, bf16[1,7168,256]{2,1,0:T(8,128)(2,1)}, u32[]{:S(2)}, u32[]{:S(2)}) collective-permute-start(bf16[1,7168,256]{2,1,0:T(8,128)(2,1)} %refs_6_.1), channel_id=1, source_target_pairs={{0,16},{16,0},{32,48},{48,32},{64,80},{80,64},{96,112},{112,96},{1... | collective-permute-start | bytes 11010056 | tf_op jit(solution)/shard_map/ppermute | solution.py:384
  0.5 41.2 %collective-permute-start.2 = (bf16[1,256,7168]{2,1,0:T(8,128)(2,1)}, bf16[1,256,7168]{2,1,0:T(8,128)(2,1)}, u32[]{:S(2)}, u32[]{:S(2)}) collective-permute-start(bf16[1,256,7168]{2,1,0:T(8,128)(2,1)} %refs_7_.1), channel_id=1, source_target_pairs={{0,16},{16,0},{32,48},{48,32},{64,80},{80,64},{96,112},{112,96},{1... | collective-permute-start | bytes 11010056 | tf_op jit(solution)/shard_map/ppermute | solution.py:384
  11.0 8.2 %copy-start.7 = (bf16[7168]{0:T(1024)(128)(2,1)S(1)}, bf16[7168]{0:T(1024)(128)(2,1)}, u32[]{:S(2)}) copy-start(bf16[7168]{0:T(1024)(128)(2,1)} %param.22) | copy-start | bytes 43012
  11.0 8.2 %copy-start.8 = (s32[6,8]{1,0:T(8,128)S(1)}, s32[6,8]{1,0:T(8,128)}, u32[]{:S(2)}) copy-start(s32[6,8]{1,0:T(8,128)} %param.23) | copy-start | bytes 580
  11.0 8.2 %copy-start.9 = (f32[6,8]{1,0:T(8,128)S(1)}, f32[6,8]{1,0:T(8,128)}, u32[]{:S(2)}) copy-start(f32[6,8]{1,0:T(8,128)} %param.24) | copy-start | bytes 580
  11.0 30.9 %copy-start.2 = (bf16[6,7168]{1,0:T(8,128)(2,1)S(1)}, bf16[6,7168]{1,0:T(8,128)(2,1)}, u32[]{:S(2)}) copy-start(bf16[6,7168]{1,0:T(8,128)(2,1)} %param.21) | copy-start | bytes 258052
  11.0 30.7 %all-to-all-start = ((bf16[16,24,1792]{2,1,0:T(8,128)(2,1)}), bf16[16,24,1792]{2,1,0:T(8,128)(2,1)S(1)}, u32[]{:S(2)}, u32[]{:S(2)}) async-start(bf16[16,24,1792]{2,1,0:T(8,128)(2,1)} %shard_map.136), calls=%async_computation | async-start | bytes 2752512 | tf_op jit(solution)/shard_map/all_to_all | solution.py:382
  42.3 10.8 %collective-permute-start.8 = (bf16[6,3712]{1,0:T(8,128)(2,1)S(1)}, bf16[6,3712]{1,0:T(8,128)(2,1)S(1)}, u32[]{:S(2)}, u32[]{:S(2)}) collective-permute-start(bf16[6,3712]{1,0:T(8,128)(2,1)S(1)} %get-tuple-element.39), channel_id=1, source_target_pairs={{96,0},{112,16},{0,32},{16,48},{32,64},{48,80},{64,96},{80,112},{9... | collective-permute-start | bytes 133640 | tf_op jit(solution)/shard_map/ppermute | solution.py:337
  43.9 9.2 %collective-permute-start.7 = (bf16[6,3712]{1,0:T(8,128)(2,1)S(1)}, bf16[6,3712]{1,0:T(8,128)(2,1)S(1)}, u32[]{:S(2)}, u32[]{:S(2)}) collective-permute-start(bf16[6,3712]{1,0:T(8,128)(2,1)S(1)} %get-tuple-element.39), channel_id=1, source_target_pairs={{64,0},{80,16},{96,32},{112,48},{0,64},{16,80},{32,96},{48,112},{6... | collective-permute-start | bytes 133640 | tf_op jit(solution)/shard_map/ppermute | solution.py:337
  46.9 6.3 %collective-permute-start.6 = (bf16[6,3712]{1,0:T(8,128)(2,1)S(1)}, bf16[6,3712]{1,0:T(8,128)(2,1)S(1)}, u32[]{:S(2)}, u32[]{:S(2)}) collective-permute-start(bf16[6,3712]{1,0:T(8,128)(2,1)S(1)} %get-tuple-element.39), channel_id=1, source_target_pairs={{32,0},{48,16},{64,32},{80,48},{96,64},{112,80},{0,96},{16,112},{3... | collective-permute-start | bytes 133640 | tf_op jit(solution)/shard_map/ppermute | solution.py:337
  49.4 13.4 %all-to-all-start.1 = ((bf16[16,4,3584]{2,1,0:T(4,128)(2,1)}), bf16[16,4,3584]{2,1,0:T(4,128)(2,1)S(1)}, u32[]{:S(2)}, u32[]{:S(2)}) async-start(bf16[16,4,3584]{2,1,0:T(4,128)(2,1)} %reshape.118), calls=%async_computation.1 | async-start | bytes 917504 | tf_op jit(solution)/shard_map/all_to_all | solution.py:398
  62.9 27.9 %all-to-all-start.2 = ((bf16[16,16,3584]{2,1,0:T(8,128)(2,1)}), bf16[16,16,3584]{2,1,0:T(8,128)(2,1)S(1)}, u32[]{:S(2)}, u32[]{:S(2)}) async-start(bf16[16,16,3584]{2,1,0:T(8,128)(2,1)} %bitcast.40), calls=%async_computation.2 | async-start | bytes 3670016 | tf_op jit(solution)/shard_map/all_to_all | solution.py:411
  66.7 24.1 %copy-start.1 = (bf16[64,3584]{1,0:T(8,128)(2,1)}, bf16[64,3584]{1,0:T(8,128)(2,1)S(1)}, u32[]{:S(2)}) copy-start(bf16[64,3584]{1,0:T(8,128)(2,1)S(1)} %reshape.119.refs_0_) | copy-start | bytes 1376260
  66.7 13.5 %collective-permute-start.3 = (bf16[64,3584]{1,0:T(8,128)(2,1)S(1)}, bf16[64,3584]{1,0:T(8,128)(2,1)S(1)}, u32[]{:S(2)}, u32[]{:S(2)}) collective-permute-start(bf16[64,3584]{1,0:T(8,128)(2,1)S(1)} %reshape.119.refs_0_), channel_id=1, source_target_pairs={{32,0},{48,16},{64,32},{80,48},{96,64},{112,80},{0,96},{16,112},{3... | collective-permute-start | bytes 1376264 | tf_op jit(solution)/shard_map/ppermute | solution.py:337
  66.8 15.0 %collective-permute-start.4 = (bf16[64,3584]{1,0:T(8,128)(2,1)S(1)}, bf16[64,3584]{1,0:T(8,128)(2,1)S(1)}, u32[]{:S(2)}, u32[]{:S(2)}) collective-permute-start(bf16[64,3584]{1,0:T(8,128)(2,1)S(1)} %reshape.119.refs_0_), channel_id=1, source_target_pairs={{64,0},{80,16},{96,32},{112,48},{0,64},{16,80},{32,96},{48,112},{6... | collective-permute-start | bytes 1376264 | tf_op jit(solution)/shard_map/ppermute | solution.py:337
  69.5 18.4 %collective-permute-start.5 = (bf16[64,3584]{1,0:T(8,128)(2,1)S(1)}, bf16[64,3584]{1,0:T(8,128)(2,1)}, u32[]{:S(2)}, u32[]{:S(2)}) collective-permute-start(bf16[64,3584]{1,0:T(8,128)(2,1)S(1)} %reshape.119.refs_0_), channel_id=1, source_target_pairs={{96,0},{112,16},{0,32},{16,48},{32,64},{48,80},{64,96},{80,112},{9... | collective-permute-start | bytes 1376264 | tf_op jit(solution)/shard_map/ppermute | solution.py:337
  80.2 10.6 %copy-start.5 = (bf16[64,3584]{1,0:T(8,128)(2,1)}, bf16[64,3584]{1,0:T(8,128)(2,1)S(1)}, u32[]{:S(2)}) copy-start(bf16[64,3584]{1,0:T(8,128)(2,1)S(1)} %collective-permute-done.3.refs_1_) | copy-start | bytes 1376260
  81.8 0.8 copy-start.6
  90.8 1.3 copy-start
  104.2 23.9 %collective-permute-start.11 = (bf16[64,4096]{1,0:T(8,128)(2,1)}, bf16[64,4096]{1,0:T(8,128)(2,1)}, u32[]{:S(2)}, u32[]{:S(2)}) collective-permute-start(bf16[64,4096]{1,0:T(8,128)(2,1)} %get-tuple-element.31), channel_id=1, source_target_pairs={{96,0},{112,16},{0,32},{16,48},{32,64},{48,80},{64,96},{80,112},{9... | collective-permute-start | bytes 1572872 | tf_op jit(solution)/shard_map/ppermute | solution.py:337
  105.0 23.1 %collective-permute-start.10 = (bf16[64,4096]{1,0:T(8,128)(2,1)}, bf16[64,4096]{1,0:T(8,128)(2,1)}, u32[]{:S(2)}, u32[]{:S(2)}) collective-permute-start(bf16[64,4096]{1,0:T(8,128)(2,1)} %get-tuple-element.30), channel_id=1, source_target_pairs={{64,0},{80,16},{96,32},{112,48},{0,64},{16,80},{32,96},{48,112},{6... | collective-permute-start | bytes 1572872 | tf_op jit(solution)/shard_map/ppermute | solution.py:337
  105.9 22.8 %collective-permute-start.9 = (bf16[64,4096]{1,0:T(8,128)(2,1)}, bf16[64,4096]{1,0:T(8,128)(2,1)}, u32[]{:S(2)}, u32[]{:S(2)}) collective-permute-start(bf16[64,4096]{1,0:T(8,128)(2,1)} %get-tuple-element.29), channel_id=1, source_target_pairs={{32,0},{48,16},{64,32},{80,48},{96,64},{112,80},{0,96},{16,112},{3... | collective-permute-start | bytes 1572872 | tf_op jit(solution)/shard_map/ppermute | solution.py:337
  107.7 21.0 %copy-start.4 = (bf16[64,4096]{1,0:T(8,128)(2,1)S(1)}, bf16[64,4096]{1,0:T(8,128)(2,1)}, u32[]{:S(2)}) copy-start(bf16[64,4096]{1,0:T(8,128)(2,1)} %get-tuple-element.28) | copy-start | bytes 1572868
  107.7 27.3 %all-to-all-start.4 = ((bf16[16,16,3072]{2,1,0:T(8,128)(2,1)}), bf16[16,16,3072]{2,1,0:T(8,128)(2,1)S(1)}, u32[]{:S(2)}, u32[]{:S(2)}) async-start(bf16[16,16,3072]{2,1,0:T(8,128)(2,1)} %bitcast.45), calls=%async_computation.4 | async-start | bytes 3145728 | tf_op jit(solution)/shard_map/all_to_all | solution.py:423
  131.3 18.0 %copy-start.3 = (bf16[6,7168]{1,0:T(8,128)(2,1)S(1)}, bf16[6,7168]{1,0:T(8,128)(2,1)}, u32[]{:S(2)}) copy-start(bf16[6,7168]{1,0:T(8,128)(2,1)} %param.21) | copy-start | bytes 258052
  135.0 13.7 %all-to-all-start.3 = ((bf16[16,4,4096]{2,1,0:T(4,128)(2,1)}), bf16[16,4,4096]{2,1,0:T(4,128)(2,1)S(1)}, u32[]{:S(2)}, u32[]{:S(2)}) async-start(bf16[16,4,4096]{2,1,0:T(4,128)(2,1)} %reshape.123), calls=%async_computation.3 | async-start | bytes 1048576 | tf_op jit(solution)/shard_map/all_to_all | solution.py:435
  139.4 9.9 %collective-permute-start.14 = (bf16[6,3072]{1,0:T(8,128)(2,1)S(1)}, bf16[6,3072]{1,0:T(8,128)(2,1)S(1)}, u32[]{:S(2)}, u32[]{:S(2)}) collective-permute-start(bf16[6,3072]{1,0:T(8,128)(2,1)S(1)} %get-tuple-element.36), channel_id=1, source_target_pairs={{96,0},{112,16},{0,32},{16,48},{32,64},{48,80},{64,96},{80,112},{9... | collective-permute-start | bytes 110600 | tf_op jit(solution)/shard_map/ppermute | solution.py:337
  140.3 9.1 %collective-permute-start.13 = (bf16[6,3072]{1,0:T(8,128)(2,1)S(1)}, bf16[6,3072]{1,0:T(8,128)(2,1)S(1)}, u32[]{:S(2)}, u32[]{:S(2)}) collective-permute-start(bf16[6,3072]{1,0:T(8,128)(2,1)S(1)} %get-tuple-element.37), channel_id=1, source_target_pairs={{64,0},{80,16},{96,32},{112,48},{0,64},{16,80},{32,96},{48,112},{6... | collective-permute-start | bytes 110600 | tf_op jit(solution)/shard_map/ppermute | solution.py:337
  143.1 6.2 %collective-permute-start.12 = (bf16[6,3072]{1,0:T(8,128)(2,1)S(1)}, bf16[6,3072]{1,0:T(8,128)(2,1)S(1)}, u32[]{:S(2)}, u32[]{:S(2)}) collective-permute-start(bf16[6,3072]{1,0:T(8,128)(2,1)S(1)} %get-tuple-element.35), channel_id=1, source_target_pairs={{32,0},{48,16},{64,32},{80,48},{96,64},{112,80},{0,96},{16,112},{3... | collective-permute-start | bytes 110600 | tf_op jit(solution)/shard_map/ppermute | solution.py:337

commit v6 on v5

v6 whole, which is shorter than its diff:
```python
import math

import jax
import jax.numpy as jnp
from jax import lax
from jax.experimental import pallas as pl
from jax.experimental.pallas import tpu as pltpu
from jax.sharding import PartitionSpec as P

PARTS = 4
UNIT = 512
IN_RING = 3072
OUT_RING = 4096
F32 = jnp.float32
BF16 = jnp.bfloat16


def dot(a, b):
    return jnp.dot(a, b, preferred_element_type=F32)


GROUP = 4
STEPS = 3

def attend_kernel(
    scale,
    owners,
    parts,
    lengths,
    query,
    cache_here,
    query_rope,
    cache_rope,
    value_here,
    out_proj,
    out,
    rope,
    latent,
    values,
    weights,
    cache,
    value_up,
    arrived,
):
    all_rows, heads, depth = query.shape
    positions = cache.shape[1]
    rows = all_rows // STEPS
    count = GROUP * heads
    width = weights.shape[1] // parts

    def fetch(source, target, at):
        copy = pltpu.make_async_copy(source, target, arrived.at[at])
        copy.start()
        return copy

    chunks = []
    for step in range(STEPS):
        here = pl.ds(step * rows, rows)
        chunks.append(fetch(cache_here.at[here], cache.at[here], step))
    value_fetch = fetch(value_here, value_up, STEPS)
    fetches = []
    for part in range(parts):
        columns = pl.ds(part * width, width)
        fetches.append(
            fetch(out_proj.at[:, columns], weights.at[:, columns], STEPS + 1 + part)
        )

    for h in range(heads):
        vector = query_rope[h].astype(F32)
        terms = []
        for at in range(positions):
            terms.append(jnp.sum(vector * cache_rope[at].astype(F32), axis=0, keepdims=True))
        wide = jnp.concatenate(terms, axis=0).T
        rope[pl.ds(h, all_rows, heads), :] = jnp.concatenate([wide] * 2, axis=1)

    groups = rows // GROUP
    total = rows * heads
    for step in range(STEPS):
        chunks[step].wait()
        first = step * rows
        base = step * total
        keys = [
            cache[first + group * GROUP : first + (group + 1) * GROUP].reshape(
                GROUP * positions, depth
            )
            for group in range(groups)
        ]
        scores = []
        for group in range(groups):
            queries = jnp.concatenate(
                [query[first + group * GROUP + i] for i in range(GROUP)], axis=0
            )
            scores.append(
                lax.dot_general(
                    queries, keys[group], (((1,), (1,)), ((), ())), preferred_element_type=F32
                )
            )
        scores = jnp.concatenate(scores, axis=0)
        near = rope[base : base + total, :]
        scores = (scores + jnp.concatenate([near] * (GROUP // 2), axis=1)) * scale
        row = lax.broadcasted_iota(jnp.int32, scores.shape, 0) // heads
        own = lax.broadcasted_iota(jnp.int32, scores.shape, 1) - (row % GROUP) * positions
        limit = jnp.concatenate(
            [
                jnp.full((heads, GROUP * positions), lengths[first + i], jnp.int32)
                for i in range(rows)
            ],
            axis=0,
        )
        live = (own >= 0) & (own < limit)
        scores = jnp.where(live, scores, F32(-1e30))
        top = jnp.max(scores, axis=1, keepdims=True)
        expo = jnp.where(live, jnp.exp(scores - top), F32(0.0))
        probs = (expo / jnp.sum(expo, axis=1, keepdims=True)).astype(BF16)
        mixed = jnp.concatenate(
            [
                dot(probs[group * count : (group + 1) * count], keys[group])
                for group in range(groups)
            ],
            axis=0,
        )
        for part in range(depth // 128):
            latent[part, base : base + total, :] = mixed[:, part * 128 : (part + 1) * 128]

    value_fetch.wait()
    size = value_up.shape[2]
    for h in range(heads):
        mixed = jnp.concatenate(
            [latent[part, pl.ds(h, all_rows, heads), :] for part in range(depth // 128)], axis=1
        ).astype(BF16)
        values[:, h * size : (h + 1) * size] = dot(mixed, value_up[h]).astype(BF16)
    own_rows = all_rows // owners
    for part, copy in enumerate(fetches):
        copy.wait()
        result = dot(values[...], weights[:, part * width : (part + 1) * width]).astype(BF16)
        for f in range(owners):
            out[f, part * own_rows : (part + 1) * own_rows] = result[
                f * own_rows : (f + 1) * own_rows
            ]


def attend(query, query_rope, cache, cache_rope, lengths, value_up, out_proj, scale, owners, parts):
    rows, heads, depth = query.shape
    positions = cache.shape[1]
    size = heads * value_up.shape[2]
    width = out_proj.shape[2]
    shape = (owners, parts * (rows // owners), width // parts)
    anywhere = pl.BlockSpec(memory_space=pl.ANY)
    inside = pl.BlockSpec(memory_space=pltpu.VMEM)
    query_rope = jnp.transpose(query_rope, (1, 2, 0))
    cache_rope = jnp.transpose(cache_rope, (1, 2, 0))
    return pl.pallas_call(
        lambda *refs: attend_kernel(scale, owners, parts, *refs),
        out_shape=jax.ShapeDtypeStruct(shape, BF16),
        in_specs=[
            pl.BlockSpec(memory_space=pltpu.SMEM),
            inside,
            anywhere,
            inside,
            inside,
            anywhere,
            anywhere,
        ],
        out_specs=inside,
        scratch_shapes=[
            pltpu.VMEM((rows * heads, 2 * positions), F32),
            pltpu.VMEM((depth // 128, rows * heads, 128), F32),
            pltpu.VMEM((rows, size), BF16),
            pltpu.VMEM((size, width), BF16),
            pltpu.VMEM(cache.shape, BF16),
            pltpu.VMEM(value_up.shape, BF16),
            pltpu.SemaphoreType.DMA((STEPS + 1 + parts,)),
        ],
        compiler_params=pltpu.CompilerParams(vmem_limit_bytes=60 << 20),
        cost_estimate=pl.CostEstimate(
            flops=4 * rows * heads * positions * depth * GROUP + 2 * rows * size * width,
            bytes_accessed=2 * rows * positions * depth + 2 * size * width,
            transcendentals=rows * heads * positions,
        ),
    )(lengths, query, cache, query_rope, cache_rope, value_up, out_proj.reshape(size, width))


OWNED = 4
SLAB = 2048
INNER = 2


def fetch(source, target, sem):
    copy = pltpu.make_async_copy(source, target, sem)
    copy.start()
    return copy


def front_kernel(planes, sides, *refs):
    blocks, refs = refs[:planes], refs[planes:]
    weights, refs = refs[: 2 * sides], refs[2 * sides :]
    gate, up, x, gate_w, up_w, row_sem, weight_sem = refs
    depth = x.shape[1]
    block = gate.shape[1]
    tile = depth // INNER
    half = gate_w.shape[1] // sides
    waits = []
    for at in range(INNER):
        here = pl.ds(at * tile, tile)
        copies = []
        for i, source in enumerate(weights):
            target = (gate_w, up_w)[i % 2].at[here, pl.ds(i // 2 * half, half)]
            copies.append(fetch(source.at[0, here], target, weight_sem.at[at, i]))
        for i, ref in enumerate(blocks):
            target = x.at[pl.ds(i * block, block), here]
            copies.append(fetch(ref.at[:, here], target, row_sem.at[at, i]))
        waits.append(copies)
    for at in range(INNER):
        for copy in waits[at]:
            copy.wait()
        here = slice(at * tile, (at + 1) * tile)
        gate_part = dot(x[:, here], gate_w[here]).reshape(gate.shape)
        up_part = dot(x[:, here], up_w[here]).reshape(up.shape)
        if at == 0:
            gate[...] = gate_part
            up[...] = up_part
        else:
            gate[...] += gate_part
            up[...] += up_part


def expert_front(blocks, weights):
    planes, sides = len(blocks), len(weights)
    block, depth = blocks[0].shape
    hidden = sides * weights[0][0].shape[2]
    wide = jax.ShapeDtypeStruct((planes, block, hidden), F32)
    anywhere = pl.BlockSpec(memory_space=pl.ANY)
    inside = pl.BlockSpec(memory_space=pltpu.VMEM)
    return pl.pallas_call(
        lambda *refs: front_kernel(planes, sides, *refs),
        out_shape=[wide, wide],
        in_specs=[anywhere] * (planes + 2 * sides),
        out_specs=[inside, inside],
        scratch_shapes=[
            pltpu.VMEM((planes * block, depth), BF16),
            pltpu.VMEM((depth, hidden), BF16),
            pltpu.VMEM((depth, hidden), BF16),
            pltpu.SemaphoreType.DMA((INNER, planes)),
            pltpu.SemaphoreType.DMA((INNER, 2 * sides)),
        ],
        compiler_params=pltpu.CompilerParams(vmem_limit_bytes=60 << 20),
        cost_estimate=pl.CostEstimate(
            flops=4 * planes * block * depth * hidden,
            bytes_accessed=2 * planes * block * depth + 4 * depth * hidden,
            transcendentals=0,
        ),
    )(*blocks, *[v for side in weights for v in side[:2]])


def expert_kernel(planes, sides, *refs):
    gate_ring, up_ring, mine, refs = refs[0], refs[1], refs[2], refs[3:]
    weights = [refs[3 * side : 3 * side + 3] for side in range(sides)]
    refs = refs[3 * sides :]
    outs, refs = refs[: planes + 1], refs[planes + 1 :]
    x, gate_w, up_w, down_w, *refs = refs
    gate_rest, up_rest, gate, up, spread, share_ring, share_rest = refs[:-3]
    row_sem, weight_sem, sent = refs[-3:]
    rest = x.shape[1]
    depth = weights[0][0].shape[1] - rest
    block = gate.shape[1]
    own = block // OWNED
    tile = rest // INNER
    size = share_ring.shape[1]
    half = gate_w.shape[1] // sides

    waits = []
    for at in range(INNER):
        copies = []
        here = pl.ds(at * tile, tile)
        for side in range(sides):
            columns = pl.ds(side * half, half)
            for i, target in enumerate((gate_w, up_w)):
                source = weights[side][i].at[0, pl.ds(depth + at * tile, tile)]
                copies.append(
                    fetch(source, target.at[here, columns], weight_sem.at[at, 2 * side + i])
                )
        copies.append(fetch(mine.at[:, here], x.at[:, here], row_sem.at[at]))
        waits.append(copies)
    ring_waits = [
        fetch(gate_ring, gate, row_sem.at[INNER]),
        fetch(up_ring, up, row_sem.at[INNER + 1]),
    ]
    down_waits = [
        fetch(weights[side][2].at[0], down_w.at[pl.ds(side * half, half)], weight_sem.at[INNER, side])
        for side in range(sides)
    ]

    for at in range(INNER):
        for copy in waits[at]:
            copy.wait()
        here = slice(at * tile, (at + 1) * tile)
        gate_part = dot(x[:, here], gate_w[here])
        up_part = dot(x[:, here], up_w[here])
        if at == 0:
            gate_rest[...] = gate_part
            up_rest[...] = up_part
        else:
            gate_rest[...] += gate_part
            up_rest[...] += up_part
    for copy in ring_waits:
        copy.wait()
    for turn in range(planes):
        for f in range(own):
            start = (f * planes + turn) * OWNED
            target = slice(f * OWNED, (f + 1) * OWNED)
            gate[turn, target] += gate_rest[start : start + OWNED]
            up[turn, target] += up_rest[start : start + OWNED]
    gated = gate[...]
    hidden = gated * jax.nn.sigmoid(gated) * up[...]
    gate[...] = hidden
    for copy in down_waits:
        copy.wait()
    hidden = hidden.reshape(planes * block, gate.shape[2]).astype(BF16)
    sends = []
    for at in range(0, size, SLAB):
        columns = slice(at, min(at + SLAB, size))
        share_ring[:, columns] = dot(hidden, down_w[:, columns]).astype(BF16)
    for turn in range(planes):
        piece = share_ring.at[pl.ds(turn * block, block)]
        sends.append(fetch(piece, outs[turn], sent.at[turn]))
        for f in range(own):
            start = (f * planes + turn) * OWNED
            spread[start : start + OWNED] = gate[turn, f * OWNED : (f + 1) * OWNED]
    share_rest[...] = dot(spread[...].astype(BF16), down_w[:, size:]).astype(BF16)
    sends.append(fetch(share_rest, outs[planes], sent.at[planes]))
    for copy in sends:
        copy.wait()


def expert(gate_ring, up_ring, mine, weights, size):
    planes, block, hidden = gate_ring.shape
    sides = len(weights)
    count, rest = mine.shape
    width = weights[0][2].shape[2]
    wide = (planes, block, hidden)
    anywhere = pl.BlockSpec(memory_space=pl.ANY)
    return pl.pallas_call(
        lambda *refs: expert_kernel(planes, sides, *refs),
        out_shape=[jax.ShapeDtypeStruct((block, size), BF16)] * planes
        + [jax.ShapeDtypeStruct((count, width - size), BF16)],
        in_specs=[anywhere] * (3 + 3 * sides),
        out_specs=[anywhere] * (planes + 1),
        scratch_shapes=[
            pltpu.VMEM((count, rest), BF16),
            pltpu.VMEM((rest, hidden), BF16),
            pltpu.VMEM((rest, hidden), BF16),
            pltpu.VMEM((hidden, width), BF16),
            pltpu.VMEM((count, hidden), F32),
            pltpu.VMEM((count, hidden), F32),
            pltpu.VMEM(wide, F32),
            pltpu.VMEM(wide, F32),
            pltpu.VMEM((count, hidden), F32),
            pltpu.VMEM((count, size), BF16),
            pltpu.VMEM((count, width - size), BF16),
            pltpu.SemaphoreType.DMA((INNER + 2,)),
            pltpu.SemaphoreType.DMA((INNER + 1, 2 * sides)),
            pltpu.SemaphoreType.DMA((planes + 1,)),
        ],
        compiler_params=pltpu.CompilerParams(vmem_limit_bytes=60 << 20),
        cost_estimate=pl.CostEstimate(
            flops=4 * count * rest * hidden + 2 * count * width * hidden,
            bytes_accessed=2 * count * (width + rest) + (4 * rest + 2 * width) * hidden,
            transcendentals=count * hidden,
        ),
    )(gate_ring, up_ring, mine, *[v for side in weights for v in side])


def local(
    query_latent,
    query_rope,
    cache_latent,
    cache_rope,
    lengths,
    value_up,
    out_proj,
    residual,
    norm_gain,
    expert_ids,
    route_weights,
    gate_proj,
    up_proj,
    down_proj,
):
    row_count, width = residual.shape
    owners = lax.axis_size("ffn")
    cores = 2
    planes = lax.axis_size("attn") // cores
    swap = [(a, a ^ 1) for a in range(planes * cores)]

    def from_plane(v, ahead):
        pairs = [
            (((y + ahead) % planes) * cores + c, y * cores + c)
            for y in range(planes)
            for c in range(cores)
        ]
        return lax.ppermute(v, "attn", pairs)

    def along_planes(v):
        return jnp.stack([v] + [from_plane(v, ahead) for ahead in range(1, planes)])

    named = expert_ids[:, :, None] == jnp.arange(owners, dtype=jnp.int32)[None, None, :]
    routed = jnp.sum(named.astype(F32), axis=1)
    row_weights = jnp.sum(jnp.where(named, route_weights[:, :, None], F32(0.0)), axis=1)
    capacity = min(row_count, row_count * expert_ids.shape[1] // owners + 1)

    def slots_of(routed, weight):
        rank = jnp.cumsum(routed, axis=-2) - routed
        routed, weight, rank = (jnp.moveaxis(v, -1, 0)[..., None, :] for v in (routed, weight, rank))
        slot = jnp.arange(capacity, dtype=jnp.int32).astype(F32)[:, None]
        placed = ((routed == 1.0) & (rank == slot)).astype(F32)
        return placed, placed * weight

    score_scale = (value_up.shape[2] + query_rope.shape[2]) ** (-0.5)
    pieces = attend(
        query_latent,
        query_rope,
        cache_latent,
        cache_rope,
        lengths,
        value_up,
        out_proj,
        score_scale,
        owners,
        PARTS,
    )
    eye = jnp.eye(planes, dtype=F32)

    def block_diagonal(v):
        spread = v[:, :, :, None, :] * eye[None, :, None, :, None]
        return spread.reshape(owners * planes * capacity, planes * row_count)

    placed, weighting = slots_of(routed, row_weights)
    placed = placed.reshape(owners * capacity, row_count).astype(BF16)
    weighting = weighting.reshape(owners * capacity, row_count)
    terms, left = [routed], row_weights
    for _ in range(3):
        term = lax.reduce_precision(left, 8, 7)
        terms.append(term)
        left = left - term
    table = jnp.pad(jnp.concatenate(terms, axis=1), ((0, 0), (0, 128 - 4 * owners))).astype(BF16)
    pieces = lax.all_to_all(pieces, "ffn", split_axis=0, concat_axis=0, tiled=True)
    weights_here = (gate_proj, up_proj, down_proj)
    weights_there = [lax.ppermute(v, "attn", swap) for v in weights_here]
    pieces, weights_there = lax.optimization_barrier((pieces, weights_there))
    attended = (
        jnp.sum(pieces.astype(F32), axis=0)
        .reshape(PARTS, row_count, width // PARTS)
        .transpose(1, 0, 2)
        .reshape(row_count, width)
    )
    mixed = residual.astype(F32) + attended
    inverse = lax.rsqrt(jnp.mean(mixed * mixed, axis=1, keepdims=True) + 1e-06)
    normed = (mixed * inverse * norm_gain.astype(F32)[None, :]).astype(BF16)

    outgoing = dot(placed, normed[:, :IN_RING]).astype(BF16).reshape(owners, capacity, IN_RING)
    near = jnp.concatenate([normed[:, IN_RING:], table], axis=1)
    arrived = lax.all_to_all(outgoing, "ffn", split_axis=0, concat_axis=0, tiled=True)
    arrived = arrived.reshape(owners * capacity, IN_RING)

    rest = width - IN_RING
    by_plane = [arrived] + [from_plane(arrived, ahead) for ahead in range(1, planes)]
    near = along_planes(near)
    tables = near[:, :, rest:].astype(F32)
    tables = [tables[:, :, at * owners : (at + 1) * owners] for at in range(4)]
    placed_all, weighting_all = slots_of(tables[0], tables[1] + tables[2] + tables[3])
    placed_all = block_diagonal(placed_all).astype(BF16)
    weighting_all = block_diagonal(weighting_all)
    near = near[:, :, :rest].reshape(planes * row_count, rest)
    outgoing = dot(placed_all, near).astype(BF16).reshape(owners, planes * capacity, rest)
    mine = lax.all_to_all(outgoing, "ffn", split_axis=0, concat_axis=0, tiled=True)
    weights = (weights_here, weights_there)
    gate_ring, up_ring = expert_front(by_plane, weights)
    gate_ring, up_ring, mine = lax.optimization_barrier((gate_ring, up_ring, mine))
    mine = mine.reshape(owners * planes * capacity, rest)
    *ring, ours = expert(gate_ring, up_ring, mine, weights, OUT_RING)

    summed = ring[0].astype(F32)
    for ahead in range(1, planes):
        summed = summed + from_plane(ring[planes - ahead], ahead).astype(F32)
    summed = summed.astype(BF16)

    rest = width - OUT_RING
    ours = ours.reshape(owners, planes * capacity, rest)
    ours = lax.all_to_all(ours, "ffn", split_axis=0, concat_axis=0, tiled=True)
    ours = jnp.einsum(
        "sr,sd->rd",
        weighting_all,
        ours.reshape(owners * planes * capacity, rest).astype(F32),
        precision=lax.Precision.HIGHEST,
    ).astype(BF16)
    ours = ours.reshape(planes, row_count, rest)
    sum_rest = ours[0].astype(F32)
    for ahead in range(1, planes):
        sum_rest = sum_rest + from_plane(ours[planes - ahead], ahead).astype(F32)

    returned = lax.all_to_all(
        summed.reshape(owners, capacity, OUT_RING), "ffn", split_axis=0, concat_axis=0, tiled=True
    )
    sum_ring = jnp.einsum(
        "sr,sd->rd",
        weighting,
        returned.reshape(owners * capacity, OUT_RING).astype(F32),
        precision=lax.Precision.HIGHEST,
    )
    return (mixed + jnp.concatenate([sum_ring, sum_rest], axis=1)).astype(BF16)


def solution(mesh):
    return jax.shard_map(
        local,
        mesh=mesh,
        in_specs=(
            P("attn", "ffn", None),
            P("attn", "ffn", None),
            P("attn", None, None),
            P("attn", None, None),
            P("attn"),
            P("ffn", None, None),
            P("ffn", None, None),
            P(("attn", "ffn"), None),
            P(),
            P(("attn", "ffn"), None),
            P(("attn", "ffn"), None),
            P("ffn", None, "attn"),
            P("ffn", None, "attn"),
            P("ffn", "attn", None),
        ),
        out_specs=P(("attn", "ffn"), None),
        check_vma=False,
    )
```

time: 151 us -> 149 us (0.987)
  starting transfers between devices: 42 us -> 40.2 us
  Pallas kernels: 22.6 us -> 24.2 us
    pallas_call x0 -> x1, Pallas kernels: none -> 5.13 us  [expert_front(): pl.pallas_call(lambda *refs: front_kernel(planes, sides, *refs), out_shap...]
    ppermute x12, waiting for transfers between devices: 33 us -> 30 us  [from_plane(): return lax.ppermute(v, 'attn', pairs)]
    pallas_call x1, Pallas kernels: 12.1 us -> 9.88 us  [expert(): pl.pallas_call(lambda *refs: expert_kernel(planes, sides, *refs), out_sha...]
  transfers between devices with their start and end apart: 20 -> 20, of which waited for: 10 -> 10; matrix products, arithmetic and copies ran while one was open for 6% -> 7% of each run, Pallas kernels for 7% -> 10%
where the time goes in v6:
time: 149 us
  waiting for transfers between devices  70.7 us (47%)
  starting transfers between devices  40.2 us (27%)
  Pallas kernels  24.2 us (16%)
  local copies, waits for them, and re-layouts  5.65 us (4%)
  other arithmetic  3.79 us (3%)
  matrix products  3.76 us (3%)
    ppermute x12, waiting for transfers between devices, from_plane(): return lax.ppermute(v, 'attn', pairs)  30 us
    all_to_all x1, waiting for transfers between devices, local(): lax.all_to_all(pieces, 'ffn', split_axis=0, concat_axis=0, tiled=True)  21.8 us
    ppermute x12, starting transfers between devices, from_plane(): return lax.ppermute(v, 'attn', pairs)  16.1 us
    pallas_call x1, Pallas kernels, expert(): pl.pallas_call(lambda *refs: expert_kernel(planes, sides, *refs), out_sha...  9.88 us
    pallas_call x1, Pallas kernels, attend(): pl.pallas_call(lambda *refs: attend_kernel(scale, owners, parts, *refs),...  9.22 us
    all_to_all x2, waiting for transfers between devices, local(): lax.all_to_all(outgoing, 'ffn', split_axis=0, concat_axis=0, tiled=True)  9.05 us
    all_to_all x1, starting transfers between devices, local(): lax.all_to_all(pieces, 'ffn', split_axis=0, concat_axis=0, tiled=True)  8.1 us
    all_to_all x2, starting transfers between devices, local(): lax.all_to_all(outgoing, 'ffn', split_axis=0, concat_axis=0, tiled=True)  7.38 us
  transfers between devices with their start and end apart: 20, of which 10 were waited for; matrix products, arithmetic and copies ran while one was open for 7% of the time, Pallas kernels for 10%

profile of v6, /device:TPU:0, one launch (start us, length us, event | category | flops | bytes accessed | tf_op | source)
XLA Modules:
  0.0 148.7 jit_solution(8773284538275639895)
XLA Ops:
  0.5 9.2 %shard_map.136 = bf16[16,24,1792]{2,1,0:T(8,128)(2,1)} custom-call(s32[96]{0:T(128)} %refs_0_.1, bf16[96,4,512]{2,1,0:T(4,128)(2,1)} %refs_1_.1, bf16[96,64,512]{2,1,0:T(8,128)(2,1)} %refs_2_.1, bf16[4,64,96]{2,1,0:T(8,128)(2,1)} %bitcast.54, bf16[64,64,96]{2,1,0:T(8,128)(2,1)} %bitcast.46, bf16[4,512,128]{2,1,0:T(8,128)(2,1)} %refs_5_.3, ...), custom_call_target="tpu_custom_call" | custom-call | flops 905969664 | bytes 13631488 | tf_op jit(solution)/shard_map/pallas_call | solution.py:152
  9.8 8.1 %all-to-all-start = ((bf16[16,24,1792]{2,1,0:T(8,128)(2,1)}), bf16[16,24,1792]{2,1,0:T(8,128)(2,1)S(1)}, u32[]{:S(2)}, u32[]{:S(2)}) async-start(bf16[16,24,1792]{2,1,0:T(8,128)(2,1)} %shard_map.136), calls=%async_computation | async-start | bytes 2752512 | tf_op jit(solution)/shard_map/all_to_all | solution.py:446
  18.6 21.8 %all-to-all-done = bf16[16,24,1792]{2,1,0:T(8,128)(2,1)S(1)} async-done(((bf16[16,24,1792]{2,1,0:T(8,128)(2,1)}), bf16[16,24,1792]{2,1,0:T(8,128)(2,1)S(1)}, u32[]{:S(2)}, u32[]{:S(2)}) %all-to-all-start) | async-done | bytes 1376288 | tf_op jit(solution)/shard_map/all_to_all | solution.py:446
  41.0 1.7 %collective-permute-start.8 = (bf16[6,4224]{1,0:T(8,128)(2,1)S(1)}, bf16[6,4224]{1,0:T(8,128)(2,1)S(1)}, u32[]{:S(2)}, u32[]{:S(2)}) collective-permute-start(bf16[6,4224]{1,0:T(8,128)(2,1)S(1)} %get-tuple-element.39), channel_id=1, source_target_pairs={{96,0},{112,16},{0,32},{16,48},{32,64},{48,80},{64,96},{80,112},{9... | collective-permute-start | bytes 152072 | tf_op jit(solution)/shard_map/ppermute | solution.py:401
  42.7 2.9 %collective-permute-start.7 = (bf16[6,4224]{1,0:T(8,128)(2,1)S(1)}, bf16[6,4224]{1,0:T(8,128)(2,1)S(1)}, u32[]{:S(2)}, u32[]{:S(2)}) collective-permute-start(bf16[6,4224]{1,0:T(8,128)(2,1)S(1)} %get-tuple-element.39), channel_id=1, source_target_pairs={{64,0},{80,16},{96,32},{112,48},{0,64},{16,80},{32,96},{48,112},{6... | collective-permute-start | bytes 152072 | tf_op jit(solution)/shard_map/ppermute | solution.py:401
  45.6 1.3 collective-permute-start.6
  47.3 0.9 reshape.118
  48.2 3.7 %all-to-all-start.1 = ((bf16[16,4,3072]{2,1,0:T(4,128)(2,1)}), bf16[16,4,3072]{2,1,0:T(4,128)(2,1)S(1)}, u32[]{:S(2)}, u32[]{:S(2)}) async-start(bf16[16,4,3072]{2,1,0:T(4,128)(2,1)} %reshape.118), calls=%async_computation.1 | async-start | bytes 786432 | tf_op jit(solution)/shard_map/all_to_all | solution.py:462
  53.1 2.1 %convolution_convert_fusion = bf16[256,4096]{1,0:T(8,128)(2,1)} fusion(bf16[256,24]{1,0:T(8,128)(2,1)S(1)} %convert_element_type.126, bf16[24,4096]{1,0:T(8,128)(2,1)S(1)} %reshape.120), kind=kOutput, calls=%fused_computation | convolution fusion | flops 51380224 | bytes 2306048 | tf_op jit(solution)/shard_map/dot_general | solution.py:19
  55.3 5.7 %all-to-all-done.1 = bf16[16,4,3072]{2,1,0:T(4,128)(2,1)S(1)} async-done(((bf16[16,4,3072]{2,1,0:T(4,128)(2,1)}), bf16[16,4,3072]{2,1,0:T(4,128)(2,1)S(1)}, u32[]{:S(2)}, u32[]{:S(2)}) %all-to-all-start.1) | async-done | bytes 393248 | tf_op jit(solution)/shard_map/all_to_all | solution.py:462
  60.9 3.7 %all-to-all-start.2 = ((bf16[16,16,4096]{2,1,0:T(8,128)(2,1)}), bf16[16,16,4096]{2,1,0:T(8,128)(2,1)S(1)}, u32[]{:S(2)}, u32[]{:S(2)}) async-start(bf16[16,16,4096]{2,1,0:T(8,128)(2,1)} %bitcast.39), calls=%async_computation.2 | async-start | bytes 4194304 | tf_op jit(solution)/shard_map/all_to_all | solution.py:475
  64.7 0.8 reshape.119.refs_0_
  65.5 2.7 %collective-permute-start.4 = (bf16[64,3072]{1,0:T(8,128)(2,1)}, bf16[64,3072]{1,0:T(8,128)(2,1)S(1)}, u32[]{:S(2)}, u32[]{:S(2)}) collective-permute-start(bf16[64,3072]{1,0:T(8,128)(2,1)} %reshape.119.refs_0_), channel_id=1, source_target_pairs={{64,0},{80,16},{96,32},{112,48},{0,64},{16,80},{32,96},{48,112},{6... | collective-permute-start | bytes 1179656 | tf_op jit(solution)/shard_map/ppermute | solution.py:401
  68.3 9.5 %collective-permute-done.3.refs_1_ = bf16[64,3072]{1,0:T(8,128)(2,1)S(1)} collective-permute-done((bf16[64,3072]{1,0:T(8,128)(2,1)}, bf16[64,3072]{1,0:T(8,128)(2,1)S(1)}, u32[]{:S(2)}, u32[]{:S(2)}) %collective-permute-start.3) | collective-permute-done | bytes 393248 | tf_op jit(solution)/shard_map/ppermute | solution.py:401
  77.8 1.5 %collective-permute-done.4.refs_2_ = bf16[64,3072]{1,0:T(8,128)(2,1)S(1)} collective-permute-done((bf16[64,3072]{1,0:T(8,128)(2,1)}, bf16[64,3072]{1,0:T(8,128)(2,1)S(1)}, u32[]{:S(2)}, u32[]{:S(2)}) %collective-permute-start.4) | collective-permute-done | bytes 393248 | tf_op jit(solution)/shard_map/ppermute | solution.py:401
  79.3 4.5 %collective-permute-done.5.refs_3_ = bf16[64,3072]{1,0:T(8,128)(2,1)} collective-permute-done((bf16[64,3072]{1,0:T(8,128)(2,1)}, bf16[64,3072]{1,0:T(8,128)(2,1)}, u32[]{:S(2)}, u32[]{:S(2)}) %collective-permute-start.5) | collective-permute-done | bytes 393248 | tf_op jit(solution)/shard_map/ppermute | solution.py:401
  83.8 5.1 %shard_map.137 = (f32[4,64,512]{2,1,0:T(8,128)}, f32[4,64,512]{2,1,0:T(8,128)}) custom-call(bf16[64,3072]{1,0:T(8,128)(2,1)} %reshape.119.refs_0_, bf16[64,3072]{1,0:T(8,128)(2,1)} %copy-done.3, bf16[64,3072]{1,0:T(8,128)(2,1)} %copy-done.4, bf16[64,3072]{1,0:T(8,128)(2,1)} %collective-permute-done.5.refs_3_, bf16[1,7168,256]{2,1,0:T(8,128)(2,1)} %refs_3_.1, ...), custom_call_target="tpu_custom_call" | custom-call | flops 1610612736 | bytes 7864320 | tf_op jit(solution)/shard_map/pallas_call | solution.py:234
  88.9 3.4 %all-to-all-done.2 = bf16[16,16,4096]{2,1,0:T(8,128)(2,1)S(1)} async-done(((bf16[16,16,4096]{2,1,0:T(8,128)(2,1)}), bf16[16,16,4096]{2,1,0:T(8,128)(2,1)S(1)}, u32[]{:S(2)}, u32[]{:S(2)}) %all-to-all-start.2) | async-done | bytes 2097184 | tf_op jit(solution)/shard_map/all_to_all | solution.py:475
  92.3 1.4 copy-done
  93.7 9.9 %shard_map.138 = (bf16[64,4096]{1,0:T(8,128)(2,1)}, bf16[64,4096]{1,0:T(8,128)(2,1)}, bf16[64,4096]{1,0:T(8,128)(2,1)}, bf16[64,4096]{1,0:T(8,128)(2,1)}, bf16[256,3072]{1,0:T(8,128)(2,1)}) custom-call(f32[4,64,512]{2,1,0:T(8,128)} %get-tuple-element.24.refs_0_, f32[4,64,512]{2,1,0:T(8,128)} %get-tuple-element.25.refs_1_, bf16[256,4096]{1,0:T(8,128)(2,1)} %bitcast.38, ...), custom_call_target="tpu_custom_call" | custom-call | flops 4026531840 | bytes 21495808 | tf_op jit(solution)/shard_map/pallas_call | solution.py:342
  104.4 0.9 collective-permute-start.10
  105.3 1.8 %collective-permute-start.9 = (bf16[64,4096]{1,0:T(8,128)(2,1)}, bf16[64,4096]{1,0:T(8,128)(2,1)}, u32[]{:S(2)}, u32[]{:S(2)}) collective-permute-start(bf16[64,4096]{1,0:T(8,128)(2,1)} %get-tuple-element.29), channel_id=1, source_target_pairs={{32,0},{48,16},{64,32},{80,48},{96,64},{112,80},{0,96},{16,112},{3... | collective-permute-start | bytes 1572872 | tf_op jit(solution)/shard_map/ppermute | solution.py:401
  107.1 4.5 %all-to-all-start.4 = ((bf16[16,16,3072]{2,1,0:T(8,128)(2,1)}), bf16[16,16,3072]{2,1,0:T(8,128)(2,1)S(1)}, u32[]{:S(2)}, u32[]{:S(2)}) async-start(bf16[16,16,3072]{2,1,0:T(8,128)(2,1)} %bitcast.45), calls=%async_computation.4 | async-start | bytes 3145728 | tf_op jit(solution)/shard_map/all_to_all | solution.py:489
  112.2 13.8 %collective-permute-done.11 = bf16[64,4096]{1,0:T(8,128)(2,1)} collective-permute-done((bf16[64,4096]{1,0:T(8,128)(2,1)}, bf16[64,4096]{1,0:T(8,128)(2,1)}, u32[]{:S(2)}, u32[]{:S(2)}) %collective-permute-start.11) | collective-permute-done | bytes 524320 | tf_op jit(solution)/shard_map/ppermute | solution.py:401
  126.6 1.6 %add_convert_fusion = bf16[64,4096]{1,0:T(8,128)(2,1)S(1)} fusion(bf16[64,4096]{1,0:T(8,128)(2,1)} %collective-permute-done.11, bf16[64,4096]{1,0:T(8,128)(2,1)} %collective-permute-done.10, bf16[64,4096]{1,0:T(8,128)(2,1)} %collective-permute-done.9, bf16[64,4096]{1,0:T(8,128)(2,1)S(1)} %copy-done.2), kind=kLoop, calls=%fused_computation.5 | loop fusion | flops 2097152 | bytes 2621440 | tf_op jit(solution)/shard_map/convert_element_type | solution.py:485
  128.2 1.0 reshape.123
  129.2 4.5 %all-to-all-done.4 = bf16[16,16,3072]{2,1,0:T(8,128)(2,1)S(1)} async-done(((bf16[16,16,3072]{2,1,0:T(8,128)(2,1)}), bf16[16,16,3072]{2,1,0:T(8,128)(2,1)S(1)}, u32[]{:S(2)}, u32[]{:S(2)}) %all-to-all-start.4) | async-done | bytes 1572896 | tf_op jit(solution)/shard_map/all_to_all | solution.py:489
  133.7 3.6 %all-to-all-start.3 = ((bf16[16,4,4096]{2,1,0:T(4,128)(2,1)}), bf16[16,4,4096]{2,1,0:T(4,128)(2,1)S(1)}, u32[]{:S(2)}, u32[]{:S(2)}) async-start(bf16[16,4,4096]{2,1,0:T(4,128)(2,1)} %reshape.123), calls=%async_computation.3 | async-start | bytes 1048576 | tf_op jit(solution)/shard_map/all_to_all | solution.py:501
  137.3 0.8 convolution_convert_fusion.2
  138.4 2.5 %collective-permute-start.13 = (bf16[6,3072]{1,0:T(8,128)(2,1)S(1)}, bf16[6,3072]{1,0:T(8,128)(2,1)S(1)}, u32[]{:S(2)}, u32[]{:S(2)}) collective-permute-start(bf16[6,3072]{1,0:T(8,128)(2,1)S(1)} %get-tuple-element.37), channel_id=1, source_target_pairs={{64,0},{80,16},{96,32},{112,48},{0,64},{16,80},{32,96},{48,112},{6... | collective-permute-start | bytes 110600 | tf_op jit(solution)/shard_map/ppermute | solution.py:401
  140.9 1.2 collective-permute-start.12
  142.1 5.3 %all-to-all-done.3 = bf16[16,4,4096]{2,1,0:T(4,128)(2,1)S(1)} async-done(((bf16[16,4,4096]{2,1,0:T(4,128)(2,1)}), bf16[16,4,4096]{2,1,0:T(4,128)(2,1)S(1)}, u32[]{:S(2)}, u32[]{:S(2)}) %all-to-all-start.3) | async-done | bytes 524320 | tf_op jit(solution)/shard_map/all_to_all | solution.py:501
  (75 shorter events, 6.7 us)
Async XLA Ops:
  0.0 40.5 %collective-permute-start = (bf16[1,7168,256]{2,1,0:T(8,128)(2,1)}, bf16[1,7168,256]{2,1,0:T(8,128)(2,1)}, u32[]{:S(2)}, u32[]{:S(2)}) collective-permute-start(bf16[1,7168,256]{2,1,0:T(8,128)(2,1)} %refs_3_.1), channel_id=1, source_target_pairs={{0,16},{16,0},{32,48},{48,32},{64,80},{80,64},{96,112},{112,96},{1... | collective-permute-start | bytes 11010056 | tf_op jit(solution)/shard_map/ppermute | solution.py:448
  0.0 40.5 %collective-permute-start.1 = (bf16[1,7168,256]{2,1,0:T(8,128)(2,1)}, bf16[1,7168,256]{2,1,0:T(8,128)(2,1)}, u32[]{:S(2)}, u32[]{:S(2)}) collective-permute-start(bf16[1,7168,256]{2,1,0:T(8,128)(2,1)} %refs_4_.3), channel_id=1, source_target_pairs={{0,16},{16,0},{32,48},{48,32},{64,80},{80,64},{96,112},{112,96},{1... | collective-permute-start | bytes 11010056 | tf_op jit(solution)/shard_map/ppermute | solution.py:448
  0.5 40.0 %collective-permute-start.2 = (bf16[1,256,7168]{2,1,0:T(8,128)(2,1)}, bf16[1,256,7168]{2,1,0:T(8,128)(2,1)}, u32[]{:S(2)}, u32[]{:S(2)}) collective-permute-start(bf16[1,256,7168]{2,1,0:T(8,128)(2,1)} %refs_5_.5), channel_id=1, source_target_pairs={{0,16},{16,0},{32,48},{48,32},{64,80},{80,64},{96,112},{112,96},{1... | collective-permute-start | bytes 11010056 | tf_op jit(solution)/shard_map/ppermute | solution.py:448
  9.7 8.2 %copy-start.5 = (bf16[7168]{0:T(1024)(128)(2,1)S(1)}, bf16[7168]{0:T(1024)(128)(2,1)}, u32[]{:S(2)}) copy-start(bf16[7168]{0:T(1024)(128)(2,1)} %param.22) | copy-start | bytes 43012
  9.8 8.2 %copy-start.6 = (s32[6,8]{1,0:T(8,128)S(1)}, s32[6,8]{1,0:T(8,128)}, u32[]{:S(2)}) copy-start(s32[6,8]{1,0:T(8,128)} %param.23) | copy-start | bytes 580
  9.8 8.2 %copy-start.7 = (f32[6,8]{1,0:T(8,128)S(1)}, f32[6,8]{1,0:T(8,128)}, u32[]{:S(2)}) copy-start(f32[6,8]{1,0:T(8,128)} %param.24) | copy-start | bytes 580
  9.8 30.9 %copy-start.1 = (bf16[6,7168]{1,0:T(8,128)(2,1)S(1)}, bf16[6,7168]{1,0:T(8,128)(2,1)}, u32[]{:S(2)}) copy-start(bf16[6,7168]{1,0:T(8,128)(2,1)} %param.21) | copy-start | bytes 258052
  9.8 30.7 %all-to-all-start = ((bf16[16,24,1792]{2,1,0:T(8,128)(2,1)}), bf16[16,24,1792]{2,1,0:T(8,128)(2,1)S(1)}, u32[]{:S(2)}, u32[]{:S(2)}) async-start(bf16[16,24,1792]{2,1,0:T(8,128)(2,1)} %shard_map.136), calls=%async_computation | async-start | bytes 2752512 | tf_op jit(solution)/shard_map/all_to_all | solution.py:446
  41.0 10.8 %collective-permute-start.8 = (bf16[6,4224]{1,0:T(8,128)(2,1)S(1)}, bf16[6,4224]{1,0:T(8,128)(2,1)S(1)}, u32[]{:S(2)}, u32[]{:S(2)}) collective-permute-start(bf16[6,4224]{1,0:T(8,128)(2,1)S(1)} %get-tuple-element.39), channel_id=1, source_target_pairs={{96,0},{112,16},{0,32},{16,48},{32,64},{48,80},{64,96},{80,112},{9... | collective-permute-start | bytes 152072 | tf_op jit(solution)/shard_map/ppermute | solution.py:401
  42.7 9.1 %collective-permute-start.7 = (bf16[6,4224]{1,0:T(8,128)(2,1)S(1)}, bf16[6,4224]{1,0:T(8,128)(2,1)S(1)}, u32[]{:S(2)}, u32[]{:S(2)}) collective-permute-start(bf16[6,4224]{1,0:T(8,128)(2,1)S(1)} %get-tuple-element.39), channel_id=1, source_target_pairs={{64,0},{80,16},{96,32},{112,48},{0,64},{16,80},{32,96},{48,112},{6... | collective-permute-start | bytes 152072 | tf_op jit(solution)/shard_map/ppermute | solution.py:401
  45.6 6.2 %collective-permute-start.6 = (bf16[6,4224]{1,0:T(8,128)(2,1)S(1)}, bf16[6,4224]{1,0:T(8,128)(2,1)S(1)}, u32[]{:S(2)}, u32[]{:S(2)}) collective-permute-start(bf16[6,4224]{1,0:T(8,128)(2,1)S(1)} %get-tuple-element.39), channel_id=1, source_target_pairs={{32,0},{48,16},{64,32},{80,48},{96,64},{112,80},{0,96},{16,112},{3... | collective-permute-start | bytes 152072 | tf_op jit(solution)/shard_map/ppermute | solution.py:401
  48.2 12.8 %all-to-all-start.1 = ((bf16[16,4,3072]{2,1,0:T(4,128)(2,1)}), bf16[16,4,3072]{2,1,0:T(4,128)(2,1)S(1)}, u32[]{:S(2)}, u32[]{:S(2)}) async-start(bf16[16,4,3072]{2,1,0:T(4,128)(2,1)} %reshape.118), calls=%async_computation.1 | async-start | bytes 786432 | tf_op jit(solution)/shard_map/all_to_all | solution.py:462
  60.9 31.4 %all-to-all-start.2 = ((bf16[16,16,4096]{2,1,0:T(8,128)(2,1)}), bf16[16,16,4096]{2,1,0:T(8,128)(2,1)S(1)}, u32[]{:S(2)}, u32[]{:S(2)}) async-start(bf16[16,16,4096]{2,1,0:T(8,128)(2,1)} %bitcast.39), calls=%async_computation.2 | async-start | bytes 4194304 | tf_op jit(solution)/shard_map/all_to_all | solution.py:475
  65.5 12.3 %collective-permute-start.3 = (bf16[64,3072]{1,0:T(8,128)(2,1)}, bf16[64,3072]{1,0:T(8,128)(2,1)S(1)}, u32[]{:S(2)}, u32[]{:S(2)}) collective-permute-start(bf16[64,3072]{1,0:T(8,128)(2,1)} %reshape.119.refs_0_), channel_id=1, source_target_pairs={{32,0},{48,16},{64,32},{80,48},{96,64},{112,80},{0,96},{16,112},{3... | collective-permute-start | bytes 1179656 | tf_op jit(solution)/shard_map/ppermute | solution.py:401
  65.5 13.8 %collective-permute-start.4 = (bf16[64,3072]{1,0:T(8,128)(2,1)}, bf16[64,3072]{1,0:T(8,128)(2,1)S(1)}, u32[]{:S(2)}, u32[]{:S(2)}) collective-permute-start(bf16[64,3072]{1,0:T(8,128)(2,1)} %reshape.119.refs_0_), channel_id=1, source_target_pairs={{64,0},{80,16},{96,32},{112,48},{0,64},{16,80},{32,96},{48,112},{6... | collective-permute-start | bytes 1179656 | tf_op jit(solution)/shard_map/ppermute | solution.py:401
  68.3 15.5 %collective-permute-start.5 = (bf16[64,3072]{1,0:T(8,128)(2,1)}, bf16[64,3072]{1,0:T(8,128)(2,1)}, u32[]{:S(2)}, u32[]{:S(2)}) collective-permute-start(bf16[64,3072]{1,0:T(8,128)(2,1)} %reshape.119.refs_0_), channel_id=1, source_target_pairs={{96,0},{112,16},{0,32},{16,48},{32,64},{48,80},{64,96},{80,112},{9... | collective-permute-start | bytes 1179656 | tf_op jit(solution)/shard_map/ppermute | solution.py:401
  77.8 6.0 %copy-start.3 = (bf16[64,3072]{1,0:T(8,128)(2,1)}, bf16[64,3072]{1,0:T(8,128)(2,1)S(1)}, u32[]{:S(2)}) copy-start(bf16[64,3072]{1,0:T(8,128)(2,1)S(1)} %collective-permute-done.3.refs_1_) | copy-start | bytes 1179652
  79.3 4.5 %copy-start.4 = (bf16[64,3072]{1,0:T(8,128)(2,1)}, bf16[64,3072]{1,0:T(8,128)(2,1)S(1)}, u32[]{:S(2)}) copy-start(bf16[64,3072]{1,0:T(8,128)(2,1)S(1)} %collective-permute-done.4.refs_2_) | copy-start | bytes 1179652
  92.3 1.4 copy-start
  103.6 23.0 %copy-start.2 = (bf16[64,4096]{1,0:T(8,128)(2,1)S(1)}, bf16[64,4096]{1,0:T(8,128)(2,1)}, u32[]{:S(2)}) copy-start(bf16[64,4096]{1,0:T(8,128)(2,1)} %get-tuple-element.28) | copy-start | bytes 1572868
  103.6 22.4 %collective-permute-start.11 = (bf16[64,4096]{1,0:T(8,128)(2,1)}, bf16[64,4096]{1,0:T(8,128)(2,1)}, u32[]{:S(2)}, u32[]{:S(2)}) collective-permute-start(bf16[64,4096]{1,0:T(8,128)(2,1)} %get-tuple-element.31), channel_id=1, source_target_pairs={{96,0},{112,16},{0,32},{16,48},{32,64},{48,80},{64,96},{80,112},{9... | collective-permute-start | bytes 1572872 | tf_op jit(solution)/shard_map/ppermute | solution.py:401
  104.4 21.6 %collective-permute-start.10 = (bf16[64,4096]{1,0:T(8,128)(2,1)}, bf16[64,4096]{1,0:T(8,128)(2,1)}, u32[]{:S(2)}, u32[]{:S(2)}) collective-permute-start(bf16[64,4096]{1,0:T(8,128)(2,1)} %get-tuple-element.30), channel_id=1, source_target_pairs={{64,0},{80,16},{96,32},{112,48},{0,64},{16,80},{32,96},{48,112},{6... | collective-permute-start | bytes 1572872 | tf_op jit(solution)/shard_map/ppermute | solution.py:401
  105.3 21.3 %collective-permute-start.9 = (bf16[64,4096]{1,0:T(8,128)(2,1)}, bf16[64,4096]{1,0:T(8,128)(2,1)}, u32[]{:S(2)}, u32[]{:S(2)}) collective-permute-start(bf16[64,4096]{1,0:T(8,128)(2,1)} %get-tuple-element.29), channel_id=1, source_target_pairs={{32,0},{48,16},{64,32},{80,48},{96,64},{112,80},{0,96},{16,112},{3... | collective-permute-start | bytes 1572872 | tf_op jit(solution)/shard_map/ppermute | solution.py:401
  107.1 26.6 %all-to-all-start.4 = ((bf16[16,16,3072]{2,1,0:T(8,128)(2,1)}), bf16[16,16,3072]{2,1,0:T(8,128)(2,1)S(1)}, u32[]{:S(2)}, u32[]{:S(2)}) async-start(bf16[16,16,3072]{2,1,0:T(8,128)(2,1)} %bitcast.45), calls=%async_computation.4 | async-start | bytes 3145728 | tf_op jit(solution)/shard_map/all_to_all | solution.py:489
  133.7 13.6 %all-to-all-start.3 = ((bf16[16,4,4096]{2,1,0:T(4,128)(2,1)}), bf16[16,4,4096]{2,1,0:T(4,128)(2,1)S(1)}, u32[]{:S(2)}, u32[]{:S(2)}) async-start(bf16[16,4,4096]{2,1,0:T(4,128)(2,1)} %reshape.123), calls=%async_computation.3 | async-start | bytes 1048576 | tf_op jit(solution)/shard_map/all_to_all | solution.py:501
  138.1 9.8 %collective-permute-start.14 = (bf16[6,3072]{1,0:T(8,128)(2,1)S(1)}, bf16[6,3072]{1,0:T(8,128)(2,1)S(1)}, u32[]{:S(2)}, u32[]{:S(2)}) collective-permute-start(bf16[6,3072]{1,0:T(8,128)(2,1)S(1)} %get-tuple-element.36), channel_id=1, source_target_pairs={{96,0},{112,16},{0,32},{16,48},{32,64},{48,80},{64,96},{80,112},{9... | collective-permute-start | bytes 110600 | tf_op jit(solution)/shard_map/ppermute | solution.py:401
  138.4 9.6 %collective-permute-start.13 = (bf16[6,3072]{1,0:T(8,128)(2,1)S(1)}, bf16[6,3072]{1,0:T(8,128)(2,1)S(1)}, u32[]{:S(2)}, u32[]{:S(2)}) collective-permute-start(bf16[6,3072]{1,0:T(8,128)(2,1)S(1)} %get-tuple-element.37), channel_id=1, source_target_pairs={{64,0},{80,16},{96,32},{112,48},{0,64},{16,80},{32,96},{48,112},{6... | collective-permute-start | bytes 110600 | tf_op jit(solution)/shard_map/ppermute | solution.py:401
  140.9 7.1 %collective-permute-start.12 = (bf16[6,3072]{1,0:T(8,128)(2,1)S(1)}, bf16[6,3072]{1,0:T(8,128)(2,1)S(1)}, u32[]{:S(2)}, u32[]{:S(2)}) collective-permute-start(bf16[6,3072]{1,0:T(8,128)(2,1)S(1)} %get-tuple-element.35), channel_id=1, source_target_pairs={{32,0},{48,16},{64,32},{80,48},{96,64},{112,80},{0,96},{16,112},{3... | collective-permute-start | bytes 110600 | tf_op jit(solution)/shard_map/ppermute | solution.py:401

commit v7 on v6

--- a/solution.py
+++ b/solution.py
@@ -171,7 +171,7 @@
             pltpu.VMEM(value_up.shape, BF16),
             pltpu.SemaphoreType.DMA((STEPS + 1 + parts,)),
         ],
-        compiler_params=pltpu.CompilerParams(vmem_limit_bytes=60 << 20),
+        compiler_params=pltpu.CompilerParams(vmem_limit_bytes=62 << 20),
         cost_estimate=pl.CostEstimate(
             flops=4 * rows * heads * positions * depth * GROUP + 2 * rows * size * width,
             bytes_accessed=2 * rows * positions * depth + 2 * size * width,
@@ -243,7 +243,7 @@
             pltpu.SemaphoreType.DMA((INNER, planes)),
             pltpu.SemaphoreType.DMA((INNER, 2 * sides)),
         ],
-        compiler_params=pltpu.CompilerParams(vmem_limit_bytes=60 << 20),
+        compiler_params=pltpu.CompilerParams(vmem_limit_bytes=62 << 20),
         cost_estimate=pl.CostEstimate(
             flops=4 * planes * block * depth * hidden,
             bytes_accessed=2 * planes * block * depth + 4 * depth * hidden,
@@ -361,7 +361,7 @@
             pltpu.SemaphoreType.DMA((INNER + 1, 2 * sides)),
             pltpu.SemaphoreType.DMA((planes + 1,)),
         ],
-        compiler_params=pltpu.CompilerParams(vmem_limit_bytes=60 << 20),
+        compiler_params=pltpu.CompilerParams(vmem_limit_bytes=62 << 20),
         cost_estimate=pl.CostEstimate(
             flops=4 * count * rest * hidden + 2 * count * width * hidden,
             bytes_accessed=2 * count * (width + rest) + (4 * rest + 2 * width) * hidden,

time: 149 us -> 148 us (level)
  no operation moved by 1% of the time
where the time goes in v7:
time: 148 us; the launch traced here: 147 us
  waiting for transfers between devices  69.4 us (47%)
  starting transfers between devices  41.4 us (28%)
  Pallas kernels  24.2 us (16%)
  local copies, waits for them, and re-layouts  4.22 us (3%)
  other arithmetic  3.78 us (3%)
  matrix products  3.63 us (2%)
    ppermute x12, waiting for transfers between devices, from_plane(): return lax.ppermute(v, 'attn', pairs)  28.5 us
    all_to_all x1, waiting for transfers between devices, local(): lax.all_to_all(pieces, 'ffn', split_axis=0, concat_axis=0, tiled=True)  21.8 us
    ppermute x12, starting transfers between devices, from_plane(): return lax.ppermute(v, 'attn', pairs)  16.6 us
    all_to_all x2, waiting for transfers between devices, local(): lax.all_to_all(outgoing, 'ffn', split_axis=0, concat_axis=0, tiled=True)  10 us
    pallas_call x1, Pallas kernels, expert(): pl.pallas_call(lambda *refs: expert_kernel(planes, sides, *refs), out_sha...  9.88 us
    pallas_call x1, Pallas kernels, attend(): pl.pallas_call(lambda *refs: attend_kernel(scale, owners, parts, *refs),...  9.22 us
    all_to_all x1, starting transfers between devices, local(): lax.all_to_all(pieces, 'ffn', split_axis=0, concat_axis=0, tiled=True)  8.1 us
    all_to_all x2, starting transfers between devices, local(): lax.all_to_all(outgoing, 'ffn', split_axis=0, concat_axis=0, tiled=True)  8.08 us
  transfers between devices with their start and end apart: 20, of which 10 were waited for; matrix products, arithmetic and copies ran while one was open for 7% of the time, Pallas kernels for 10%

profile of v7, /device:TPU:0, one launch (start us, length us, event | category | flops | bytes accessed | tf_op | source)
XLA Modules:
  0.0 147.1 jit_solution(18188352939957982631)
XLA Ops:
  0.5 9.2 %shard_map.136 = bf16[16,24,1792]{2,1,0:T(8,128)(2,1)} custom-call(s32[96]{0:T(128)} %refs_0_.1, bf16[96,4,512]{2,1,0:T(4,128)(2,1)} %refs_1_.1, bf16[96,64,512]{2,1,0:T(8,128)(2,1)} %refs_2_.1, bf16[4,64,96]{2,1,0:T(8,128)(2,1)} %bitcast.52, bf16[64,64,96]{2,1,0:T(8,128)(2,1)} %bitcast.44, bf16[4,512,128]{2,1,0:T(8,128)(2,1)} %refs_5_.3, ...), custom_call_target="tpu_custom_call" | custom-call | flops 905969664 | bytes 13631488 | tf_op jit(solution)/shard_map/pallas_call | solution.py:152
  9.8 8.1 %all-to-all-start = ((bf16[16,24,1792]{2,1,0:T(8,128)(2,1)}), bf16[16,24,1792]{2,1,0:T(8,128)(2,1)S(1)}, u32[]{:S(2)}, u32[]{:S(2)}) async-start(bf16[16,24,1792]{2,1,0:T(8,128)(2,1)} %shard_map.136), calls=%async_computation | async-start | bytes 2752512 | tf_op jit(solution)/shard_map/all_to_all | solution.py:446
  18.6 21.8 %all-to-all-done = bf16[16,24,1792]{2,1,0:T(8,128)(2,1)S(1)} async-done(((bf16[16,24,1792]{2,1,0:T(8,128)(2,1)}), bf16[16,24,1792]{2,1,0:T(8,128)(2,1)S(1)}, u32[]{:S(2)}, u32[]{:S(2)}) %all-to-all-start) | async-done | bytes 1376288 | tf_op jit(solution)/shard_map/all_to_all | solution.py:446
  41.0 1.7 %collective-permute-start.8 = (bf16[6,4224]{1,0:T(8,128)(2,1)S(1)}, bf16[6,4224]{1,0:T(8,128)(2,1)S(1)}, u32[]{:S(2)}, u32[]{:S(2)}) collective-permute-start(bf16[6,4224]{1,0:T(8,128)(2,1)S(1)} %get-tuple-element.39), channel_id=1, source_target_pairs={{96,0},{112,16},{0,32},{16,48},{32,64},{48,80},{64,96},{80,112},{9... | collective-permute-start | bytes 152072 | tf_op jit(solution)/shard_map/ppermute | solution.py:401
  42.7 2.9 %collective-permute-start.7 = (bf16[6,4224]{1,0:T(8,128)(2,1)S(1)}, bf16[6,4224]{1,0:T(8,128)(2,1)S(1)}, u32[]{:S(2)}, u32[]{:S(2)}) collective-permute-start(bf16[6,4224]{1,0:T(8,128)(2,1)S(1)} %get-tuple-element.39), channel_id=1, source_target_pairs={{64,0},{80,16},{96,32},{112,48},{0,64},{16,80},{32,96},{48,112},{6... | collective-permute-start | bytes 152072 | tf_op jit(solution)/shard_map/ppermute | solution.py:401
  45.6 1.3 collective-permute-start.6
  47.3 0.9 reshape.118
  48.1 3.7 %all-to-all-start.1 = ((bf16[16,4,3072]{2,1,0:T(4,128)(2,1)}), bf16[16,4,3072]{2,1,0:T(4,128)(2,1)S(1)}, u32[]{:S(2)}, u32[]{:S(2)}) async-start(bf16[16,4,3072]{2,1,0:T(4,128)(2,1)} %reshape.118), calls=%async_computation.1 | async-start | bytes 786432 | tf_op jit(solution)/shard_map/all_to_all | solution.py:462
  53.1 2.0 %convolution_convert_fusion = bf16[256,4096]{1,0:T(8,128)(2,1)} fusion(bf16[256,24]{1,0:T(8,128)(2,1)S(1)} %convert_element_type.126, bf16[24,4096]{1,0:T(8,128)(2,1)S(1)} %reshape.120), kind=kOutput, calls=%fused_computation | convolution fusion | flops 51380224 | bytes 2306048 | tf_op jit(solution)/shard_map/dot_general | solution.py:19
  55.1 5.8 %all-to-all-done.1 = bf16[16,4,3072]{2,1,0:T(4,128)(2,1)S(1)} async-done(((bf16[16,4,3072]{2,1,0:T(4,128)(2,1)}), bf16[16,4,3072]{2,1,0:T(4,128)(2,1)S(1)}, u32[]{:S(2)}, u32[]{:S(2)}) %all-to-all-start.1) | async-done | bytes 393248 | tf_op jit(solution)/shard_map/all_to_all | solution.py:462
  60.9 4.4 %all-to-all-start.2 = ((bf16[16,16,4096]{2,1,0:T(8,128)(2,1)}), bf16[16,16,4096]{2,1,0:T(8,128)(2,1)}, u32[]{:S(2)}, u32[]{:S(2)}) async-start(bf16[16,16,4096]{2,1,0:T(8,128)(2,1)} %bitcast.14), calls=%async_computation.2 | async-start | bytes 4194304 | tf_op jit(solution)/shard_map/all_to_all | solution.py:475
  65.6 2.7 %collective-permute-start.4 = (bf16[64,3072]{1,0:T(8,128)(2,1)S(1)}, bf16[64,3072]{1,0:T(8,128)(2,1)S(1)}, u32[]{:S(2)}, u32[]{:S(2)}) collective-permute-start(bf16[64,3072]{1,0:T(8,128)(2,1)S(1)} %reshape.119.refs_0_), channel_id=1, source_target_pairs={{64,0},{80,16},{96,32},{112,48},{0,64},{16,80},{32,96},{48,112},{6... | collective-permute-start | bytes 1179656 | tf_op jit(solution)/shard_map/ppermute | solution.py:401
  68.3 9.3 %collective-permute-done.3.refs_1_ = bf16[64,3072]{1,0:T(8,128)(2,1)S(1)} collective-permute-done((bf16[64,3072]{1,0:T(8,128)(2,1)S(1)}, bf16[64,3072]{1,0:T(8,128)(2,1)S(1)}, u32[]{:S(2)}, u32[]{:S(2)}) %collective-permute-start.3) | collective-permute-done | bytes 393248 | tf_op jit(solution)/shard_map/ppermute | solution.py:401
  77.6 1.6 %collective-permute-done.4.refs_2_ = bf16[64,3072]{1,0:T(8,128)(2,1)S(1)} collective-permute-done((bf16[64,3072]{1,0:T(8,128)(2,1)S(1)}, bf16[64,3072]{1,0:T(8,128)(2,1)S(1)}, u32[]{:S(2)}, u32[]{:S(2)}) %collective-permute-start.4) | collective-permute-done | bytes 393248 | tf_op jit(solution)/shard_map/ppermute | solution.py:401
  79.2 0.8 copy-done.4
  80.0 3.8 %collective-permute-done.5.refs_3_ = bf16[64,3072]{1,0:T(8,128)(2,1)} collective-permute-done((bf16[64,3072]{1,0:T(8,128)(2,1)S(1)}, bf16[64,3072]{1,0:T(8,128)(2,1)}, u32[]{:S(2)}, u32[]{:S(2)}) %collective-permute-start.5) | collective-permute-done | bytes 393248 | tf_op jit(solution)/shard_map/ppermute | solution.py:401
  83.7 5.1 %shard_map.137 = (f32[4,64,512]{2,1,0:T(8,128)}, f32[4,64,512]{2,1,0:T(8,128)}) custom-call(bf16[64,3072]{1,0:T(8,128)(2,1)} %copy-done, bf16[64,3072]{1,0:T(8,128)(2,1)} %copy-done.3, bf16[64,3072]{1,0:T(8,128)(2,1)} %copy-done.4, bf16[64,3072]{1,0:T(8,128)(2,1)} %collective-permute-done.5.refs_3_, bf16[1,7168,256]{2,1,0:T(8,128)(2,1)} %refs_3_.1, ...), custom_call_target="tpu_custom_call" | custom-call | flops 1610612736 | bytes 7864320 | tf_op jit(solution)/shard_map/pallas_call | solution.py:234
  88.8 4.2 %all-to-all-done.2 = bf16[16,16,4096]{2,1,0:T(8,128)(2,1)} async-done(((bf16[16,16,4096]{2,1,0:T(8,128)(2,1)}), bf16[16,16,4096]{2,1,0:T(8,128)(2,1)}, u32[]{:S(2)}, u32[]{:S(2)}) %all-to-all-start.2) | async-done | bytes 2097184 | tf_op jit(solution)/shard_map/all_to_all | solution.py:475
  93.0 9.9 %shard_map.138 = (bf16[64,4096]{1,0:T(8,128)(2,1)}, bf16[64,4096]{1,0:T(8,128)(2,1)}, bf16[64,4096]{1,0:T(8,128)(2,1)}, bf16[64,4096]{1,0:T(8,128)(2,1)}, bf16[256,3072]{1,0:T(8,128)(2,1)}) custom-call(f32[4,64,512]{2,1,0:T(8,128)} %get-tuple-element.24.refs_0_, f32[4,64,512]{2,1,0:T(8,128)} %get-tuple-element.25.refs_1_, ...), custom_call_target="tpu_custom_call" | custom-call | flops 4026531840 | bytes 21495808 | tf_op jit(solution)/shard_map/pallas_call | solution.py:342
  102.9 0.7 collective-permute-start.11
  103.7 0.9 collective-permute-start.10
  104.6 1.9 %collective-permute-start.9 = (bf16[64,4096]{1,0:T(8,128)(2,1)}, bf16[64,4096]{1,0:T(8,128)(2,1)}, u32[]{:S(2)}, u32[]{:S(2)}) collective-permute-start(bf16[64,4096]{1,0:T(8,128)(2,1)} %get-tuple-element.29), channel_id=1, source_target_pairs={{32,0},{48,16},{64,32},{80,48},{96,64},{112,80},{0,96},{16,112},{3... | collective-permute-start | bytes 1572872 | tf_op jit(solution)/shard_map/ppermute | solution.py:401
  106.4 4.3 %all-to-all-start.4 = ((bf16[16,16,3072]{2,1,0:T(8,128)(2,1)}), bf16[16,16,3072]{2,1,0:T(8,128)(2,1)S(1)}, u32[]{:S(2)}, u32[]{:S(2)}) async-start(bf16[16,16,3072]{2,1,0:T(8,128)(2,1)} %bitcast.43), calls=%async_computation.4 | async-start | bytes 3145728 | tf_op jit(solution)/shard_map/all_to_all | solution.py:489
  111.3 13.3 %collective-permute-done.11 = bf16[64,4096]{1,0:T(8,128)(2,1)} collective-permute-done((bf16[64,4096]{1,0:T(8,128)(2,1)}, bf16[64,4096]{1,0:T(8,128)(2,1)}, u32[]{:S(2)}, u32[]{:S(2)}) %collective-permute-start.11) | collective-permute-done | bytes 524320 | tf_op jit(solution)/shard_map/ppermute | solution.py:401
  125.1 1.6 %add_convert_fusion = bf16[64,4096]{1,0:T(8,128)(2,1)S(1)} fusion(bf16[64,4096]{1,0:T(8,128)(2,1)} %collective-permute-done.11, bf16[64,4096]{1,0:T(8,128)(2,1)} %collective-permute-done.10, bf16[64,4096]{1,0:T(8,128)(2,1)} %collective-permute-done.9, bf16[64,4096]{1,0:T(8,128)(2,1)S(1)} %copy-done.2), kind=kLoop, calls=%fused_computation.5 | loop fusion | flops 2097152 | bytes 2621440 | tf_op jit(solution)/shard_map/convert_element_type | solution.py:485
  126.7 1.0 reshape.123
  127.7 4.2 %all-to-all-done.4 = bf16[16,16,3072]{2,1,0:T(8,128)(2,1)S(1)} async-done(((bf16[16,16,3072]{2,1,0:T(8,128)(2,1)}), bf16[16,16,3072]{2,1,0:T(8,128)(2,1)S(1)}, u32[]{:S(2)}, u32[]{:S(2)}) %all-to-all-start.4) | async-done | bytes 1572896 | tf_op jit(solution)/shard_map/all_to_all | solution.py:489
  131.9 3.8 %all-to-all-start.3 = ((bf16[16,4,4096]{2,1,0:T(4,128)(2,1)}), bf16[16,4,4096]{2,1,0:T(4,128)(2,1)S(1)}, u32[]{:S(2)}, u32[]{:S(2)}) async-start(bf16[16,4,4096]{2,1,0:T(4,128)(2,1)} %reshape.123), calls=%async_computation.3 | async-start | bytes 1048576 | tf_op jit(solution)/shard_map/all_to_all | solution.py:501
  135.7 0.8 convolution_convert_fusion.2
  136.8 2.6 %collective-permute-start.13 = (bf16[6,3072]{1,0:T(8,128)(2,1)S(1)}, bf16[6,3072]{1,0:T(8,128)(2,1)S(1)}, u32[]{:S(2)}, u32[]{:S(2)}) collective-permute-start(bf16[6,3072]{1,0:T(8,128)(2,1)S(1)} %get-tuple-element.37), channel_id=1, source_target_pairs={{64,0},{80,16},{96,32},{112,48},{0,64},{16,80},{32,96},{48,112},{6... | collective-permute-start | bytes 110600 | tf_op jit(solution)/shard_map/ppermute | solution.py:401
  139.4 1.5 %collective-permute-start.12 = (bf16[6,3072]{1,0:T(8,128)(2,1)S(1)}, bf16[6,3072]{1,0:T(8,128)(2,1)S(1)}, u32[]{:S(2)}, u32[]{:S(2)}) collective-permute-start(bf16[6,3072]{1,0:T(8,128)(2,1)S(1)} %get-tuple-element.35), channel_id=1, source_target_pairs={{32,0},{48,16},{64,32},{80,48},{96,64},{112,80},{0,96},{16,112},{3... | collective-permute-start | bytes 110600 | tf_op jit(solution)/shard_map/ppermute | solution.py:401
  140.9 4.9 %all-to-all-done.3 = bf16[16,4,4096]{2,1,0:T(4,128)(2,1)S(1)} async-done(((bf16[16,4,4096]{2,1,0:T(4,128)(2,1)}), bf16[16,4,4096]{2,1,0:T(4,128)(2,1)S(1)}, u32[]{:S(2)}, u32[]{:S(2)}) %all-to-all-start.3) | async-done | bytes 524320 | tf_op jit(solution)/shard_map/all_to_all | solution.py:501
  (75 shorter events, 6.1 us)
Async XLA Ops:
  0.0 40.5 %collective-permute-start = (bf16[1,7168,256]{2,1,0:T(8,128)(2,1)}, bf16[1,7168,256]{2,1,0:T(8,128)(2,1)}, u32[]{:S(2)}, u32[]{:S(2)}) collective-permute-start(bf16[1,7168,256]{2,1,0:T(8,128)(2,1)} %refs_3_.1), channel_id=1, source_target_pairs={{0,16},{16,0},{32,48},{48,32},{64,80},{80,64},{96,112},{112,96},{1... | collective-permute-start | bytes 11010056 | tf_op jit(solution)/shard_map/ppermute | solution.py:448
  0.0 40.5 %collective-permute-start.1 = (bf16[1,7168,256]{2,1,0:T(8,128)(2,1)}, bf16[1,7168,256]{2,1,0:T(8,128)(2,1)}, u32[]{:S(2)}, u32[]{:S(2)}) collective-permute-start(bf16[1,7168,256]{2,1,0:T(8,128)(2,1)} %refs_4_.3), channel_id=1, source_target_pairs={{0,16},{16,0},{32,48},{48,32},{64,80},{80,64},{96,112},{112,96},{1... | collective-permute-start | bytes 11010056 | tf_op jit(solution)/shard_map/ppermute | solution.py:448
  0.5 40.0 %collective-permute-start.2 = (bf16[1,256,7168]{2,1,0:T(8,128)(2,1)}, bf16[1,256,7168]{2,1,0:T(8,128)(2,1)}, u32[]{:S(2)}, u32[]{:S(2)}) collective-permute-start(bf16[1,256,7168]{2,1,0:T(8,128)(2,1)} %refs_5_.5), channel_id=1, source_target_pairs={{0,16},{16,0},{32,48},{48,32},{64,80},{80,64},{96,112},{112,96},{1... | collective-permute-start | bytes 11010056 | tf_op jit(solution)/shard_map/ppermute | solution.py:448
  9.7 8.2 %copy-start.5 = (bf16[7168]{0:T(1024)(128)(2,1)S(1)}, bf16[7168]{0:T(1024)(128)(2,1)}, u32[]{:S(2)}) copy-start(bf16[7168]{0:T(1024)(128)(2,1)} %param.22) | copy-start | bytes 43012
  9.8 8.2 %copy-start.6 = (s32[6,8]{1,0:T(8,128)S(1)}, s32[6,8]{1,0:T(8,128)}, u32[]{:S(2)}) copy-start(s32[6,8]{1,0:T(8,128)} %param.23) | copy-start | bytes 580
  9.8 8.2 %copy-start.7 = (f32[6,8]{1,0:T(8,128)S(1)}, f32[6,8]{1,0:T(8,128)}, u32[]{:S(2)}) copy-start(f32[6,8]{1,0:T(8,128)} %param.24) | copy-start | bytes 580
  9.8 30.9 %copy-start.1 = (bf16[6,7168]{1,0:T(8,128)(2,1)S(1)}, bf16[6,7168]{1,0:T(8,128)(2,1)}, u32[]{:S(2)}) copy-start(bf16[6,7168]{1,0:T(8,128)(2,1)} %param.21) | copy-start | bytes 258052
  9.8 30.7 %all-to-all-start = ((bf16[16,24,1792]{2,1,0:T(8,128)(2,1)}), bf16[16,24,1792]{2,1,0:T(8,128)(2,1)S(1)}, u32[]{:S(2)}, u32[]{:S(2)}) async-start(bf16[16,24,1792]{2,1,0:T(8,128)(2,1)} %shard_map.136), calls=%async_computation | async-start | bytes 2752512 | tf_op jit(solution)/shard_map/all_to_all | solution.py:446
  41.0 10.8 %collective-permute-start.8 = (bf16[6,4224]{1,0:T(8,128)(2,1)S(1)}, bf16[6,4224]{1,0:T(8,128)(2,1)S(1)}, u32[]{:S(2)}, u32[]{:S(2)}) collective-permute-start(bf16[6,4224]{1,0:T(8,128)(2,1)S(1)} %get-tuple-element.39), channel_id=1, source_target_pairs={{96,0},{112,16},{0,32},{16,48},{32,64},{48,80},{64,96},{80,112},{9... | collective-permute-start | bytes 152072 | tf_op jit(solution)/shard_map/ppermute | solution.py:401
  42.7 9.1 %collective-permute-start.7 = (bf16[6,4224]{1,0:T(8,128)(2,1)S(1)}, bf16[6,4224]{1,0:T(8,128)(2,1)S(1)}, u32[]{:S(2)}, u32[]{:S(2)}) collective-permute-start(bf16[6,4224]{1,0:T(8,128)(2,1)S(1)} %get-tuple-element.39), channel_id=1, source_target_pairs={{64,0},{80,16},{96,32},{112,48},{0,64},{16,80},{32,96},{48,112},{6... | collective-permute-start | bytes 152072 | tf_op jit(solution)/shard_map/ppermute | solution.py:401
  45.6 6.2 %collective-permute-start.6 = (bf16[6,4224]{1,0:T(8,128)(2,1)S(1)}, bf16[6,4224]{1,0:T(8,128)(2,1)S(1)}, u32[]{:S(2)}, u32[]{:S(2)}) collective-permute-start(bf16[6,4224]{1,0:T(8,128)(2,1)S(1)} %get-tuple-element.39), channel_id=1, source_target_pairs={{32,0},{48,16},{64,32},{80,48},{96,64},{112,80},{0,96},{16,112},{3... | collective-permute-start | bytes 152072 | tf_op jit(solution)/shard_map/ppermute | solution.py:401
  48.1 12.8 %all-to-all-start.1 = ((bf16[16,4,3072]{2,1,0:T(4,128)(2,1)}), bf16[16,4,3072]{2,1,0:T(4,128)(2,1)S(1)}, u32[]{:S(2)}, u32[]{:S(2)}) async-start(bf16[16,4,3072]{2,1,0:T(4,128)(2,1)} %reshape.118), calls=%async_computation.1 | async-start | bytes 786432 | tf_op jit(solution)/shard_map/all_to_all | solution.py:462
  60.9 32.1 %all-to-all-start.2 = ((bf16[16,16,4096]{2,1,0:T(8,128)(2,1)}), bf16[16,16,4096]{2,1,0:T(8,128)(2,1)}, u32[]{:S(2)}, u32[]{:S(2)}) async-start(bf16[16,16,4096]{2,1,0:T(8,128)(2,1)} %bitcast.14), calls=%async_computation.2 | async-start | bytes 4194304 | tf_op jit(solution)/shard_map/all_to_all | solution.py:475
  65.5 18.2 %copy-start = (bf16[64,3072]{1,0:T(8,128)(2,1)}, bf16[64,3072]{1,0:T(8,128)(2,1)S(1)}, u32[]{:S(2)}) copy-start(bf16[64,3072]{1,0:T(8,128)(2,1)S(1)} %reshape.119.refs_0_) | copy-start | bytes 1179652
  65.5 12.1 %collective-permute-start.3 = (bf16[64,3072]{1,0:T(8,128)(2,1)S(1)}, bf16[64,3072]{1,0:T(8,128)(2,1)S(1)}, u32[]{:S(2)}, u32[]{:S(2)}) collective-permute-start(bf16[64,3072]{1,0:T(8,128)(2,1)S(1)} %reshape.119.refs_0_), channel_id=1, source_target_pairs={{32,0},{48,16},{64,32},{80,48},{96,64},{112,80},{0,96},{16,112},{3... | collective-permute-start | bytes 1179656 | tf_op jit(solution)/shard_map/ppermute | solution.py:401
  65.6 13.6 %collective-permute-start.4 = (bf16[64,3072]{1,0:T(8,128)(2,1)S(1)}, bf16[64,3072]{1,0:T(8,128)(2,1)S(1)}, u32[]{:S(2)}, u32[]{:S(2)}) collective-permute-start(bf16[64,3072]{1,0:T(8,128)(2,1)S(1)} %reshape.119.refs_0_), channel_id=1, source_target_pairs={{64,0},{80,16},{96,32},{112,48},{0,64},{16,80},{32,96},{48,112},{6... | collective-permute-start | bytes 1179656 | tf_op jit(solution)/shard_map/ppermute | solution.py:401
  68.3 15.4 %collective-permute-start.5 = (bf16[64,3072]{1,0:T(8,128)(2,1)S(1)}, bf16[64,3072]{1,0:T(8,128)(2,1)}, u32[]{:S(2)}, u32[]{:S(2)}) collective-permute-start(bf16[64,3072]{1,0:T(8,128)(2,1)S(1)} %reshape.119.refs_0_), channel_id=1, source_target_pairs={{96,0},{112,16},{0,32},{16,48},{32,64},{48,80},{64,96},{80,112},{9... | collective-permute-start | bytes 1179656 | tf_op jit(solution)/shard_map/ppermute | solution.py:401
  77.6 6.1 %copy-start.3 = (bf16[64,3072]{1,0:T(8,128)(2,1)}, bf16[64,3072]{1,0:T(8,128)(2,1)S(1)}, u32[]{:S(2)}) copy-start(bf16[64,3072]{1,0:T(8,128)(2,1)S(1)} %collective-permute-done.3.refs_1_) | copy-start | bytes 1179652
  79.2 0.8 copy-start.4
  102.9 22.2 %copy-start.2 = (bf16[64,4096]{1,0:T(8,128)(2,1)S(1)}, bf16[64,4096]{1,0:T(8,128)(2,1)}, u32[]{:S(2)}) copy-start(bf16[64,4096]{1,0:T(8,128)(2,1)} %get-tuple-element.28) | copy-start | bytes 1572868
  102.9 21.6 %collective-permute-start.11 = (bf16[64,4096]{1,0:T(8,128)(2,1)}, bf16[64,4096]{1,0:T(8,128)(2,1)}, u32[]{:S(2)}, u32[]{:S(2)}) collective-permute-start(bf16[64,4096]{1,0:T(8,128)(2,1)} %get-tuple-element.31), channel_id=1, source_target_pairs={{96,0},{112,16},{0,32},{16,48},{32,64},{48,80},{64,96},{80,112},{9... | collective-permute-start | bytes 1572872 | tf_op jit(solution)/shard_map/ppermute | solution.py:401
  103.7 20.8 %collective-permute-start.10 = (bf16[64,4096]{1,0:T(8,128)(2,1)}, bf16[64,4096]{1,0:T(8,128)(2,1)}, u32[]{:S(2)}, u32[]{:S(2)}) collective-permute-start(bf16[64,4096]{1,0:T(8,128)(2,1)} %get-tuple-element.30), channel_id=1, source_target_pairs={{64,0},{80,16},{96,32},{112,48},{0,64},{16,80},{32,96},{48,112},{6... | collective-permute-start | bytes 1572872 | tf_op jit(solution)/shard_map/ppermute | solution.py:401
  104.6 20.5 %collective-permute-start.9 = (bf16[64,4096]{1,0:T(8,128)(2,1)}, bf16[64,4096]{1,0:T(8,128)(2,1)}, u32[]{:S(2)}, u32[]{:S(2)}) collective-permute-start(bf16[64,4096]{1,0:T(8,128)(2,1)} %get-tuple-element.29), channel_id=1, source_target_pairs={{32,0},{48,16},{64,32},{80,48},{96,64},{112,80},{0,96},{16,112},{3... | collective-permute-start | bytes 1572872 | tf_op jit(solution)/shard_map/ppermute | solution.py:401
  106.4 25.5 %all-to-all-start.4 = ((bf16[16,16,3072]{2,1,0:T(8,128)(2,1)}), bf16[16,16,3072]{2,1,0:T(8,128)(2,1)S(1)}, u32[]{:S(2)}, u32[]{:S(2)}) async-start(bf16[16,16,3072]{2,1,0:T(8,128)(2,1)} %bitcast.43), calls=%async_computation.4 | async-start | bytes 3145728 | tf_op jit(solution)/shard_map/all_to_all | solution.py:489
  131.9 13.9 %all-to-all-start.3 = ((bf16[16,4,4096]{2,1,0:T(4,128)(2,1)}), bf16[16,4,4096]{2,1,0:T(4,128)(2,1)S(1)}, u32[]{:S(2)}, u32[]{:S(2)}) async-start(bf16[16,4,4096]{2,1,0:T(4,128)(2,1)} %reshape.123), calls=%async_computation.3 | async-start | bytes 1048576 | tf_op jit(solution)/shard_map/all_to_all | solution.py:501
  136.5 9.9 %collective-permute-start.14 = (bf16[6,3072]{1,0:T(8,128)(2,1)S(1)}, bf16[6,3072]{1,0:T(8,128)(2,1)S(1)}, u32[]{:S(2)}, u32[]{:S(2)}) collective-permute-start(bf16[6,3072]{1,0:T(8,128)(2,1)S(1)} %get-tuple-element.36), channel_id=1, source_target_pairs={{96,0},{112,16},{0,32},{16,48},{32,64},{48,80},{64,96},{80,112},{9... | collective-permute-start | bytes 110600 | tf_op jit(solution)/shard_map/ppermute | solution.py:401
  136.8 9.6 %collective-permute-start.13 = (bf16[6,3072]{1,0:T(8,128)(2,1)S(1)}, bf16[6,3072]{1,0:T(8,128)(2,1)S(1)}, u32[]{:S(2)}, u32[]{:S(2)}) collective-permute-start(bf16[6,3072]{1,0:T(8,128)(2,1)S(1)} %get-tuple-element.37), channel_id=1, source_target_pairs={{64,0},{80,16},{96,32},{112,48},{0,64},{16,80},{32,96},{48,112},{6... | collective-permute-start | bytes 110600 | tf_op jit(solution)/shard_map/ppermute | solution.py:401
  139.4 7.0 %collective-permute-start.12 = (bf16[6,3072]{1,0:T(8,128)(2,1)S(1)}, bf16[6,3072]{1,0:T(8,128)(2,1)S(1)}, u32[]{:S(2)}, u32[]{:S(2)}) collective-permute-start(bf16[6,3072]{1,0:T(8,128)(2,1)S(1)} %get-tuple-element.35), channel_id=1, source_target_pairs={{32,0},{48,16},{64,32},{80,48},{96,64},{112,80},{0,96},{16,112},{3... | collective-permute-start | bytes 110600 | tf_op jit(solution)/shard_map/ppermute | solution.py:401

commit v8 on v7

--- a/solution.py
+++ b/solution.py
@@ -171,7 +171,7 @@
             pltpu.VMEM(value_up.shape, BF16),
             pltpu.SemaphoreType.DMA((STEPS + 1 + parts,)),
         ],
-        compiler_params=pltpu.CompilerParams(vmem_limit_bytes=62 << 20),
+        compiler_params=pltpu.CompilerParams(vmem_limit_bytes=63 << 20),
         cost_estimate=pl.CostEstimate(
             flops=4 * rows * heads * positions * depth * GROUP + 2 * rows * size * width,
             bytes_accessed=2 * rows * positions * depth + 2 * size * width,
@@ -243,7 +243,7 @@
             pltpu.SemaphoreType.DMA((INNER, planes)),
             pltpu.SemaphoreType.DMA((INNER, 2 * sides)),
         ],
-        compiler_params=pltpu.CompilerParams(vmem_limit_bytes=62 << 20),
+        compiler_params=pltpu.CompilerParams(vmem_limit_bytes=63 << 20),
         cost_estimate=pl.CostEstimate(
             flops=4 * planes * block * depth * hidden,
             bytes_accessed=2 * planes * block * depth + 4 * depth * hidden,
@@ -361,7 +361,7 @@
             pltpu.SemaphoreType.DMA((INNER + 1, 2 * sides)),
             pltpu.SemaphoreType.DMA((planes + 1,)),
         ],
-        compiler_params=pltpu.CompilerParams(vmem_limit_bytes=62 << 20),
+        compiler_params=pltpu.CompilerParams(vmem_limit_bytes=63 << 20),
         cost_estimate=pl.CostEstimate(
             flops=4 * count * rest * hidden + 2 * count * width * hidden,
             bytes_accessed=2 * count * (width + rest) + (4 * rest + 2 * width) * hidden,

time: 148 us -> 148 us (level)
  no operation moved by 1% of the time
where the time goes in v8:
time: 148 us; the launch traced here: 147 us
  waiting for transfers between devices  69.2 us (47%)
  starting transfers between devices  41.4 us (28%)
  Pallas kernels  24.2 us (16%)
  local copies, waits for them, and re-layouts  4.3 us (3%)
  other arithmetic  3.95 us (3%)
  matrix products  3.63 us (2%)
    ppermute x12, waiting for transfers between devices, from_plane(): return lax.ppermute(v, 'attn', pairs)  28.5 us
    all_to_all x1, waiting for transfers between devices, local(): lax.all_to_all(pieces, 'ffn', split_axis=0, concat_axis=0, tiled=True)  21.8 us
    ppermute x12, starting transfers between devices, from_plane(): return lax.ppermute(v, 'attn', pairs)  16.6 us
    all_to_all x2, waiting for transfers between devices, local(): lax.all_to_all(outgoing, 'ffn', split_axis=0, concat_axis=0, tiled=True)  10 us
    pallas_call x1, Pallas kernels, expert(): pl.pallas_call(lambda *refs: expert_kernel(planes, sides, *refs), out_sha...  9.88 us
    pallas_call x1, Pallas kernels, attend(): pl.pallas_call(lambda *refs: attend_kernel(scale, owners, parts, *refs),...  9.22 us
    all_to_all x1, starting transfers between devices, local(): lax.all_to_all(pieces, 'ffn', split_axis=0, concat_axis=0, tiled=True)  8.1 us
    all_to_all x2, starting transfers between devices, local(): lax.all_to_all(outgoing, 'ffn', split_axis=0, concat_axis=0, tiled=True)  8.08 us
  transfers between devices with their start and end apart: 20, of which 10 were waited for; matrix products, arithmetic and copies ran while one was open for 7% of the time, Pallas kernels for 10%

profile of v8, /device:TPU:0, one launch (start us, length us, event | category | flops | bytes accessed | tf_op | source)
XLA Modules:
  0.0 147.1 jit_solution(7331268073278994314)
XLA Ops:
  0.5 9.2 %shard_map.136 = bf16[16,24,1792]{2,1,0:T(8,128)(2,1)} custom-call(s32[96]{0:T(128)} %refs_0_.1, bf16[96,4,512]{2,1,0:T(4,128)(2,1)} %refs_1_.1, bf16[96,64,512]{2,1,0:T(8,128)(2,1)} %refs_2_.1, bf16[4,64,96]{2,1,0:T(8,128)(2,1)} %bitcast.52, bf16[64,64,96]{2,1,0:T(8,128)(2,1)} %bitcast.44, bf16[4,512,128]{2,1,0:T(8,128)(2,1)} %refs_5_.3, ...), custom_call_target="tpu_custom_call" | custom-call | flops 905969664 | bytes 13631488 | tf_op jit(solution)/shard_map/pallas_call | solution.py:152
  9.8 8.1 %all-to-all-start = ((bf16[16,24,1792]{2,1,0:T(8,128)(2,1)}), bf16[16,24,1792]{2,1,0:T(8,128)(2,1)S(1)}, u32[]{:S(2)}, u32[]{:S(2)}) async-start(bf16[16,24,1792]{2,1,0:T(8,128)(2,1)} %shard_map.136), calls=%async_computation | async-start | bytes 2752512 | tf_op jit(solution)/shard_map/all_to_all | solution.py:446
  18.6 21.8 %all-to-all-done = bf16[16,24,1792]{2,1,0:T(8,128)(2,1)S(1)} async-done(((bf16[16,24,1792]{2,1,0:T(8,128)(2,1)}), bf16[16,24,1792]{2,1,0:T(8,128)(2,1)S(1)}, u32[]{:S(2)}, u32[]{:S(2)}) %all-to-all-start) | async-done | bytes 1376288 | tf_op jit(solution)/shard_map/all_to_all | solution.py:446
  41.0 1.7 %collective-permute-start.8 = (bf16[6,4224]{1,0:T(8,128)(2,1)S(1)}, bf16[6,4224]{1,0:T(8,128)(2,1)S(1)}, u32[]{:S(2)}, u32[]{:S(2)}) collective-permute-start(bf16[6,4224]{1,0:T(8,128)(2,1)S(1)} %get-tuple-element.39), channel_id=1, source_target_pairs={{96,0},{112,16},{0,32},{16,48},{32,64},{48,80},{64,96},{80,112},{9... | collective-permute-start | bytes 152072 | tf_op jit(solution)/shard_map/ppermute | solution.py:401
  42.7 2.9 %collective-permute-start.7 = (bf16[6,4224]{1,0:T(8,128)(2,1)S(1)}, bf16[6,4224]{1,0:T(8,128)(2,1)S(1)}, u32[]{:S(2)}, u32[]{:S(2)}) collective-permute-start(bf16[6,4224]{1,0:T(8,128)(2,1)S(1)} %get-tuple-element.39), channel_id=1, source_target_pairs={{64,0},{80,16},{96,32},{112,48},{0,64},{16,80},{32,96},{48,112},{6... | collective-permute-start | bytes 152072 | tf_op jit(solution)/shard_map/ppermute | solution.py:401
  45.6 1.3 collective-permute-start.6
  47.3 0.9 reshape.118
  48.1 3.7 %all-to-all-start.1 = ((bf16[16,4,3072]{2,1,0:T(4,128)(2,1)}), bf16[16,4,3072]{2,1,0:T(4,128)(2,1)S(1)}, u32[]{:S(2)}, u32[]{:S(2)}) async-start(bf16[16,4,3072]{2,1,0:T(4,128)(2,1)} %reshape.118), calls=%async_computation.1 | async-start | bytes 786432 | tf_op jit(solution)/shard_map/all_to_all | solution.py:462
  53.1 2.0 %convolution_convert_fusion = bf16[256,4096]{1,0:T(8,128)(2,1)} fusion(bf16[256,24]{1,0:T(8,128)(2,1)S(1)} %convert_element_type.126, bf16[24,4096]{1,0:T(8,128)(2,1)S(1)} %reshape.120), kind=kOutput, calls=%fused_computation | convolution fusion | flops 51380224 | bytes 2306048 | tf_op jit(solution)/shard_map/dot_general | solution.py:19
  55.1 5.8 %all-to-all-done.1 = bf16[16,4,3072]{2,1,0:T(4,128)(2,1)S(1)} async-done(((bf16[16,4,3072]{2,1,0:T(4,128)(2,1)}), bf16[16,4,3072]{2,1,0:T(4,128)(2,1)S(1)}, u32[]{:S(2)}, u32[]{:S(2)}) %all-to-all-start.1) | async-done | bytes 393248 | tf_op jit(solution)/shard_map/all_to_all | solution.py:462
  60.9 4.4 %all-to-all-start.2 = ((bf16[16,16,4096]{2,1,0:T(8,128)(2,1)}), bf16[16,16,4096]{2,1,0:T(8,128)(2,1)}, u32[]{:S(2)}, u32[]{:S(2)}) async-start(bf16[16,16,4096]{2,1,0:T(8,128)(2,1)} %bitcast.14), calls=%async_computation.2 | async-start | bytes 4194304 | tf_op jit(solution)/shard_map/all_to_all | solution.py:475
  65.6 2.7 %collective-permute-start.4 = (bf16[64,3072]{1,0:T(8,128)(2,1)S(1)}, bf16[64,3072]{1,0:T(8,128)(2,1)S(1)}, u32[]{:S(2)}, u32[]{:S(2)}) collective-permute-start(bf16[64,3072]{1,0:T(8,128)(2,1)S(1)} %reshape.119.refs_0_), channel_id=1, source_target_pairs={{64,0},{80,16},{96,32},{112,48},{0,64},{16,80},{32,96},{48,112},{6... | collective-permute-start | bytes 1179656 | tf_op jit(solution)/shard_map/ppermute | solution.py:401
  68.3 9.3 %collective-permute-done.3.refs_1_ = bf16[64,3072]{1,0:T(8,128)(2,1)S(1)} collective-permute-done((bf16[64,3072]{1,0:T(8,128)(2,1)S(1)}, bf16[64,3072]{1,0:T(8,128)(2,1)S(1)}, u32[]{:S(2)}, u32[]{:S(2)}) %collective-permute-start.3) | collective-permute-done | bytes 393248 | tf_op jit(solution)/shard_map/ppermute | solution.py:401
  77.6 1.6 %collective-permute-done.4.refs_2_ = bf16[64,3072]{1,0:T(8,128)(2,1)S(1)} collective-permute-done((bf16[64,3072]{1,0:T(8,128)(2,1)S(1)}, bf16[64,3072]{1,0:T(8,128)(2,1)S(1)}, u32[]{:S(2)}, u32[]{:S(2)}) %collective-permute-start.4) | collective-permute-done | bytes 393248 | tf_op jit(solution)/shard_map/ppermute | solution.py:401
  79.2 0.8 copy-done.4
  80.0 3.8 %collective-permute-done.5.refs_3_ = bf16[64,3072]{1,0:T(8,128)(2,1)} collective-permute-done((bf16[64,3072]{1,0:T(8,128)(2,1)S(1)}, bf16[64,3072]{1,0:T(8,128)(2,1)}, u32[]{:S(2)}, u32[]{:S(2)}) %collective-permute-start.5) | collective-permute-done | bytes 393248 | tf_op jit(solution)/shard_map/ppermute | solution.py:401
  83.7 5.1 %shard_map.137 = (f32[4,64,512]{2,1,0:T(8,128)}, f32[4,64,512]{2,1,0:T(8,128)}) custom-call(bf16[64,3072]{1,0:T(8,128)(2,1)} %copy-done, bf16[64,3072]{1,0:T(8,128)(2,1)} %copy-done.3, bf16[64,3072]{1,0:T(8,128)(2,1)} %copy-done.4, bf16[64,3072]{1,0:T(8,128)(2,1)} %collective-permute-done.5.refs_3_, bf16[1,7168,256]{2,1,0:T(8,128)(2,1)} %refs_3_.1, ...), custom_call_target="tpu_custom_call" | custom-call | flops 1610612736 | bytes 7864320 | tf_op jit(solution)/shard_map/pallas_call | solution.py:234
  88.8 4.2 %all-to-all-done.2 = bf16[16,16,4096]{2,1,0:T(8,128)(2,1)} async-done(((bf16[16,16,4096]{2,1,0:T(8,128)(2,1)}), bf16[16,16,4096]{2,1,0:T(8,128)(2,1)}, u32[]{:S(2)}, u32[]{:S(2)}) %all-to-all-start.2) | async-done | bytes 2097184 | tf_op jit(solution)/shard_map/all_to_all | solution.py:475
  93.0 9.9 %shard_map.138 = (bf16[64,4096]{1,0:T(8,128)(2,1)}, bf16[64,4096]{1,0:T(8,128)(2,1)}, bf16[64,4096]{1,0:T(8,128)(2,1)}, bf16[64,4096]{1,0:T(8,128)(2,1)}, bf16[256,3072]{1,0:T(8,128)(2,1)}) custom-call(f32[4,64,512]{2,1,0:T(8,128)} %get-tuple-element.24.refs_0_, f32[4,64,512]{2,1,0:T(8,128)} %get-tuple-element.25.refs_1_, ...), custom_call_target="tpu_custom_call" | custom-call | flops 4026531840 | bytes 21495808 | tf_op jit(solution)/shard_map/pallas_call | solution.py:342
  102.9 0.7 collective-permute-start.11
  103.7 0.9 collective-permute-start.10
  104.6 1.9 %collective-permute-start.9 = (bf16[64,4096]{1,0:T(8,128)(2,1)}, bf16[64,4096]{1,0:T(8,128)(2,1)}, u32[]{:S(2)}, u32[]{:S(2)}) collective-permute-start(bf16[64,4096]{1,0:T(8,128)(2,1)} %get-tuple-element.29), channel_id=1, source_target_pairs={{32,0},{48,16},{64,32},{80,48},{96,64},{112,80},{0,96},{16,112},{3... | collective-permute-start | bytes 1572872 | tf_op jit(solution)/shard_map/ppermute | solution.py:401
  106.4 4.3 %all-to-all-start.4 = ((bf16[16,16,3072]{2,1,0:T(8,128)(2,1)}), bf16[16,16,3072]{2,1,0:T(8,128)(2,1)S(1)}, u32[]{:S(2)}, u32[]{:S(2)}) async-start(bf16[16,16,3072]{2,1,0:T(8,128)(2,1)} %bitcast.43), calls=%async_computation.4 | async-start | bytes 3145728 | tf_op jit(solution)/shard_map/all_to_all | solution.py:489
  111.2 13.1 %collective-permute-done.11 = bf16[64,4096]{1,0:T(8,128)(2,1)S(1)} collective-permute-done((bf16[64,4096]{1,0:T(8,128)(2,1)}, bf16[64,4096]{1,0:T(8,128)(2,1)S(1)}, u32[]{:S(2)}, u32[]{:S(2)}) %collective-permute-start.11) | collective-permute-done | bytes 524320 | tf_op jit(solution)/shard_map/ppermute | solution.py:401
  125.2 1.8 %add_convert_fusion = bf16[64,4096]{1,0:T(8,128)(2,1)S(1)} fusion(bf16[64,4096]{1,0:T(8,128)(2,1)} %copy-done.2, bf16[64,4096]{1,0:T(8,128)(2,1)} %collective-permute-done.10, bf16[64,4096]{1,0:T(8,128)(2,1)} %collective-permute-done.9, bf16[64,4096]{1,0:T(8,128)(2,1)} %get-tuple-element.28), kind=kLoop, calls=%fused_computation.5 | loop fusion | flops 2097152 | bytes 2621440 | tf_op jit(solution)/shard_map/convert_element_type | solution.py:485
  127.0 1.0 reshape.123
  128.0 3.9 %all-to-all-done.4 = bf16[16,16,3072]{2,1,0:T(8,128)(2,1)S(1)} async-done(((bf16[16,16,3072]{2,1,0:T(8,128)(2,1)}), bf16[16,16,3072]{2,1,0:T(8,128)(2,1)S(1)}, u32[]{:S(2)}, u32[]{:S(2)}) %all-to-all-start.4) | async-done | bytes 1572896 | tf_op jit(solution)/shard_map/all_to_all | solution.py:489
  131.9 3.8 %all-to-all-start.3 = ((bf16[16,4,4096]{2,1,0:T(4,128)(2,1)}), bf16[16,4,4096]{2,1,0:T(4,128)(2,1)S(1)}, u32[]{:S(2)}, u32[]{:S(2)}) async-start(bf16[16,4,4096]{2,1,0:T(4,128)(2,1)} %reshape.123), calls=%async_computation.3 | async-start | bytes 1048576 | tf_op jit(solution)/shard_map/all_to_all | solution.py:501
  135.7 0.8 convolution_convert_fusion.2
  136.9 2.6 %collective-permute-start.13 = (bf16[6,3072]{1,0:T(8,128)(2,1)S(1)}, bf16[6,3072]{1,0:T(8,128)(2,1)S(1)}, u32[]{:S(2)}, u32[]{:S(2)}) collective-permute-start(bf16[6,3072]{1,0:T(8,128)(2,1)S(1)} %get-tuple-element.37), channel_id=1, source_target_pairs={{64,0},{80,16},{96,32},{112,48},{0,64},{16,80},{32,96},{48,112},{6... | collective-permute-start | bytes 110600 | tf_op jit(solution)/shard_map/ppermute | solution.py:401
  139.5 1.4 collective-permute-start.12
  140.9 4.9 %all-to-all-done.3 = bf16[16,4,4096]{2,1,0:T(4,128)(2,1)S(1)} async-done(((bf16[16,4,4096]{2,1,0:T(4,128)(2,1)}), bf16[16,4,4096]{2,1,0:T(4,128)(2,1)S(1)}, u32[]{:S(2)}, u32[]{:S(2)}) %all-to-all-start.3) | async-done | bytes 524320 | tf_op jit(solution)/shard_map/all_to_all | solution.py:501
  (75 shorter events, 6.5 us)
Async XLA Ops:
  0.0 40.5 %collective-permute-start = (bf16[1,7168,256]{2,1,0:T(8,128)(2,1)}, bf16[1,7168,256]{2,1,0:T(8,128)(2,1)}, u32[]{:S(2)}, u32[]{:S(2)}) collective-permute-start(bf16[1,7168,256]{2,1,0:T(8,128)(2,1)} %refs_3_.1), channel_id=1, source_target_pairs={{0,16},{16,0},{32,48},{48,32},{64,80},{80,64},{96,112},{112,96},{1... | collective-permute-start | bytes 11010056 | tf_op jit(solution)/shard_map/ppermute | solution.py:448
  0.0 40.5 %collective-permute-start.1 = (bf16[1,7168,256]{2,1,0:T(8,128)(2,1)}, bf16[1,7168,256]{2,1,0:T(8,128)(2,1)}, u32[]{:S(2)}, u32[]{:S(2)}) collective-permute-start(bf16[1,7168,256]{2,1,0:T(8,128)(2,1)} %refs_4_.3), channel_id=1, source_target_pairs={{0,16},{16,0},{32,48},{48,32},{64,80},{80,64},{96,112},{112,96},{1... | collective-permute-start | bytes 11010056 | tf_op jit(solution)/shard_map/ppermute | solution.py:448
  0.5 40.0 %collective-permute-start.2 = (bf16[1,256,7168]{2,1,0:T(8,128)(2,1)}, bf16[1,256,7168]{2,1,0:T(8,128)(2,1)}, u32[]{:S(2)}, u32[]{:S(2)}) collective-permute-start(bf16[1,256,7168]{2,1,0:T(8,128)(2,1)} %refs_5_.5), channel_id=1, source_target_pairs={{0,16},{16,0},{32,48},{48,32},{64,80},{80,64},{96,112},{112,96},{1... | collective-permute-start | bytes 11010056 | tf_op jit(solution)/shard_map/ppermute | solution.py:448
  9.7 8.2 %copy-start.5 = (bf16[7168]{0:T(1024)(128)(2,1)S(1)}, bf16[7168]{0:T(1024)(128)(2,1)}, u32[]{:S(2)}) copy-start(bf16[7168]{0:T(1024)(128)(2,1)} %param.22) | copy-start | bytes 43012
  9.8 8.2 %copy-start.6 = (s32[6,8]{1,0:T(8,128)S(1)}, s32[6,8]{1,0:T(8,128)}, u32[]{:S(2)}) copy-start(s32[6,8]{1,0:T(8,128)} %param.23) | copy-start | bytes 580
  9.8 8.2 %copy-start.7 = (f32[6,8]{1,0:T(8,128)S(1)}, f32[6,8]{1,0:T(8,128)}, u32[]{:S(2)}) copy-start(f32[6,8]{1,0:T(8,128)} %param.24) | copy-start | bytes 580
  9.8 30.9 %copy-start.1 = (bf16[6,7168]{1,0:T(8,128)(2,1)S(1)}, bf16[6,7168]{1,0:T(8,128)(2,1)}, u32[]{:S(2)}) copy-start(bf16[6,7168]{1,0:T(8,128)(2,1)} %param.21) | copy-start | bytes 258052
  9.8 30.7 %all-to-all-start = ((bf16[16,24,1792]{2,1,0:T(8,128)(2,1)}), bf16[16,24,1792]{2,1,0:T(8,128)(2,1)S(1)}, u32[]{:S(2)}, u32[]{:S(2)}) async-start(bf16[16,24,1792]{2,1,0:T(8,128)(2,1)} %shard_map.136), calls=%async_computation | async-start | bytes 2752512 | tf_op jit(solution)/shard_map/all_to_all | solution.py:446
  41.0 10.8 %collective-permute-start.8 = (bf16[6,4224]{1,0:T(8,128)(2,1)S(1)}, bf16[6,4224]{1,0:T(8,128)(2,1)S(1)}, u32[]{:S(2)}, u32[]{:S(2)}) collective-permute-start(bf16[6,4224]{1,0:T(8,128)(2,1)S(1)} %get-tuple-element.39), channel_id=1, source_target_pairs={{96,0},{112,16},{0,32},{16,48},{32,64},{48,80},{64,96},{80,112},{9... | collective-permute-start | bytes 152072 | tf_op jit(solution)/shard_map/ppermute | solution.py:401
  42.7 9.1 %collective-permute-start.7 = (bf16[6,4224]{1,0:T(8,128)(2,1)S(1)}, bf16[6,4224]{1,0:T(8,128)(2,1)S(1)}, u32[]{:S(2)}, u32[]{:S(2)}) collective-permute-start(bf16[6,4224]{1,0:T(8,128)(2,1)S(1)} %get-tuple-element.39), channel_id=1, source_target_pairs={{64,0},{80,16},{96,32},{112,48},{0,64},{16,80},{32,96},{48,112},{6... | collective-permute-start | bytes 152072 | tf_op jit(solution)/shard_map/ppermute | solution.py:401
  45.6 6.2 %collective-permute-start.6 = (bf16[6,4224]{1,0:T(8,128)(2,1)S(1)}, bf16[6,4224]{1,0:T(8,128)(2,1)S(1)}, u32[]{:S(2)}, u32[]{:S(2)}) collective-permute-start(bf16[6,4224]{1,0:T(8,128)(2,1)S(1)} %get-tuple-element.39), channel_id=1, source_target_pairs={{32,0},{48,16},{64,32},{80,48},{96,64},{112,80},{0,96},{16,112},{3... | collective-permute-start | bytes 152072 | tf_op jit(solution)/shard_map/ppermute | solution.py:401
  48.1 12.8 %all-to-all-start.1 = ((bf16[16,4,3072]{2,1,0:T(4,128)(2,1)}), bf16[16,4,3072]{2,1,0:T(4,128)(2,1)S(1)}, u32[]{:S(2)}, u32[]{:S(2)}) async-start(bf16[16,4,3072]{2,1,0:T(4,128)(2,1)} %reshape.118), calls=%async_computation.1 | async-start | bytes 786432 | tf_op jit(solution)/shard_map/all_to_all | solution.py:462
  60.9 32.1 %all-to-all-start.2 = ((bf16[16,16,4096]{2,1,0:T(8,128)(2,1)}), bf16[16,16,4096]{2,1,0:T(8,128)(2,1)}, u32[]{:S(2)}, u32[]{:S(2)}) async-start(bf16[16,16,4096]{2,1,0:T(8,128)(2,1)} %bitcast.14), calls=%async_computation.2 | async-start | bytes 4194304 | tf_op jit(solution)/shard_map/all_to_all | solution.py:475
  65.5 2.8 %copy-start = (bf16[64,3072]{1,0:T(8,128)(2,1)}, bf16[64,3072]{1,0:T(8,128)(2,1)S(1)}, u32[]{:S(2)}) copy-start(bf16[64,3072]{1,0:T(8,128)(2,1)S(1)} %reshape.119.refs_0_) | copy-start | bytes 1179652
  65.5 12.1 %collective-permute-start.3 = (bf16[64,3072]{1,0:T(8,128)(2,1)S(1)}, bf16[64,3072]{1,0:T(8,128)(2,1)S(1)}, u32[]{:S(2)}, u32[]{:S(2)}) collective-permute-start(bf16[64,3072]{1,0:T(8,128)(2,1)S(1)} %reshape.119.refs_0_), channel_id=1, source_target_pairs={{32,0},{48,16},{64,32},{80,48},{96,64},{112,80},{0,96},{16,112},{3... | collective-permute-start | bytes 1179656 | tf_op jit(solution)/shard_map/ppermute | solution.py:401
  65.6 13.6 %collective-permute-start.4 = (bf16[64,3072]{1,0:T(8,128)(2,1)S(1)}, bf16[64,3072]{1,0:T(8,128)(2,1)S(1)}, u32[]{:S(2)}, u32[]{:S(2)}) collective-permute-start(bf16[64,3072]{1,0:T(8,128)(2,1)S(1)} %reshape.119.refs_0_), channel_id=1, source_target_pairs={{64,0},{80,16},{96,32},{112,48},{0,64},{16,80},{32,96},{48,112},{6... | collective-permute-start | bytes 1179656 | tf_op jit(solution)/shard_map/ppermute | solution.py:401
  68.3 15.4 %collective-permute-start.5 = (bf16[64,3072]{1,0:T(8,128)(2,1)S(1)}, bf16[64,3072]{1,0:T(8,128)(2,1)}, u32[]{:S(2)}, u32[]{:S(2)}) collective-permute-start(bf16[64,3072]{1,0:T(8,128)(2,1)S(1)} %reshape.119.refs_0_), channel_id=1, source_target_pairs={{96,0},{112,16},{0,32},{16,48},{32,64},{48,80},{64,96},{80,112},{9... | collective-permute-start | bytes 1179656 | tf_op jit(solution)/shard_map/ppermute | solution.py:401
  77.6 1.6 %copy-start.3 = (bf16[64,3072]{1,0:T(8,128)(2,1)}, bf16[64,3072]{1,0:T(8,128)(2,1)S(1)}, u32[]{:S(2)}) copy-start(bf16[64,3072]{1,0:T(8,128)(2,1)S(1)} %collective-permute-done.3.refs_1_) | copy-start | bytes 1179652
  79.2 0.8 copy-start.4
  102.9 21.5 %collective-permute-start.11 = (bf16[64,4096]{1,0:T(8,128)(2,1)}, bf16[64,4096]{1,0:T(8,128)(2,1)S(1)}, u32[]{:S(2)}, u32[]{:S(2)}) collective-permute-start(bf16[64,4096]{1,0:T(8,128)(2,1)} %get-tuple-element.31), channel_id=1, source_target_pairs={{96,0},{112,16},{0,32},{16,48},{32,64},{48,80},{64,96},{80,112},{9... | collective-permute-start | bytes 1572872 | tf_op jit(solution)/shard_map/ppermute | solution.py:401
  103.7 20.7 %collective-permute-start.10 = (bf16[64,4096]{1,0:T(8,128)(2,1)}, bf16[64,4096]{1,0:T(8,128)(2,1)}, u32[]{:S(2)}, u32[]{:S(2)}) collective-permute-start(bf16[64,4096]{1,0:T(8,128)(2,1)} %get-tuple-element.30), channel_id=1, source_target_pairs={{64,0},{80,16},{96,32},{112,48},{0,64},{16,80},{32,96},{48,112},{6... | collective-permute-start | bytes 1572872 | tf_op jit(solution)/shard_map/ppermute | solution.py:401
  104.6 20.5 %collective-permute-start.9 = (bf16[64,4096]{1,0:T(8,128)(2,1)}, bf16[64,4096]{1,0:T(8,128)(2,1)}, u32[]{:S(2)}, u32[]{:S(2)}) collective-permute-start(bf16[64,4096]{1,0:T(8,128)(2,1)} %get-tuple-element.29), channel_id=1, source_target_pairs={{32,0},{48,16},{64,32},{80,48},{96,64},{112,80},{0,96},{16,112},{3... | collective-permute-start | bytes 1572872 | tf_op jit(solution)/shard_map/ppermute | solution.py:401
  106.4 25.5 %all-to-all-start.4 = ((bf16[16,16,3072]{2,1,0:T(8,128)(2,1)}), bf16[16,16,3072]{2,1,0:T(8,128)(2,1)S(1)}, u32[]{:S(2)}, u32[]{:S(2)}) async-start(bf16[16,16,3072]{2,1,0:T(8,128)(2,1)} %bitcast.43), calls=%async_computation.4 | async-start | bytes 3145728 | tf_op jit(solution)/shard_map/all_to_all | solution.py:489
  124.4 0.8 copy-start.2
  131.9 13.9 %all-to-all-start.3 = ((bf16[16,4,4096]{2,1,0:T(4,128)(2,1)}), bf16[16,4,4096]{2,1,0:T(4,128)(2,1)S(1)}, u32[]{:S(2)}, u32[]{:S(2)}) async-start(bf16[16,4,4096]{2,1,0:T(4,128)(2,1)} %reshape.123), calls=%async_computation.3 | async-start | bytes 1048576 | tf_op jit(solution)/shard_map/all_to_all | solution.py:501
  136.5 9.9 %collective-permute-start.14 = (bf16[6,3072]{1,0:T(8,128)(2,1)S(1)}, bf16[6,3072]{1,0:T(8,128)(2,1)S(1)}, u32[]{:S(2)}, u32[]{:S(2)}) collective-permute-start(bf16[6,3072]{1,0:T(8,128)(2,1)S(1)} %get-tuple-element.36), channel_id=1, source_target_pairs={{96,0},{112,16},{0,32},{16,48},{32,64},{48,80},{64,96},{80,112},{9... | collective-permute-start | bytes 110600 | tf_op jit(solution)/shard_map/ppermute | solution.py:401
  136.9 9.4 %collective-permute-start.13 = (bf16[6,3072]{1,0:T(8,128)(2,1)S(1)}, bf16[6,3072]{1,0:T(8,128)(2,1)S(1)}, u32[]{:S(2)}, u32[]{:S(2)}) collective-permute-start(bf16[6,3072]{1,0:T(8,128)(2,1)S(1)} %get-tuple-element.37), channel_id=1, source_target_pairs={{64,0},{80,16},{96,32},{112,48},{0,64},{16,80},{32,96},{48,112},{6... | collective-permute-start | bytes 110600 | tf_op jit(solution)/shard_map/ppermute | solution.py:401
  139.5 6.8 %collective-permute-start.12 = (bf16[6,3072]{1,0:T(8,128)(2,1)S(1)}, bf16[6,3072]{1,0:T(8,128)(2,1)S(1)}, u32[]{:S(2)}, u32[]{:S(2)}) collective-permute-start(bf16[6,3072]{1,0:T(8,128)(2,1)S(1)} %get-tuple-element.35), channel_id=1, source_target_pairs={{32,0},{48,16},{64,32},{80,48},{96,64},{112,80},{0,96},{16,112},{3... | collective-permute-start | bytes 110600 | tf_op jit(solution)/shard_map/ppermute | solution.py:401
